TPU v7x, 32 devices: a whole 2x2x4 slice. The times are simulated.
32 devices in a mesh: mem: 8 (over z, x), lon: 4 (over y, core).
Axes of the slice: x: 2, y: 2, z: 4, core: 2. Of those that a mesh axis runs over, the one named last changes fastest.
Arguments:
- state: bfloat16 [256, 8192], P('mem', 'lon'), may hold values from -6 to 6
- hx: bfloat16 [128, 256, 128], P('lon'), may hold values from -6 to 6
- obs_value: float32 [128, 128], P('lon'), may hold values from -10 to 10
- obs_rinv: float32 [128, 128], P('lon'), may hold values from 0.3 to 3
- obs_count: int32 [128], P('lon'), may hold values from 1 to 128
- loc_pattern: int32 [64, 8], P('lon'), may hold values from 0 to 95, as said below
Outputs:
- analysis: bfloat16 [256, 8192], P('mem', 'lon')
Inputs may be any that keep to these rules, and one draw needn't show every extreme that they name: obs_count[n] is how many of block n's first observations are valid; the rest are ignored. Each row of loc_pattern holds 8 different window positions out of 96: the previous region's blocks, the patch's own region's blocks, the next region's blocks, around the closed longitude loop.
All inputs are finite; a program needn't handle non-finite values.
Results may differ from a plain program's by a relative error of at most 0.0065.
Values may be sent and summed in bfloat16 or wider, within the bound.
No kernel may reach another device: no remote copies, remote signals or barrier semaphores. Data moves between devices by JAX's collectives and lax.ppermute only.
A program may use at most 64 MiB of HBM per device.

v0:
```python
import functools

import jax
import jax.numpy as jnp
from jax import lax
from jax.experimental import pallas as pl
from jax.experimental.pallas import tpu as pltpu
from jax.sharding import PartitionSpec as P

ITERS = 6
PAD = 16
CHUNK = 4
PAIR = 2
F32 = jnp.float32
BF16 = jnp.bfloat16

VMEM = pl.BlockSpec(memory_space=pltpu.VMEM)
SMEM = pl.BlockSpec(memory_space=pltpu.SMEM)
HBM = pl.BlockSpec(memory_space=pltpu.HBM)


def stay(value):
    return pltpu.with_memory_space_constraint(value, pltpu.HBM)


def split(value):
    high = value.astype(BF16)
    return high, (value - high.astype(F32)).astype(BF16)


def product(left, right):
    lhs = jnp.concatenate([left[0], left[0], left[1]], axis=1)
    rhs = jnp.concatenate([right[0], right[1], right[0]], axis=0)
    return jnp.dot(lhs, rhs, preferred_element_type=F32)


def share(pattern, row, side, patches, pert, weights, innov, left, right):
    blocks, members, width = pert.shape
    uses = pattern.shape[0]
    for slot in range(uses):
        position = pattern[slot, row]
        block = position - side * blocks
        here = jnp.logical_and(block >= 0, block < blocks)
        block = jnp.clip(block, 0, blocks - 1)
        spot = jnp.full((1, width), position, jnp.int32).astype(F32)
        rank = jnp.full((1, width), row, jnp.int32).astype(F32)
        offset = (spot + 0.5) / blocks - 1.0 - (rank + 0.5) / patches
        taper = jnp.exp(-0.5 * offset * offset) * jnp.where(here, 1.0, 0.0)
        cols = slice(slot * width, (slot + 1) * width)
        picked = pert[block]
        weight = taper * weights[pl.ds(block, 1), :]
        left[:members, cols] = (weight * picked.astype(F32)).astype(BF16)
        vector = taper * innov[pl.ds(block, 1), :]
        left[members:, cols] = jnp.broadcast_to(vector, (PAD, width)).astype(BF16)
        right[:, cols] = picked
    return lax.dot_general(
        left[...], right[...], (((1,), (1,)), ((), ())), preferred_element_type=F32
    )


def own_kernel(
    patches,
    here,
    count_all,
    pattern_all,
    hx,
    value_all,
    rinv_all,
    pert,
    weights,
    innov,
    own,
    raw,
    count,
    pattern,
    value,
    rinv,
    left,
    right,
    sems,
    small,
):
    blocks, members, width = raw.shape
    smalls = [
        pltpu.make_async_copy(source, target, small.at[i])
        for i, (source, target) in enumerate(
            ((count_all, count), (value_all, value), (rinv_all, rinv), (pattern_all, pattern))
        )
    ]
    copies = [
        pltpu.make_async_copy(hx.at[pl.ds(i, CHUNK)], raw.at[pl.ds(i, CHUNK)], sems.at[i // CHUNK])
        for i in range(0, blocks, CHUNK)
    ]
    for copy in smalls + copies:
        copy.start()
    for copy in smalls:
        copy.wait()
    lane = lax.broadcasted_iota(jnp.int32, (1, width), 1)
    for block in range(blocks):
        if block % CHUNK == 0:
            copies[block // CHUNK].wait()
        member = raw[block].astype(F32)
        mean = jnp.sum(member, axis=0, keepdims=True) / members
        pert[block] = (member - mean).astype(BF16)
        weight = jnp.where(lane < count[block], rinv[block : block + 1, :], 0.0)
        gap = weight * (value[block : block + 1, :] - mean)
        weights[block : block + 1, :] = weight.astype(BF16).astype(F32)
        innov[block : block + 1, :] = gap
    mine = own.shape[0]
    for patch in range(mine):
        row = here[0] * mine + patch
        own[patch] = share(pattern, row, 1, patches, pert, weights, innov, left, right)


def neighbour_kernel(
    patches,
    here,
    before,
    after,
    pert,
    weights,
    innov,
    state,
    paired,
    to_before,
    to_after,
    *rest,
):
    slabs, (left, right, sems) = rest[:-3], rest[-3:]
    span = slabs[0].shape[2]
    length = len(slabs)
    layer, side = here[0] // PAIR, here[0] % PAIR
    moves = []
    for shift, slab in enumerate(slabs):
        target = lax.rem(layer + shift, length) * PAIR + side
        cols = pl.ds(pl.multiple_of(target * span, span), span)
        moves.append((state.at[:, cols], slab.at[side]))
        moves.append((paired.at[:, cols], slab.at[1 - side]))
    moves = [pltpu.make_async_copy(*move, sems.at[i]) for i, move in enumerate(moves)]
    for move in moves:
        move.start()
    members = pert.shape[1]
    half = members // 2
    mine = to_before.shape[0]
    above = lax.broadcasted_iota(jnp.int32, (half, half), 0)
    across = lax.broadcasted_iota(jnp.int32, (half, half), 1)
    for pattern, side, out in ((before, 2, to_before), (after, 0, to_after)):
        for patch in range(mine):
            row = here[0] * mine + patch
            part = share(pattern, row, side, patches, pert, weights, innov, left, right)
            corner = part[half:members, half:]
            out[patch, :half, :] = part[:half, half:].astype(BF16)
            out[patch, half:members, :] = jnp.where(
                above >= across, part[:half, :half], corner
            ).astype(BF16)
            diagonal = jnp.sum(jnp.where(above == across, corner, 0.0), axis=0, keepdims=True)
            force = part[members : members + 1]
            rows = [diagonal, force[:, :half], force[:, half:]]
            parts = [split(value) for value in rows]
            index = lax.broadcasted_iota(jnp.int32, (PAD, half), 0)
            tail = jnp.zeros((PAD, half), F32)
            for i, (high, low) in enumerate(parts):
                tail = jnp.where(index == 2 * i, high.astype(F32), tail)
                tail = jnp.where(index == 2 * i + 1, low.astype(F32), tail)
            out[patch, members:, :] = tail.astype(BF16)
    for move in moves:
        move.wait()


def total(value):
    return jnp.sum(jnp.sum(value, axis=0, keepdims=True), axis=1, keepdims=True)


def root_kernel(own, before, after, root_out, rows_out):
    mine, _, members = own.shape
    half = members // 2
    above = lax.broadcasted_iota(jnp.int32, (half, half), 0)
    across = lax.broadcasted_iota(jnp.int32, (half, half), 1)
    row = lax.broadcasted_iota(jnp.int32, (members, members), 0)
    col = lax.broadcasted_iota(jnp.int32, (members, members), 1)
    diagonal = row == col

    def less(value, amount):
        return value - jnp.where(diagonal, amount, 0.0)

    def dot(left, right):
        return jnp.dot(left, right, preferred_element_type=F32)

    each = range(mine)
    rest, share_of, scale, forcing = [], [], [], []
    base = members - 1.0
    for patch in each:
        packed = before[patch].astype(F32) + after[patch].astype(F32)
        upper = packed[:half]
        mixed = packed[half:members]
        last = packed[members:]
        corner = last[0:1] + last[1:2]
        force = jnp.concatenate([last[2:3] + last[3:4], last[4:5] + last[5:6]], axis=1)
        flipped = mixed.T
        first = jnp.where(above >= across, mixed, flipped)
        second = jnp.where(above < across, mixed, flipped)
        second = jnp.where(above == across, corner, second)
        far = jnp.concatenate(
            [
                jnp.concatenate([first, upper], axis=1),
                jnp.concatenate([upper.T, second], axis=1),
            ],
            axis=0,
        )
        grams = own[patch, :members, :] + far
        trace = total(jnp.where(diagonal, grams, 0.0))
        norm = jnp.sqrt(total(grams * grams) + 2.0 * base * trace + base * base * members)
        scale.append(norm)
        forcing.append(force + own[patch, members : members + 1, :])
        share_of.append((trace / members + base) / norm)
        rest.append(less(grams, trace / members) * (1.0 / norm))
    lead, tail = [None] * mine, [None] * mine
    for step in range(ITERS):
        final = step == ITERS - 1
        small = [rest[p].astype(BF16) for p in each]
        squares, crosses = [None] * mine, [None] * mine
        for p in each:
            if step == 0:
                squares[p] = dot(small[p], small[p])
            elif final:
                crosses[p] = dot(tail[p].astype(BF16), small[p])
            else:
                both = dot(jnp.concatenate([small[p], tail[p].astype(BF16)], axis=0), small[p])
                squares[p], crosses[p] = both[:members], both[members:]
        for p in each:
            factor = 1.5 - 0.5 * share_of[p]
            if step == 0:
                lead[p], tail[p] = factor, -0.5 * rest[p]
            else:
                part = total(tail[p] * rest[p]) / members
                tail[p] = (
                    factor * tail[p] - 0.5 * lead[p] * rest[p] - 0.5 * less(crosses[p], part)
                )
                lead[p] = factor * lead[p] - 0.5 * part
        if final:
            break
        for p in each:
            squares[p] = less(squares[p], total(rest[p] * rest[p]) / members)
        cubes = [dot(squares[p].astype(BF16), small[p]) for p in each]
        for p in each:
            m = share_of[p]
            factor = 1.5 - 0.5 * m
            part = total(rest[p] * rest[p]) / members
            third = total(rest[p] * squares[p]) / members
            share_of[p] = m * factor * factor + (0.25 * m - factor) * part + 0.25 * third
            rest[p] = (
                (factor * factor - m * factor + 0.25 * part) * rest[p]
                + (0.25 * m - factor) * squares[p]
                + 0.25 * less(cubes[p], third)
            )
    for p in each:
        high = tail[p].astype(BF16)
        root_out[p] = high
        force = jnp.broadcast_to(forcing[p], (PAD, members))
        gain = (lead[p] * force + dot(force.astype(BF16), high)) / scale[p]
        index = lax.broadcasted_iota(jnp.int32, (PAD, members), 0)
        spread = jnp.sqrt(base) / jnp.sqrt(scale[p])
        rows_out[p] = jnp.where(index == 0, gain, jnp.where(index == 1, lead[p], spread))


def apply_kernel(here, root, rows, *rest):
    slabs, (out, columns) = rest[:-2], rest[-2:]
    mine, members, _ = root.shape
    points = out.shape[1] // mine
    length = len(slabs)
    _, local, _ = slabs[0].shape
    for shift, slab in enumerate(slabs):
        source = lax.rem(here[0] // PAIR - shift + length, length)
        for i in range(PAIR):
            place = pl.ds(pl.multiple_of((source * PAIR + i) * local, local), local)
            columns[place, :] = slab[i]
    for p in range(mine):
        cols = slice(p * points, (p + 1) * points)
        member = columns[:, cols].astype(F32)
        mean = jnp.sum(member, axis=0, keepdims=True) / members
        deviation = member - mean
        spread = rows[p, 1:2, :points] * deviation + jnp.dot(
            root[p], deviation.astype(BF16), preferred_element_type=F32
        )
        shift = mean + product(split(rows[p]), split(spread))[0:1]
        out[:, cols] = (shift + rows[p, 2:3, :points] * spread).astype(BF16)


def layout_kernel(pieces, out, sems):
    count, _, width = pieces.shape
    copies = [
        pltpu.make_async_copy(
            pieces.at[i], out.at[:, pl.ds(i * width, width)], sems.at[i]
        )
        for i in range(count)
    ]
    for copy in copies:
        copy.start()
    for copy in copies:
        copy.wait()


def body(state, hx, obs_value, obs_rinv, obs_count, loc_pattern):
    blocks, members, width = hx.shape
    patches, uses = loc_pattern.shape
    mem_total = lax.axis_size("mem")
    mine = patches // mem_total
    local, points = state.shape
    ring = lax.axis_size("lon")
    up = [(i, (i + 1) % ring) for i in range(ring)]
    down = [(j, i) for i, j in up]
    here = lax.axis_index("mem").astype(jnp.int32).reshape(1)
    shape = jax.ShapeDtypeStruct
    padded = members + PAD

    span = points // mem_total
    length = mem_total // PAIR
    swap = [(i, i + 1 - 2 * (i % PAIR)) for i in range(mem_total)]

    pattern = loc_pattern.T
    before = lax.ppermute(pattern, "lon", up)
    after = lax.ppermute(pattern, "lon", down)
    paired = lax.ppermute(state, "mem", swap)
    operands = [
        pltpu.VMEM((padded, uses * width), BF16),
        pltpu.VMEM((members, uses * width), BF16),
    ]
    limit = pltpu.CompilerParams(vmem_limit_bytes=16 * 1024 * 1024)
    gram = 2 * padded * members * uses * width
    pert, weights, innov, own = pl.pallas_call(
        functools.partial(own_kernel, patches),
        out_shape=(
            shape((blocks, members, width), BF16),
            shape((blocks, width), F32),
            shape((blocks, width), F32),
            shape((mine, padded, members), F32),
        ),
        in_specs=[SMEM] + [HBM] * 5,
        out_specs=(VMEM,) * 4,
        scratch_shapes=[
            pltpu.VMEM((blocks, members, width), BF16),
            pltpu.SMEM(obs_count.shape, jnp.int32),
            pltpu.SMEM(pattern.shape, jnp.int32),
            pltpu.VMEM(obs_value.shape, F32),
            pltpu.VMEM(obs_rinv.shape, F32),
        ]
        + operands
        + [pltpu.SemaphoreType.DMA((blocks // CHUNK,)), pltpu.SemaphoreType.DMA((4,))],
        compiler_params=limit,
        cost_estimate=pl.CostEstimate(
            flops=mine * gram, bytes_accessed=2 * hx.size * 2, transcendentals=0
        ),
        name="own_share",
    )(here, *(stay(value) for value in (obs_count, pattern, hx, obs_value, obs_rinv)))
    packed = shape((mine, padded, members // 2), BF16)
    slab = shape((PAIR, local, span), BF16)
    to_before, to_after, *slabs = pl.pallas_call(
        functools.partial(neighbour_kernel, patches),
        out_shape=(packed, packed) + (slab,) * length,
        in_specs=[SMEM] * 3 + [VMEM] * 3 + [HBM] * 2,
        out_specs=(VMEM,) * (2 + length),
        scratch_shapes=operands + [pltpu.SemaphoreType.DMA((PAIR * length,))],
        compiler_params=limit,
        cost_estimate=pl.CostEstimate(
            flops=2 * mine * gram, bytes_accessed=hx.size * 2, transcendentals=0
        ),
        name="neighbour_share",
    )(here, before, after, pert, weights, innov, state, paired)
    from_before = lax.ppermute(to_after, "lon", up)
    from_after = lax.ppermute(to_before, "lon", down)
    for shift in range(1, length):
        turn = [(i, (i + shift * PAIR) % mem_total) for i in range(mem_total)]
        slabs[shift] = lax.ppermute(slabs[shift], "mem", turn)
    root, rows = pl.pallas_call(
        root_kernel,
        out_shape=(shape((mine, members, members), BF16), shape((mine, PAD, members), F32)),
        in_specs=[VMEM] * 3,
        out_specs=(VMEM,) * 2,
        compiler_params=limit,
        cost_estimate=pl.CostEstimate(
            flops=mine * 15 * 2 * members**3, bytes_accessed=2**20, transcendentals=0
        ),
        name="root",
    )(own, from_before, from_after)
    updated = pl.pallas_call(
        apply_kernel,
        out_shape=shape((members, span), BF16),
        in_specs=[SMEM] + [VMEM] * (2 + length),
        out_specs=VMEM,
        scratch_shapes=[pltpu.VMEM((members, span), BF16)],
        compiler_params=limit,
        cost_estimate=pl.CostEstimate(
            flops=2 * members**2 * span, bytes_accessed=2**19, transcendentals=0
        ),
        name="apply",
    )(here, root, rows, *slabs)
    pieces = lax.all_to_all(
        updated.reshape(mem_total, local, span), "mem", split_axis=0, concat_axis=0
    )
    return pl.pallas_call(
        layout_kernel,
        out_shape=shape((local, points), BF16),
        in_specs=[pl.BlockSpec(memory_space=pl.ANY)],
        out_specs=HBM,
        scratch_shapes=[pltpu.SemaphoreType.DMA((mem_total,))],
        name="layout",
    )(pieces)


def solution(mesh):
    in_specs = (
        P("mem", "lon"),
        P("lon", None, None),
        P("lon", None),
        P("lon", None),
        P("lon"),
        P("lon", None),
    )
    out_specs = P("mem", "lon")
    return jax.shard_map(body, mesh=mesh, in_specs=in_specs, out_specs=out_specs, check_vma=False)
```

profile of v0, /device:TPU:0, one launch (start us, length us, event | category | flops | bytes accessed | tf_op | source)
XLA Modules:
  0.0 37.6 jit_solution(14856047537397261571)
XLA Ops:
  0.0 0.0 copy-start
  0.0 2.9 %collective-permute-start.2 = (bf16[32,2048]{1,0:T(8,128)(2,1)}, bf16[32,2048]{1,0:T(8,128)(2,1)S(1)}, u32[]{:S(2)}, u32[]{:S(2)}) collective-permute-start(bf16[32,2048]{1,0:T(8,128)(2,1)} %state.1), channel_id=1, source_target_pairs={{0,4},{4,0},{8,12},{12,8},{16,20},{20,16},{24,28},{28,24},{1,5},{5... | collective-permute-start | bytes 393224 | tf_op jit(solution)/shard_map/ppermute | solution.py:323
  2.9 0.7 %collective-permute-start.1 = (s32[8,16]{1,0:T(8,128)}, s32[8,16]{1,0:T(8,128)S(1)}, u32[]{:S(2)}, u32[]{:S(2)}) collective-permute-start(s32[8,16]{1,0:T(8,128)} %bitcast.4), channel_id=1, source_target_pairs={{1,0},{2,1},{3,2},{0,3},{5,4},{6,5},{7,6},{4,7},{9,8},{10,9},{11,1... | collective-permute-start | bytes 1544 | tf_op jit(solution)/shard_map/ppermute | solution.py:322
  3.6 0.0 collective-permute-start
  3.6 2.9 %own_share.1 = (bf16[32,256,128]{2,1,0:T(8,128)(2,1)S(1)}, f32[32,128]{1,0:T(8,128)S(1)}, f32[32,128]{1,0:T(8,128)S(1)}, f32[2,272,256]{2,1,0:T(8,128)S(1)}) custom-call(s32[1]{0:T(128)} %bitcast.here, s32[32]{0:T(128)} %count_all.1, s32[8,16]{1,0:T(8,128)} %bitcast.6, bf16[32,256,128]{2,1,0:T(8,128)(2,1)} %hx.1, f32[32,128]{1,0:T(8,128)} %value_all.1, ...), custom_call_target="tpu_custom_call" | custom-call | flops 285212672 | bytes 4194304 | tf_op jit(solution)/shard_map/own_share/pallas_call | solution.py:330
  6.6 0.0 collective-permute-done.1.after
  6.6 0.3 collective-permute-done.before
  6.9 0.0 collective-permute-done.2.paired
  6.9 0.0 copy-done
  6.9 2.4 %neighbour_share.1 = (bf16[2,272,128]{2,1,0:T(8,128)(2,1)S(1)}, bf16[2,272,128]{2,1,0:T(8,128)(2,1)S(1)}, bf16[2,32,256]{2,1,0:T(8,128)(2,1)S(1)}, bf16[2,32,256...) custom-call(s32[1]{0:T(128)} %bitcast.here, ...), custom_call_target="tpu_custom_call" | custom-call | flops 570425344 | bytes 2097152 | tf_op jit(solution)/shard_map/neighbour_share/pallas_call | solution.py:357
  9.3 0.7 %collective-permute-start.3 = (bf16[2,272,128]{2,1,0:T(8,128)(2,1)S(1)}, bf16[2,272,128]{2,1,0:T(8,128)(2,1)S(1)}, u32[]{:S(2)}, u32[]{:S(2)}) collective-permute-start(bf16[2,272,128]{2,1,0:T(8,128)(2,1)S(1)} %get-tuple-element.21), channel_id=1, source_target_pairs={{0,1},{1,2},{2,3},{3,0},{4,5},{5,6},{6,7},{7,4},{8,9},{9,10},{10,1... | collective-permute-start | bytes 417800 | tf_op jit(solution)/shard_map/ppermute | solution.py:369
  10.1 1.0 %collective-permute-start.4 = (bf16[2,272,128]{2,1,0:T(8,128)(2,1)S(1)}, bf16[2,272,128]{2,1,0:T(8,128)(2,1)S(1)}, u32[]{:S(2)}, u32[]{:S(2)}) collective-permute-start(bf16[2,272,128]{2,1,0:T(8,128)(2,1)S(1)} %get-tuple-element.22), channel_id=1, source_target_pairs={{1,0},{2,1},{3,2},{0,3},{5,4},{6,5},{7,6},{4,7},{9,8},{10,9},{11,1... | collective-permute-start | bytes 417800 | tf_op jit(solution)/shard_map/ppermute | solution.py:370
  11.1 1.6 %collective-permute-start.5 = (bf16[2,32,256]{2,1,0:T(8,128)(2,1)S(1)}, bf16[2,32,256]{2,1,0:T(8,128)(2,1)S(1)}, u32[]{:S(2)}, u32[]{:S(2)}) collective-permute-start(bf16[2,32,256]{2,1,0:T(8,128)(2,1)S(1)} %get-tuple-element.26), channel_id=1, source_target_pairs={{0,8},{4,12},{8,16},{12,20},{16,24},{20,28},{24,0},{28,4},{1,9},{5... | collective-permute-start | bytes 98312 | tf_op jit(solution)/shard_map/ppermute | solution.py:373
  12.7 2.6 %collective-permute-start.6 = (bf16[2,32,256]{2,1,0:T(8,128)(2,1)S(1)}, bf16[2,32,256]{2,1,0:T(8,128)(2,1)S(1)}, u32[]{:S(2)}, u32[]{:S(2)}) collective-permute-start(bf16[2,32,256]{2,1,0:T(8,128)(2,1)S(1)} %get-tuple-element.27), channel_id=1, source_target_pairs={{0,16},{4,20},{8,24},{12,28},{16,0},{20,4},{24,8},{28,12},{1,17},{... | collective-permute-start | bytes 98312 | tf_op jit(solution)/shard_map/ppermute | solution.py:373
  15.3 1.3 %collective-permute-start.7 = (bf16[2,32,256]{2,1,0:T(8,128)(2,1)S(1)}, bf16[2,32,256]{2,1,0:T(8,128)(2,1)S(1)}, u32[]{:S(2)}, u32[]{:S(2)}) collective-permute-start(bf16[2,32,256]{2,1,0:T(8,128)(2,1)S(1)} %get-tuple-element.28), channel_id=1, source_target_pairs={{0,24},{4,28},{8,0},{12,4},{16,8},{20,12},{24,16},{28,20},{1,25},{... | collective-permute-start | bytes 98312 | tf_op jit(solution)/shard_map/ppermute | solution.py:373
  16.7 0.0 collective-permute-done.3.before
  16.7 0.0 collective-permute-done.4.after
  16.7 3.4 %root.1 = (bf16[2,256,256]{2,1,0:T(8,128)(2,1)S(1)}, f32[2,16,256]{2,1,0:T(8,128)S(1)}) custom-call(f32[2,272,256]{2,1,0:T(8,128)S(1)} %get-tuple-element.17.own, bf16[2,272,128]{2,1,0:T(8,128)(2,1)S(1)} %collective-permute-done.3.before, bf16[2,272,128]{2,1,0:T(8,128)(2,1)S(1)} %collective-permute-done.4.after), custom_call_target="tpu_custom_call" | custom-call | flops 1006632960 | bytes 1048576 | tf_op jit(solution)/shard_map/root/pallas_call | solution.py:374
  20.0 0.0 collective-permute-done.5.rest_1_
  20.0 0.0 collective-permute-done.6.rest_2_
  20.0 0.0 collective-permute-done.7.rest_3_
  20.1 0.7 %apply.1 = bf16[256,256]{1,0:T(8,128)(2,1)S(1)} custom-call(s32[1]{0:T(128)} %bitcast.here, bf16[2,256,256]{2,1,0:T(8,128)(2,1)S(1)} %get-tuple-element.23.root, f32[2,16,256]{2,1,0:T(8,128)S(1)} %get-tuple-element.24.rows, bf16[2,32,256]{2,1,0:T(8,128)(2,1)S(1)} %get-tuple-element.25.rest_0_, bf16[2,32,256]{2,1,0:T(8,128)(2,1)S(1)} %collective-permute-done.5.rest_1_, ...), custom_call_target="tpu_custom_call" | custom-call | flops 33554432 | bytes 524288 | tf_op jit(solution)/shard_map/apply/pallas_call | solution.py:385
  20.7 11.7 %all_to_all.5.pieces = bf16[8,32,256]{2,1,0:T(8,128)(2,1)} all-to-all(bf16[8,32,256]{2,1,0:T(8,128)(2,1)S(1)} %bitcast.3), channel_id=1, replica_groups=mesh['mem'=8,'lon'=4] {'mem'}, dimensions={0} | all-to-all | bytes 262144 | tf_op jit(solution)/shard_map/all_to_all | solution.py:397
  32.5 5.1 %layout.1 = bf16[32,2048]{1,0:T(8,128)(2,1)} custom-call(bf16[8,32,256]{2,1,0:T(8,128)(2,1)} %all_to_all.5.pieces), custom_call_target="tpu_custom_call" | custom-call | tf_op jit(solution)/shard_map/layout/pallas_call | solution.py:400
Async XLA Ops:
  0.0 6.9 %copy-start = (bf16[32,2048]{1,0:T(8,128)(2,1)S(1)}, bf16[32,2048]{1,0:T(8,128)(2,1)}, u32[]{:S(2)}) copy-start(bf16[32,2048]{1,0:T(8,128)(2,1)} %state.1) | copy-start | bytes 393220
  0.0 6.9 %collective-permute-start.2 = (bf16[32,2048]{1,0:T(8,128)(2,1)}, bf16[32,2048]{1,0:T(8,128)(2,1)S(1)}, u32[]{:S(2)}, u32[]{:S(2)}) collective-permute-start(bf16[32,2048]{1,0:T(8,128)(2,1)} %state.1), channel_id=1, source_target_pairs={{0,4},{4,0},{8,12},{12,8},{16,20},{20,16},{24,28},{28,24},{1,5},{5... | collective-permute-start | bytes 393224 | tf_op jit(solution)/shard_map/ppermute | solution.py:323
  2.9 3.6 %collective-permute-start.1 = (s32[8,16]{1,0:T(8,128)}, s32[8,16]{1,0:T(8,128)S(1)}, u32[]{:S(2)}, u32[]{:S(2)}) collective-permute-start(s32[8,16]{1,0:T(8,128)} %bitcast.4), channel_id=1, source_target_pairs={{1,0},{2,1},{3,2},{0,3},{5,4},{6,5},{7,6},{4,7},{9,8},{10,9},{11,1... | collective-permute-start | bytes 1544 | tf_op jit(solution)/shard_map/ppermute | solution.py:322
  3.6 3.2 %collective-permute-start = (s32[8,16]{1,0:T(8,128)}, s32[8,16]{1,0:T(8,128)S(1)}, u32[]{:S(2)}, u32[]{:S(2)}) collective-permute-start(s32[8,16]{1,0:T(8,128)} %bitcast.5), channel_id=1, source_target_pairs={{0,1},{1,2},{2,3},{3,0},{4,5},{5,6},{6,7},{7,4},{8,9},{9,10},{10,1... | collective-permute-start | bytes 1544 | tf_op jit(solution)/shard_map/ppermute | solution.py:321
  9.3 7.3 %collective-permute-start.3 = (bf16[2,272,128]{2,1,0:T(8,128)(2,1)S(1)}, bf16[2,272,128]{2,1,0:T(8,128)(2,1)S(1)}, u32[]{:S(2)}, u32[]{:S(2)}) collective-permute-start(bf16[2,272,128]{2,1,0:T(8,128)(2,1)S(1)} %get-tuple-element.21), channel_id=1, source_target_pairs={{0,1},{1,2},{2,3},{3,0},{4,5},{5,6},{6,7},{7,4},{8,9},{9,10},{10,1... | collective-permute-start | bytes 417800 | tf_op jit(solution)/shard_map/ppermute | solution.py:369
  10.1 6.6 %collective-permute-start.4 = (bf16[2,272,128]{2,1,0:T(8,128)(2,1)S(1)}, bf16[2,272,128]{2,1,0:T(8,128)(2,1)S(1)}, u32[]{:S(2)}, u32[]{:S(2)}) collective-permute-start(bf16[2,272,128]{2,1,0:T(8,128)(2,1)S(1)} %get-tuple-element.22), channel_id=1, source_target_pairs={{1,0},{2,1},{3,2},{0,3},{5,4},{6,5},{7,6},{4,7},{9,8},{10,9},{11,1... | collective-permute-start | bytes 417800 | tf_op jit(solution)/shard_map/ppermute | solution.py:370
  11.1 8.9 %collective-permute-start.5 = (bf16[2,32,256]{2,1,0:T(8,128)(2,1)S(1)}, bf16[2,32,256]{2,1,0:T(8,128)(2,1)S(1)}, u32[]{:S(2)}, u32[]{:S(2)}) collective-permute-start(bf16[2,32,256]{2,1,0:T(8,128)(2,1)S(1)} %get-tuple-element.26), channel_id=1, source_target_pairs={{0,8},{4,12},{8,16},{12,20},{16,24},{20,28},{24,0},{28,4},{1,9},{5... | collective-permute-start | bytes 98312 | tf_op jit(solution)/shard_map/ppermute | solution.py:373
  12.7 7.3 %collective-permute-start.6 = (bf16[2,32,256]{2,1,0:T(8,128)(2,1)S(1)}, bf16[2,32,256]{2,1,0:T(8,128)(2,1)S(1)}, u32[]{:S(2)}, u32[]{:S(2)}) collective-permute-start(bf16[2,32,256]{2,1,0:T(8,128)(2,1)S(1)} %get-tuple-element.27), channel_id=1, source_target_pairs={{0,16},{4,20},{8,24},{12,28},{16,0},{20,4},{24,8},{28,12},{1,17},{... | collective-permute-start | bytes 98312 | tf_op jit(solution)/shard_map/ppermute | solution.py:373
  15.3 4.7 %collective-permute-start.7 = (bf16[2,32,256]{2,1,0:T(8,128)(2,1)S(1)}, bf16[2,32,256]{2,1,0:T(8,128)(2,1)S(1)}, u32[]{:S(2)}, u32[]{:S(2)}) collective-permute-start(bf16[2,32,256]{2,1,0:T(8,128)(2,1)S(1)} %get-tuple-element.28), channel_id=1, source_target_pairs={{0,24},{4,28},{8,0},{12,4},{16,8},{20,12},{24,16},{28,20},{1,25},{... | collective-permute-start | bytes 98312 | tf_op jit(solution)/shard_map/ppermute | solution.py:373
where the time goes:
time: 37.8 us; the launch traced here: 37.6 us
  Pallas kernels  14.6 us (39%)
  blocking collectives  11.7 us (31%)
  starting transfers between devices  11 us (29%)
    all_to_all x1, blocking collectives, body(): lax.all_to_all(updated.reshape(mem_total, local, span), 'mem', split_axis...  11.7 us
    ppermute x3, starting transfers between devices, body(): slabs[shift] = lax.ppermute(slabs[shift], 'mem', turn)  5.54 us
    pallas_call x1, Pallas kernels, body(): pl.pallas_call(layout_kernel, out_shape=shape((local, points), BF16), in_...  5.14 us
    pallas_call x1, Pallas kernels, body(): pl.pallas_call(root_kernel, out_shape=(shape((mine, members, members), BF...  3.37 us
    ppermute x1, starting transfers between devices, body(): paired = lax.ppermute(state, 'mem', swap)  2.94 us
    pallas_call x1, Pallas kernels, body(): pl.pallas_call(functools.partial(own_kernel, patches), out_shape=(shape((...  2.94 us
    pallas_call x1, Pallas kernels, body(): pl.pallas_call(functools.partial(neighbour_kernel, patches), out_shape=(p...  2.43 us
    ppermute x1, starting transfers between devices, body(): from_after = lax.ppermute(to_before, 'lon', down)  1.05 us
  transfers between devices with their start and end apart: 8, of which 1 were waited for; matrix products, arithmetic and copies ran while one was open for 0% of the time, Pallas kernels for 17%

commit v1 on v0

--- a/solution.py
+++ b/solution.py
@@ -58,33 +58,14 @@
     )
 
 
-def own_kernel(
-    patches,
-    here,
-    count_all,
-    pattern_all,
-    hx,
-    value_all,
-    rinv_all,
-    pert,
-    weights,
-    innov,
-    own,
-    raw,
-    count,
-    pattern,
-    value,
-    rinv,
-    left,
-    right,
-    sems,
-    small,
+def perturb_kernel(
+    count_all, hx, value_all, rinv_all, pert, weights, innov, raw, count, value, rinv, sems, small
 ):
     blocks, members, width = raw.shape
     smalls = [
         pltpu.make_async_copy(source, target, small.at[i])
         for i, (source, target) in enumerate(
-            ((count_all, count), (value_all, value), (rinv_all, rinv), (pattern_all, pattern))
+            ((count_all, count), (value_all, value), (rinv_all, rinv))
         )
     ]
     copies = [
@@ -106,6 +87,9 @@
         gap = weight * (value[block : block + 1, :] - mean)
         weights[block : block + 1, :] = weight.astype(BF16).astype(F32)
         innov[block : block + 1, :] = gap
+
+
+def own_kernel(patches, here, pattern, pert, weights, innov, sent, own, left, right):
     mine = own.shape[0]
     for patch in range(mine):
         row = here[0] * mine + patch
@@ -286,20 +270,6 @@
         out[:, cols] = (shift + rows[p, 2:3, :points] * spread).astype(BF16)
 
 
-def layout_kernel(pieces, out, sems):
-    count, _, width = pieces.shape
-    copies = [
-        pltpu.make_async_copy(
-            pieces.at[i], out.at[:, pl.ds(i * width, width)], sems.at[i]
-        )
-        for i in range(count)
-    ]
-    for copy in copies:
-        copy.start()
-    for copy in copies:
-        copy.wait()
-
-
 def body(state, hx, obs_value, obs_rinv, obs_count, loc_pattern):
     blocks, members, width = hx.shape
     patches, uses = loc_pattern.shape
@@ -327,31 +297,29 @@
     ]
     limit = pltpu.CompilerParams(vmem_limit_bytes=16 * 1024 * 1024)
     gram = 2 * padded * members * uses * width
-    pert, weights, innov, own = pl.pallas_call(
-        functools.partial(own_kernel, patches),
+    pert, weights, innov = pl.pallas_call(
+        perturb_kernel,
         out_shape=(
             shape((blocks, members, width), BF16),
             shape((blocks, width), F32),
             shape((blocks, width), F32),
-            shape((mine, padded, members), F32),
-        ),
-        in_specs=[SMEM] + [HBM] * 5,
-        out_specs=(VMEM,) * 4,
+        ),
+        in_specs=[HBM] * 4,
+        out_specs=(VMEM,) * 3,
         scratch_shapes=[
             pltpu.VMEM((blocks, members, width), BF16),
             pltpu.SMEM(obs_count.shape, jnp.int32),
-            pltpu.SMEM(pattern.shape, jnp.int32),
             pltpu.VMEM(obs_value.shape, F32),
             pltpu.VMEM(obs_rinv.shape, F32),
-        ]
-        + operands
-        + [pltpu.SemaphoreType.DMA((blocks // CHUNK,)), pltpu.SemaphoreType.DMA((4,))],
-        compiler_params=limit,
-        cost_estimate=pl.CostEstimate(
-            flops=mine * gram, bytes_accessed=2 * hx.size * 2, transcendentals=0
-        ),
-        name="own_share",
-    )(here, *(stay(value) for value in (obs_count, pattern, hx, obs_value, obs_rinv)))
+            pltpu.SemaphoreType.DMA((blocks // CHUNK,)),
+            pltpu.SemaphoreType.DMA((3,)),
+        ],
+        compiler_params=limit,
+        cost_estimate=pl.CostEstimate(
+            flops=hx.size * 4, bytes_accessed=2 * hx.size * 2, transcendentals=0
+        ),
+        name="perturb",
+    )(*(stay(value) for value in (obs_count, hx, obs_value, obs_rinv)))
     packed = shape((mine, padded, members // 2), BF16)
     slab = shape((PAIR, local, span), BF16)
     to_before, to_after, *slabs = pl.pallas_call(
@@ -366,6 +334,18 @@
         ),
         name="neighbour_share",
     )(here, before, after, pert, weights, innov, state, paired)
+    own = pl.pallas_call(
+        functools.partial(own_kernel, patches),
+        out_shape=shape((mine, padded, members), F32),
+        in_specs=[SMEM] * 2 + [VMEM] * 3 + [pl.BlockSpec(memory_space=pl.ANY)],
+        out_specs=VMEM,
+        scratch_shapes=operands,
+        compiler_params=limit,
+        cost_estimate=pl.CostEstimate(
+            flops=mine * gram, bytes_accessed=2 * hx.size, transcendentals=0
+        ),
+        name="own_share",
+    )(here, pattern, pert, weights, innov, to_before)
     from_before = lax.ppermute(to_after, "lon", up)
     from_after = lax.ppermute(to_before, "lon", down)
     for shift in range(1, length):
@@ -397,14 +377,7 @@
     pieces = lax.all_to_all(
         updated.reshape(mem_total, local, span), "mem", split_axis=0, concat_axis=0
     )
-    return pl.pallas_call(
-        layout_kernel,
-        out_shape=shape((local, points), BF16),
-        in_specs=[pl.BlockSpec(memory_space=pl.ANY)],
-        out_specs=HBM,
-        scratch_shapes=[pltpu.SemaphoreType.DMA((mem_total,))],
-        name="layout",
-    )(pieces)
+    return jnp.swapaxes(pieces, 0, 1).reshape(local, points)
 
 
 def solution(mesh):

time: 37.8 us -> 33.2 us (0.88)
  Pallas kernels: 14.6 us -> 10 us
  blocking collectives: 11.7 us -> 10.2 us
  waiting for transfers between devices: 0.3 us -> 1.11 us
  local copies, waits for them, and re-layouts: 0.01 us -> 0.67 us
    pallas_call x2, Pallas kernels: 8.08 us -> 3.58 us  [the longest x1 2.13 us: body(): pl.pallas_call(perturb_kernel, out_shape=(shape((blocks, members, width),...]
    all_to_all x1, blocking collectives: 11.7 us -> 10.2 us  [body(): lax.all_to_all(updated.reshape(mem_total, local, span), 'mem', split_axis...]
    ppermute x1, waiting for transfers between devices: 0.28 us -> 1.09 us  [body(): before = lax.ppermute(pattern, 'lon', up)]
    ppermute x1, starting transfers between devices: 0.75 us -> 0.06 us  [body(): from_before = lax.ppermute(to_after, 'lon', up)]
    ppermute x1, starting transfers between devices: 1.05 us -> 1.73 us  [body(): from_after = lax.ppermute(to_before, 'lon', down)]
    reshape x0 -> x1, local copies, waits for them, and re-layouts: none -> 0.66 us  [body(): return jnp.swapaxes(pieces, 0, 1).reshape(local, points)]
  transfers between devices with their start and end apart: 8 -> 8, of which waited for: 1 -> 1; matrix products, arithmetic and copies ran while one was open for 0% -> 0% of each run, Pallas kernels for 17% -> 21%
where the time goes in v1:
time: 33.2 us; the launch traced here: 33 us
  starting transfers between devices  11 us (33%)
  blocking collectives  10.2 us (31%)
  Pallas kernels  10 us (30%)
  waiting for transfers between devices  1.11 us (3%)
  local copies, waits for them, and re-layouts  0.67 us (2%)
    all_to_all x1, blocking collectives, body(): lax.all_to_all(updated.reshape(mem_total, local, span), 'mem', split_axis...  10.2 us
    ppermute x3, starting transfers between devices, body(): slabs[shift] = lax.ppermute(slabs[shift], 'mem', turn)  5.54 us
    pallas_call x1, Pallas kernels, body(): pl.pallas_call(root_kernel, out_shape=(shape((mine, members, members), BF...  3.37 us
    ppermute x1, starting transfers between devices, body(): paired = lax.ppermute(state, 'mem', swap)  2.94 us
    pallas_call x1, Pallas kernels, body(): pl.pallas_call(functools.partial(neighbour_kernel, patches), out_shape=(p...  2.39 us
    pallas_call x1, Pallas kernels, body(): pl.pallas_call(perturb_kernel, out_shape=(shape((blocks, members, width),...  2.13 us
    ppermute x1, starting transfers between devices, body(): from_after = lax.ppermute(to_before, 'lon', down)  1.73 us
    pallas_call x1, Pallas kernels, body(): pl.pallas_call(functools.partial(own_kernel, patches), out_shape=shape((m...  1.45 us
  transfers between devices with their start and end apart: 8, of which 1 were waited for; matrix products, arithmetic and copies ran while one was open for 0% of the time, Pallas kernels for 21%

profile of v1, /device:TPU:0, one launch (start us, length us, event | category | flops | bytes accessed | tf_op | source)
XLA Modules:
  0.0 33.0 jit_solution(11154759544707175112)
XLA Ops:
  0.0 0.0 copy-start
  0.0 2.9 %collective-permute-start.2 = (bf16[32,2048]{1,0:T(8,128)(2,1)}, bf16[32,2048]{1,0:T(8,128)(2,1)S(1)}, u32[]{:S(2)}, u32[]{:S(2)}) collective-permute-start(bf16[32,2048]{1,0:T(8,128)(2,1)} %state.1), channel_id=1, source_target_pairs={{0,4},{4,0},{8,12},{12,8},{16,20},{20,16},{24,28},{28,24},{1,5},{5... | collective-permute-start | bytes 393224 | tf_op jit(solution)/shard_map/ppermute | solution.py:293
  2.9 0.7 %collective-permute-start.1 = (s32[8,16]{1,0:T(8,128)}, s32[8,16]{1,0:T(8,128)S(1)}, u32[]{:S(2)}, u32[]{:S(2)}) collective-permute-start(s32[8,16]{1,0:T(8,128)} %bitcast.7), channel_id=1, source_target_pairs={{1,0},{2,1},{3,2},{0,3},{5,4},{6,5},{7,6},{4,7},{9,8},{10,9},{11,1... | collective-permute-start | bytes 1544 | tf_op jit(solution)/shard_map/ppermute | solution.py:292
  3.6 0.0 collective-permute-start
  3.6 0.0 copy-start.1
  3.6 2.1 %perturb.1 = (bf16[32,256,128]{2,1,0:T(8,128)(2,1)S(1)}, f32[32,128]{1,0:T(8,128)S(1)}, f32[32,128]{1,0:T(8,128)S(1)}) custom-call(s32[32]{0:T(128)} %count_all.1, bf16[32,256,128]{2,1,0:T(8,128)(2,1)} %hx.1, f32[32,128]{1,0:T(8,128)} %value_all.1, f32[32,128]{1,0:T(8,128)} %rinv_all.1), custom_call_target="tpu_custom_call" | custom-call | flops 4194304 | bytes 4194304 | tf_op jit(solution)/shard_map/perturb/pallas_call | solution.py:300
  5.8 0.0 collective-permute-done.1.after
  5.8 1.1 %collective-permute-done.before = s32[8,16]{1,0:T(8,128)S(1)} collective-permute-done((s32[8,16]{1,0:T(8,128)}, s32[8,16]{1,0:T(8,128)S(1)}, u32[]{:S(2)}, u32[]{:S(2)}) %collective-permute-start) | collective-permute-done | bytes 544 | tf_op jit(solution)/shard_map/ppermute | solution.py:291
  6.9 0.0 collective-permute-done.2.paired
  6.9 0.0 copy-done
  6.9 2.4 %neighbour_share.1 = (bf16[2,272,128]{2,1,0:T(8,128)(2,1)S(1)}, bf16[2,272,128]{2,1,0:T(8,128)(2,1)S(1)}, bf16[2,32,256]{2,1,0:T(8,128)(2,1)S(1)}, bf16[2,32,256...) custom-call(s32[1]{0:T(128)} %bitcast.here, ...), custom_call_target="tpu_custom_call" | custom-call | flops 570425344 | bytes 2097152 | tf_op jit(solution)/shard_map/neighbour_share/pallas_call | solution.py:325
  9.3 0.1 collective-permute-start.3
  9.3 1.7 %collective-permute-start.4 = (bf16[2,272,128]{2,1,0:T(8,128)(2,1)S(1)}, bf16[2,272,128]{2,1,0:T(8,128)(2,1)S(1)}, u32[]{:S(2)}, u32[]{:S(2)}) collective-permute-start(bf16[2,272,128]{2,1,0:T(8,128)(2,1)S(1)} %get-tuple-element.19.sent), channel_id=1, source_target_pairs={{1,0},{2,1},{3,2},{0,3},{5,4},{6,5},{7,6},{4,7},{9,8},{10,9},{11,1... | collective-permute-start | bytes 417800 | tf_op jit(solution)/shard_map/ppermute | solution.py:350
  11.1 1.6 %collective-permute-start.5 = (bf16[2,32,256]{2,1,0:T(8,128)(2,1)S(1)}, bf16[2,32,256]{2,1,0:T(8,128)(2,1)S(1)}, u32[]{:S(2)}, u32[]{:S(2)}) collective-permute-start(bf16[2,32,256]{2,1,0:T(8,128)(2,1)S(1)} %get-tuple-element.24), channel_id=1, source_target_pairs={{0,8},{4,12},{8,16},{12,20},{16,24},{20,28},{24,0},{28,4},{1,9},{5... | collective-permute-start | bytes 98312 | tf_op jit(solution)/shard_map/ppermute | solution.py:353
  12.7 2.6 %collective-permute-start.6 = (bf16[2,32,256]{2,1,0:T(8,128)(2,1)S(1)}, bf16[2,32,256]{2,1,0:T(8,128)(2,1)S(1)}, u32[]{:S(2)}, u32[]{:S(2)}) collective-permute-start(bf16[2,32,256]{2,1,0:T(8,128)(2,1)S(1)} %get-tuple-element.25), channel_id=1, source_target_pairs={{0,16},{4,20},{8,24},{12,28},{16,0},{20,4},{24,8},{28,12},{1,17},{... | collective-permute-start | bytes 98312 | tf_op jit(solution)/shard_map/ppermute | solution.py:353
  15.3 1.3 %collective-permute-start.7 = (bf16[2,32,256]{2,1,0:T(8,128)(2,1)S(1)}, bf16[2,32,256]{2,1,0:T(8,128)(2,1)S(1)}, u32[]{:S(2)}, u32[]{:S(2)}) collective-permute-start(bf16[2,32,256]{2,1,0:T(8,128)(2,1)S(1)} %get-tuple-element.26), channel_id=1, source_target_pairs={{0,24},{4,28},{8,0},{12,4},{16,8},{20,12},{24,16},{28,20},{1,25},{... | collective-permute-start | bytes 98312 | tf_op jit(solution)/shard_map/ppermute | solution.py:353
  16.6 0.0 copy-done.1
  16.6 1.4 %own_share.1.own = f32[2,272,256]{2,1,0:T(8,128)S(1)} custom-call(s32[1]{0:T(128)} %bitcast.here, s32[8,16]{1,0:T(8,128)S(1)} %bitcast.9, bf16[32,256,128]{2,1,0:T(8,128)(2,1)S(1)} %get-tuple-element.16.pert, f32[32,128]{1,0:T(8,128)S(1)} %get-tuple-element.17.weights, f32[32,128]{1,0:T(8,128)S(1)} %get-tuple-element.18.innov, ...), custom_call_target="tpu_custom_call" | custom-call | flops 285212672 | bytes 2097152 | tf_op jit(solution)/shard_map/own_share/pallas_call | solution.py:337
  18.1 0.0 collective-permute-done.3.before
  18.1 0.0 collective-permute-done.4.after
  18.1 3.4 %root.1 = (bf16[2,256,256]{2,1,0:T(8,128)(2,1)S(1)}, f32[2,16,256]{2,1,0:T(8,128)S(1)}) custom-call(f32[2,272,256]{2,1,0:T(8,128)S(1)} %own_share.1.own, bf16[2,272,128]{2,1,0:T(8,128)(2,1)S(1)} %collective-permute-done.3.before, bf16[2,272,128]{2,1,0:T(8,128)(2,1)S(1)} %collective-permute-done.4.after), custom_call_target="tpu_custom_call" | custom-call | flops 1006632960 | bytes 1048576 | tf_op jit(solution)/shard_map/root/pallas_call | solution.py:354
  21.5 0.0 collective-permute-done.5.rest_1_
  21.5 0.0 collective-permute-done.6.rest_2_
  21.5 0.0 collective-permute-done.7.rest_3_
  21.5 0.7 %apply.1 = bf16[256,256]{1,0:T(8,128)(2,1)S(1)} custom-call(s32[1]{0:T(128)} %bitcast.here, bf16[2,256,256]{2,1,0:T(8,128)(2,1)S(1)} %get-tuple-element.21.root, f32[2,16,256]{2,1,0:T(8,128)S(1)} %get-tuple-element.22.rows, bf16[2,32,256]{2,1,0:T(8,128)(2,1)S(1)} %get-tuple-element.23.rest_0_, bf16[2,32,256]{2,1,0:T(8,128)(2,1)S(1)} %collective-permute-done.5.rest_1_, ...), custom_call_target="tpu_custom_call" | custom-call | flops 33554432 | bytes 524288 | tf_op jit(solution)/shard_map/apply/pallas_call | solution.py:365
  22.2 10.2 %all_to_all.5 = bf16[8,32,256]{2,1,0:T(8,128)(2,1)S(1)} all-to-all(bf16[8,32,256]{2,1,0:T(8,128)(2,1)S(1)} %bitcast.6), channel_id=1, replica_groups=mesh['mem'=8,'lon'=4] {'mem'}, dimensions={0} | all-to-all | bytes 262144 | tf_op jit(solution)/shard_map/all_to_all | solution.py:377
  32.3 0.7 %copy.8 = bf16[8,4,8,256]{3,2,0,1:T(8,128)(2,1)} copy(bf16[8,4,8,256]{3,2,1,0:T(8,128)(2,1)S(1)} %bitcast.10) | data formatting | bytes 262144 | tf_op jit(solution)/shard_map/reshape | solution.py:380
Async XLA Ops:
  0.0 6.9 %copy-start = (bf16[32,2048]{1,0:T(8,128)(2,1)S(1)}, bf16[32,2048]{1,0:T(8,128)(2,1)}, u32[]{:S(2)}) copy-start(bf16[32,2048]{1,0:T(8,128)(2,1)} %state.1) | copy-start | bytes 393220
  0.0 6.9 %collective-permute-start.2 = (bf16[32,2048]{1,0:T(8,128)(2,1)}, bf16[32,2048]{1,0:T(8,128)(2,1)S(1)}, u32[]{:S(2)}, u32[]{:S(2)}) collective-permute-start(bf16[32,2048]{1,0:T(8,128)(2,1)} %state.1), channel_id=1, source_target_pairs={{0,4},{4,0},{8,12},{12,8},{16,20},{20,16},{24,28},{28,24},{1,5},{5... | collective-permute-start | bytes 393224 | tf_op jit(solution)/shard_map/ppermute | solution.py:293
  2.9 2.8 %collective-permute-start.1 = (s32[8,16]{1,0:T(8,128)}, s32[8,16]{1,0:T(8,128)S(1)}, u32[]{:S(2)}, u32[]{:S(2)}) collective-permute-start(s32[8,16]{1,0:T(8,128)} %bitcast.7), channel_id=1, source_target_pairs={{1,0},{2,1},{3,2},{0,3},{5,4},{6,5},{7,6},{4,7},{9,8},{10,9},{11,1... | collective-permute-start | bytes 1544 | tf_op jit(solution)/shard_map/ppermute | solution.py:292
  3.6 3.2 %collective-permute-start = (s32[8,16]{1,0:T(8,128)}, s32[8,16]{1,0:T(8,128)S(1)}, u32[]{:S(2)}, u32[]{:S(2)}) collective-permute-start(s32[8,16]{1,0:T(8,128)} %bitcast.8), channel_id=1, source_target_pairs={{0,1},{1,2},{2,3},{3,0},{4,5},{5,6},{6,7},{7,4},{8,9},{9,10},{10,1... | collective-permute-start | bytes 1544 | tf_op jit(solution)/shard_map/ppermute | solution.py:291
  3.6 13.0 %copy-start.1 = (s32[16,8]{0,1:T(8,128)S(1)}, s32[16,8]{0,1:T(8,128)}, u32[]{:S(2)}) copy-start(s32[16,8]{0,1:T(8,128)} %param.11) | copy-start | bytes 1540
  9.3 8.8 %collective-permute-start.3 = (bf16[2,272,128]{2,1,0:T(8,128)(2,1)S(1)}, bf16[2,272,128]{2,1,0:T(8,128)(2,1)S(1)}, u32[]{:S(2)}, u32[]{:S(2)}) collective-permute-start(bf16[2,272,128]{2,1,0:T(8,128)(2,1)S(1)} %get-tuple-element.20), channel_id=1, source_target_pairs={{0,1},{1,2},{2,3},{3,0},{4,5},{5,6},{6,7},{7,4},{8,9},{9,10},{10,1... | collective-permute-start | bytes 417800 | tf_op jit(solution)/shard_map/ppermute | solution.py:349
  9.3 8.7 %collective-permute-start.4 = (bf16[2,272,128]{2,1,0:T(8,128)(2,1)S(1)}, bf16[2,272,128]{2,1,0:T(8,128)(2,1)S(1)}, u32[]{:S(2)}, u32[]{:S(2)}) collective-permute-start(bf16[2,272,128]{2,1,0:T(8,128)(2,1)S(1)} %get-tuple-element.19.sent), channel_id=1, source_target_pairs={{1,0},{2,1},{3,2},{0,3},{5,4},{6,5},{7,6},{4,7},{9,8},{10,9},{11,1... | collective-permute-start | bytes 417800 | tf_op jit(solution)/shard_map/ppermute | solution.py:350
  11.1 10.4 %collective-permute-start.5 = (bf16[2,32,256]{2,1,0:T(8,128)(2,1)S(1)}, bf16[2,32,256]{2,1,0:T(8,128)(2,1)S(1)}, u32[]{:S(2)}, u32[]{:S(2)}) collective-permute-start(bf16[2,32,256]{2,1,0:T(8,128)(2,1)S(1)} %get-tuple-element.24), channel_id=1, source_target_pairs={{0,8},{4,12},{8,16},{12,20},{16,24},{20,28},{24,0},{28,4},{1,9},{5... | collective-permute-start | bytes 98312 | tf_op jit(solution)/shard_map/ppermute | solution.py:353
  12.7 8.8 %collective-permute-start.6 = (bf16[2,32,256]{2,1,0:T(8,128)(2,1)S(1)}, bf16[2,32,256]{2,1,0:T(8,128)(2,1)S(1)}, u32[]{:S(2)}, u32[]{:S(2)}) collective-permute-start(bf16[2,32,256]{2,1,0:T(8,128)(2,1)S(1)} %get-tuple-element.25), channel_id=1, source_target_pairs={{0,16},{4,20},{8,24},{12,28},{16,0},{20,4},{24,8},{28,12},{1,17},{... | collective-permute-start | bytes 98312 | tf_op jit(solution)/shard_map/ppermute | solution.py:353
  15.3 6.2 %collective-permute-start.7 = (bf16[2,32,256]{2,1,0:T(8,128)(2,1)S(1)}, bf16[2,32,256]{2,1,0:T(8,128)(2,1)S(1)}, u32[]{:S(2)}, u32[]{:S(2)}) collective-permute-start(bf16[2,32,256]{2,1,0:T(8,128)(2,1)S(1)} %get-tuple-element.26), channel_id=1, source_target_pairs={{0,24},{4,28},{8,0},{12,4},{16,8},{20,12},{24,16},{28,20},{1,25},{... | collective-permute-start | bytes 98312 | tf_op jit(solution)/shard_map/ppermute | solution.py:353

commit v2 on v1

--- a/solution.py
+++ b/solution.py
@@ -34,10 +34,10 @@
     return jnp.dot(lhs, rhs, preferred_element_type=F32)
 
 
-def share(pattern, row, side, patches, pert, weights, innov, left, right):
-    blocks, members, width = pert.shape
-    uses = pattern.shape[0]
-    for slot in range(uses):
+def share(pattern, row, side, patches, pert, weights, innov):
+    blocks, _, width = pert.shape
+    left, right = [], []
+    for slot in range(pattern.shape[0]):
         position = pattern[slot, row]
         block = position - side * blocks
         here = jnp.logical_and(block >= 0, block < blocks)
@@ -46,15 +46,16 @@
         rank = jnp.full((1, width), row, jnp.int32).astype(F32)
         offset = (spot + 0.5) / blocks - 1.0 - (rank + 0.5) / patches
         taper = jnp.exp(-0.5 * offset * offset) * jnp.where(here, 1.0, 0.0)
-        cols = slice(slot * width, (slot + 1) * width)
         picked = pert[block]
-        weight = taper * weights[pl.ds(block, 1), :]
-        left[:members, cols] = (weight * picked.astype(F32)).astype(BF16)
-        vector = taper * innov[pl.ds(block, 1), :]
-        left[members:, cols] = jnp.broadcast_to(vector, (PAD, width)).astype(BF16)
-        right[:, cols] = picked
+        weight = (taper * weights[pl.ds(block, 1), :]).astype(BF16)
+        vector = jnp.broadcast_to(taper * innov[pl.ds(block, 1), :], (PAD, width)).astype(BF16)
+        left.append(jnp.concatenate([weight * picked, vector], axis=0))
+        right.append(picked)
     return lax.dot_general(
-        left[...], right[...], (((1,), (1,)), ((), ())), preferred_element_type=F32
+        jnp.concatenate(left, axis=1),
+        jnp.concatenate(right, axis=1),
+        (((1,), (1,)), ((), ())),
+        preferred_element_type=F32,
     )
 
 
@@ -89,64 +90,56 @@
         innov[block : block + 1, :] = gap
 
 
-def own_kernel(patches, here, pattern, pert, weights, innov, sent, own, left, right):
+def own_kernel(patches, here, pattern, pert, weights, innov, sent, own):
     mine = own.shape[0]
     for patch in range(mine):
         row = here[0] * mine + patch
-        own[patch] = share(pattern, row, 1, patches, pert, weights, innov, left, right)
-
-
-def neighbour_kernel(
-    patches,
-    here,
-    before,
-    after,
-    pert,
-    weights,
-    innov,
-    state,
-    paired,
-    to_before,
-    to_after,
-    *rest,
-):
-    slabs, (left, right, sems) = rest[:-3], rest[-3:]
+        own[patch] = share(pattern, row, 1, patches, pert, weights, innov)
+
+
+def pack(part, out, patch):
+    _, padded, half = out.shape
+    members = padded - PAD
+    above = lax.broadcasted_iota(jnp.int32, (half, half), 0)
+    across = lax.broadcasted_iota(jnp.int32, (half, half), 1)
+    corner = part[half:members, half:]
+    out[patch, :half, :] = part[:half, half:].astype(BF16)
+    out[patch, half:members, :] = jnp.where(above >= across, part[:half, :half], corner).astype(
+        BF16
+    )
+    diagonal = jnp.sum(jnp.where(above == across, corner, 0.0), axis=0, keepdims=True)
+    force = part[members : members + 1]
+    index = lax.broadcasted_iota(jnp.int32, (PAD, half), 0)
+    tail = jnp.zeros((PAD, half), F32)
+    for i, value in enumerate((diagonal, force[:, :half], force[:, half:])):
+        high, low = split(value)
+        tail = jnp.where(index == 2 * i, high.astype(F32), tail)
+        tail = jnp.where(index == 2 * i + 1, low.astype(F32), tail)
+    out[patch, members:, :] = tail.astype(BF16)
+
+
+def far_kernel(patches, side, here, pattern, pert, weights, innov, out):
+    mine = out.shape[0]
+    for patch in range(mine):
+        row = here[0] * mine + patch
+        pack(share(pattern, row, here[side], patches, pert, weights, innov), out, patch)
+
+
+def near_kernel(patches, side, here, pattern, pert, weights, innov, state, paired, sent, out, *rest):
+    slabs, sems = rest[:-1], rest[-1]
     span = slabs[0].shape[2]
     length = len(slabs)
-    layer, side = here[0] // PAIR, here[0] % PAIR
+    layer, place = here[0] // PAIR, here[0] % PAIR
     moves = []
     for shift, slab in enumerate(slabs):
-        target = lax.rem(layer + shift, length) * PAIR + side
+        target = lax.rem(layer + shift, length) * PAIR + place
         cols = pl.ds(pl.multiple_of(target * span, span), span)
-        moves.append((state.at[:, cols], slab.at[side]))
-        moves.append((paired.at[:, cols], slab.at[1 - side]))
+        moves.append((state.at[:, cols], slab.at[place]))
+        moves.append((paired.at[:, cols], slab.at[1 - place]))
     moves = [pltpu.make_async_copy(*move, sems.at[i]) for i, move in enumerate(moves)]
     for move in moves:
         move.start()
-    members = pert.shape[1]
-    half = members // 2
-    mine = to_before.shape[0]
-    above = lax.broadcasted_iota(jnp.int32, (half, half), 0)
-    across = lax.broadcasted_iota(jnp.int32, (half, half), 1)
-    for pattern, side, out in ((before, 2, to_before), (after, 0, to_after)):
-        for patch in range(mine):
-            row = here[0] * mine + patch
-            part = share(pattern, row, side, patches, pert, weights, innov, left, right)
-            corner = part[half:members, half:]
-            out[patch, :half, :] = part[:half, half:].astype(BF16)
-            out[patch, half:members, :] = jnp.where(
-                above >= across, part[:half, :half], corner
-            ).astype(BF16)
-            diagonal = jnp.sum(jnp.where(above == across, corner, 0.0), axis=0, keepdims=True)
-            force = part[members : members + 1]
-            rows = [diagonal, force[:, :half], force[:, half:]]
-            parts = [split(value) for value in rows]
-            index = lax.broadcasted_iota(jnp.int32, (PAD, half), 0)
-            tail = jnp.zeros((PAD, half), F32)
-            for i, (high, low) in enumerate(parts):
-                tail = jnp.where(index == 2 * i, high.astype(F32), tail)
-                tail = jnp.where(index == 2 * i + 1, low.astype(F32), tail)
-            out[patch, members:, :] = tail.astype(BF16)
+    far_kernel(patches, side, here, pattern, pert, weights, innov, out)
     for move in moves:
         move.wait()
 
@@ -164,14 +157,11 @@
     col = lax.broadcasted_iota(jnp.int32, (members, members), 1)
     diagonal = row == col
 
-    def less(value, amount):
-        return value - jnp.where(diagonal, amount, 0.0)
-
     def dot(left, right):
         return jnp.dot(left, right, preferred_element_type=F32)
 
     each = range(mine)
-    rest, share_of, scale, forcing = [], [], [], []
+    rest, factor, scale, forcing = [], [], [], []
     base = members - 1.0
     for patch in each:
         packed = before[patch].astype(F32) + after[patch].astype(F32)
@@ -196,47 +186,30 @@
         norm = jnp.sqrt(total(grams * grams) + 2.0 * base * trace + base * base * members)
         scale.append(norm)
         forcing.append(force + own[patch, members : members + 1, :])
-        share_of.append((trace / members + base) / norm)
-        rest.append(less(grams, trace / members) * (1.0 / norm))
-    lead, tail = [None] * mine, [None] * mine
-    for step in range(ITERS):
-        final = step == ITERS - 1
-        small = [rest[p].astype(BF16) for p in each]
-        squares, crosses = [None] * mine, [None] * mine
-        for p in each:
-            if step == 0:
-                squares[p] = dot(small[p], small[p])
-            elif final:
-                crosses[p] = dot(tail[p].astype(BF16), small[p])
-            else:
-                both = dot(jnp.concatenate([small[p], tail[p].astype(BF16)], axis=0), small[p])
-                squares[p], crosses[p] = both[:members], both[members:]
-        for p in each:
-            factor = 1.5 - 0.5 * share_of[p]
-            if step == 0:
-                lead[p], tail[p] = factor, -0.5 * rest[p]
-            else:
-                part = total(tail[p] * rest[p]) / members
-                tail[p] = (
-                    factor * tail[p] - 0.5 * lead[p] * rest[p] - 0.5 * less(crosses[p], part)
-                )
-                lead[p] = factor * lead[p] - 0.5 * part
-        if final:
-            break
-        for p in each:
-            squares[p] = less(squares[p], total(rest[p] * rest[p]) / members)
+        factor.append(1.5 - 0.5 * (trace / members + base) / norm)
+        level = trace / members
+        rest.append((grams - jnp.where(diagonal, level, 0.0)) * (-0.5 / norm))
+    lead, tail = list(factor), list(rest)
+    small = [rest[p].astype(BF16) for p in each]
+    squares = [dot(small[p], small[p]) for p in each]
+    for step in range(1, ITERS):
         cubes = [dot(squares[p].astype(BF16), small[p]) for p in each]
         for p in each:
-            m = share_of[p]
-            factor = 1.5 - 0.5 * m
-            part = total(rest[p] * rest[p]) / members
-            third = total(rest[p] * squares[p]) / members
-            share_of[p] = m * factor * factor + (0.25 * m - factor) * part + 0.25 * third
+            f = factor[p]
             rest[p] = (
-                (factor * factor - m * factor + 0.25 * part) * rest[p]
-                + (0.25 * m - factor) * squares[p]
-                + 0.25 * less(cubes[p], third)
+                (3.0 * f * f - 3.0 * f) * rest[p] + (3.0 * f - 1.5) * squares[p] + cubes[p]
             )
+            factor[p] = 1.5 - 1.5 * f * f + f * f * f
+            small[p] = rest[p].astype(BF16)
+        for p in each:
+            narrow = tail[p].astype(BF16)
+            if step < ITERS - 1:
+                both = dot(jnp.concatenate([small[p], narrow], axis=0), small[p])
+                squares[p], cross = both[:members], both[members:]
+            else:
+                cross = dot(narrow, small[p])
+            tail[p] = factor[p] * tail[p] + lead[p] * rest[p] + cross
+            lead[p] = factor[p] * lead[p]
     for p in each:
         high = tail[p].astype(BF16)
         root_out[p] = high
@@ -277,9 +250,10 @@
     mine = patches // mem_total
     local, points = state.shape
     ring = lax.axis_size("lon")
-    up = [(i, (i + 1) % ring) for i in range(ring)]
-    down = [(j, i) for i, j in up]
-    here = lax.axis_index("mem").astype(jnp.int32).reshape(1)
+    near = [(i, i + 1 - 2 * (i % 2)) for i in range(ring)]
+    far = [(i, (i - 1 + 2 * (i % 2)) % ring) for i in range(ring)]
+    odd = lax.axis_index("lon") % 2
+    here = jnp.stack([lax.axis_index("mem"), 2 * odd, 2 - 2 * odd]).astype(jnp.int32)
     shape = jax.ShapeDtypeStruct
     padded = members + PAD
 
@@ -288,13 +262,9 @@
     swap = [(i, i + 1 - 2 * (i % PAIR)) for i in range(mem_total)]
 
     pattern = loc_pattern.T
-    before = lax.ppermute(pattern, "lon", up)
-    after = lax.ppermute(pattern, "lon", down)
+    far_pattern = lax.ppermute(pattern, "lon", far)
+    near_pattern = lax.ppermute(pattern, "lon", near)
     paired = lax.ppermute(state, "mem", swap)
-    operands = [
-        pltpu.VMEM((padded, uses * width), BF16),
-        pltpu.VMEM((members, uses * width), BF16),
-    ]
     limit = pltpu.CompilerParams(vmem_limit_bytes=16 * 1024 * 1024)
     gram = 2 * padded * members * uses * width
     pert, weights, innov = pl.pallas_call(
@@ -322,32 +292,37 @@
     )(*(stay(value) for value in (obs_count, hx, obs_value, obs_rinv)))
     packed = shape((mine, padded, members // 2), BF16)
     slab = shape((PAIR, local, span), BF16)
-    to_before, to_after, *slabs = pl.pallas_call(
-        functools.partial(neighbour_kernel, patches),
-        out_shape=(packed, packed) + (slab,) * length,
-        in_specs=[SMEM] * 3 + [VMEM] * 3 + [HBM] * 2,
-        out_specs=(VMEM,) * (2 + length),
-        scratch_shapes=operands + [pltpu.SemaphoreType.DMA((PAIR * length,))],
-        compiler_params=limit,
-        cost_estimate=pl.CostEstimate(
-            flops=2 * mine * gram, bytes_accessed=hx.size * 2, transcendentals=0
-        ),
-        name="neighbour_share",
-    )(here, before, after, pert, weights, innov, state, paired)
+    cost = pl.CostEstimate(flops=mine * gram, bytes_accessed=hx.size, transcendentals=0)
+    to_far = pl.pallas_call(
+        functools.partial(far_kernel, patches, 2),
+        out_shape=packed,
+        in_specs=[SMEM] * 2 + [VMEM] * 3,
+        out_specs=VMEM,
+        compiler_params=limit,
+        cost_estimate=cost,
+        name="far_share",
+    )(here, far_pattern, pert, weights, innov)
+    from_far = lax.ppermute(to_far, "lon", far)
+    to_near, *slabs = pl.pallas_call(
+        functools.partial(near_kernel, patches, 1),
+        out_shape=(packed,) + (slab,) * length,
+        in_specs=[SMEM] * 2 + [VMEM] * 3 + [HBM] * 2 + [pl.BlockSpec(memory_space=pl.ANY)],
+        out_specs=(VMEM,) * (1 + length),
+        scratch_shapes=[pltpu.SemaphoreType.DMA((PAIR * length,))],
+        compiler_params=limit,
+        cost_estimate=cost,
+        name="near_share",
+    )(here, near_pattern, pert, weights, innov, state, paired, to_far)
+    from_near = lax.ppermute(to_near, "lon", near)
     own = pl.pallas_call(
         functools.partial(own_kernel, patches),
         out_shape=shape((mine, padded, members), F32),
         in_specs=[SMEM] * 2 + [VMEM] * 3 + [pl.BlockSpec(memory_space=pl.ANY)],
         out_specs=VMEM,
-        scratch_shapes=operands,
-        compiler_params=limit,
-        cost_estimate=pl.CostEstimate(
-            flops=mine * gram, bytes_accessed=2 * hx.size, transcendentals=0
-        ),
+        compiler_params=limit,
+        cost_estimate=cost,
         name="own_share",
-    )(here, pattern, pert, weights, innov, to_before)
-    from_before = lax.ppermute(to_after, "lon", up)
-    from_after = lax.ppermute(to_before, "lon", down)
+    )(here, pattern, pert, weights, innov, to_near)
     for shift in range(1, length):
         turn = [(i, (i + shift * PAIR) % mem_total) for i in range(mem_total)]
         slabs[shift] = lax.ppermute(slabs[shift], "mem", turn)
@@ -361,7 +336,7 @@
             flops=mine * 15 * 2 * members**3, bytes_accessed=2**20, transcendentals=0
         ),
         name="root",
-    )(own, from_before, from_after)
+    )(own, from_far, from_near)
     updated = pl.pallas_call(
         apply_kernel,
         out_shape=shape((members, span), BF16),

time: 33.2 us -> 32.7 us (0.985)
  blocking collectives: 10.2 us -> 11.4 us
  starting transfers between devices: 11 us -> 10.3 us
  Pallas kernels: 10 us -> 9.32 us
  waiting for transfers between devices: 1.11 us -> 0.66 us
    ppermute x1, starting transfers between devices: 2.94 us -> 1.49 us  [body(): paired = lax.ppermute(state, 'mem', swap)]
    all_to_all x1, blocking collectives: 10.2 us -> 11.4 us  [body(): lax.all_to_all(updated.reshape(mem_total, local, span), 'mem', split_axis...]
    ppermute x4, waiting for transfers between devices: 1.1 us -> 0.01 us  [the longest x1 0.01 us: body(): far_pattern = lax.ppermute(pattern, 'lon', far)]
    pallas_call x1, Pallas kernels: 3.37 us -> 2.45 us  [body(): pl.pallas_call(root_kernel, out_shape=(shape((mine, members, members), BF...]
    ppermute x4, starting transfers between devices: 2.47 us -> 3.22 us  [the longest x1 2.41 us: body(): far_pattern = lax.ppermute(pattern, 'lon', far)]
    ppermute x1, waiting for transfers between devices: 0.01 us -> 0.64 us  [body(): paired = lax.ppermute(state, 'mem', swap)]
    pallas_call x1, Pallas kernels: 0.67 us -> 1.21 us  [body(): pl.pallas_call(apply_kernel, out_shape=shape((members, span), BF16), in_s...]
    pallas_call x1, Pallas kernels: 1.45 us -> 1.11 us  [body(): pl.pallas_call(functools.partial(own_kernel, patches), out_shape=shape((m...]
  transfers between devices with their start and end apart: 8 -> 8, of which waited for: 1 -> 1; matrix products, arithmetic and copies ran while one was open for 0% -> 0% of each run, Pallas kernels for 21% -> 25%
where the time goes in v2:
time: 32.7 us; the launch traced here: 32.6 us
  blocking collectives  11.4 us (35%)
  starting transfers between devices  10.3 us (31%)
  Pallas kernels  9.32 us (29%)
  local copies, waits for them, and re-layouts  0.67 us (2%)
  waiting for transfers between devices  0.66 us (2%)
    all_to_all x1, blocking collectives, body(): lax.all_to_all(updated.reshape(mem_total, local, span), 'mem', split_axis...  11.4 us
    ppermute x3, starting transfers between devices, body(): slabs[shift] = lax.ppermute(slabs[shift], 'mem', turn)  5.57 us
    pallas_call x1, Pallas kernels, body(): pl.pallas_call(root_kernel, out_shape=(shape((mine, members, members), BF...  2.45 us
    ppermute x1, starting transfers between devices, body(): far_pattern = lax.ppermute(pattern, 'lon', far)  2.41 us
    pallas_call x1, Pallas kernels, body(): pl.pallas_call(perturb_kernel, out_shape=(shape((blocks, members, width),...  2.15 us
    ppermute x1, starting transfers between devices, body(): paired = lax.ppermute(state, 'mem', swap)  1.49 us
    pallas_call x1, Pallas kernels, body(): pl.pallas_call(functools.partial(near_kernel, patches, 1), out_shape=(pac...  1.27 us
    pallas_call x1, Pallas kernels, body(): pl.pallas_call(apply_kernel, out_shape=shape((members, span), BF16), in_s...  1.21 us
  transfers between devices with their start and end apart: 8, of which 1 were waited for; matrix products, arithmetic and copies ran while one was open for 0% of the time, Pallas kernels for 25%

profile of v2, /device:TPU:0, one launch (start us, length us, event | category | flops | bytes accessed | tf_op | source)
XLA Modules:
  0.0 32.6 jit_solution(7564710346075412222)
XLA Ops:
  0.0 2.4 %collective-permute-start.2 = (s32[8,16]{1,0:T(8,128)}, s32[8,16]{1,0:T(8,128)S(1)}, u32[]{:S(2)}, u32[]{:S(2)}) collective-permute-start(s32[8,16]{1,0:T(8,128)} %bitcast.9), channel_id=1, source_target_pairs={{0,3},{1,2},{2,1},{3,0},{4,7},{5,6},{6,5},{7,4},{8,11},{9,10},{10,... | collective-permute-start | bytes 1544 | tf_op jit(solution)/shard_map/ppermute | solution.py:265
  2.4 0.7 %collective-permute-start = (s32[8,16]{1,0:T(8,128)}, s32[8,16]{1,0:T(8,128)S(1)}, u32[]{:S(2)}, u32[]{:S(2)}) collective-permute-start(s32[8,16]{1,0:T(8,128)} %bitcast.10), channel_id=1, source_target_pairs={{0,1},{1,0},{2,3},{3,2},{4,5},{5,4},{6,7},{7,6},{8,9},{9,8},{10,11... | collective-permute-start | bytes 1544 | tf_op jit(solution)/shard_map/ppermute | solution.py:266
  3.1 1.5 %collective-permute-start.1 = (bf16[32,2048]{1,0:T(8,128)(2,1)}, bf16[32,2048]{1,0:T(8,128)(2,1)S(1)}, u32[]{:S(2)}, u32[]{:S(2)}) collective-permute-start(bf16[32,2048]{1,0:T(8,128)(2,1)} %state.1), channel_id=1, source_target_pairs={{0,4},{4,0},{8,12},{12,8},{16,20},{20,16},{24,28},{28,24},{1,5},{5... | collective-permute-start | bytes 393224 | tf_op jit(solution)/shard_map/ppermute | solution.py:267
  4.6 0.1 pad_add_fusion.here
  4.7 0.0 copy-start
  4.7 2.2 %perturb.1 = (bf16[32,256,128]{2,1,0:T(8,128)(2,1)S(1)}, f32[32,128]{1,0:T(8,128)S(1)}, f32[32,128]{1,0:T(8,128)S(1)}) custom-call(s32[32]{0:T(128)} %count_all.1, bf16[32,256,128]{2,1,0:T(8,128)(2,1)} %hx.1, f32[32,128]{1,0:T(8,128)} %value_all.1, f32[32,128]{1,0:T(8,128)} %rinv_all.1), custom_call_target="tpu_custom_call" | custom-call | flops 4194304 | bytes 4194304 | tf_op jit(solution)/shard_map/perturb/pallas_call | solution.py:270
  6.8 0.0 collective-permute-done.2.pattern
  6.8 0.0 copy-start.1
  6.8 1.1 %far_share.1.sent = bf16[2,272,128]{2,1,0:T(8,128)(2,1)S(1)} custom-call(s32[3]{0:T(128)S(1)} %pad_add_fusion.here, s32[8,16]{1,0:T(8,128)S(1)} %collective-permute-done.2.pattern, bf16[32,256,128]{2,1,0:T(8,128)(2,1)S(1)} %get-tuple-element.15.pert, f32[32,128]{1,0:T(8,128)S(1)} %get-tuple-element.16.weights, f32[32,128]{1,0:T(8,128)S(1)} %get-tuple-element.17.innov), custom_call_target="tpu_custom_call" | custom-call | flops 285212672 | bytes 1048576 | tf_op jit(solution)/shard_map/far_share/pallas_call | solution.py:296
  8.0 0.1 collective-permute-start.3
  8.0 0.0 collective-permute-done.pattern
  8.1 0.6 %collective-permute-done.1.paired = bf16[32,2048]{1,0:T(8,128)(2,1)S(1)} collective-permute-done((bf16[32,2048]{1,0:T(8,128)(2,1)}, bf16[32,2048]{1,0:T(8,128)(2,1)S(1)}, u32[]{:S(2)}, u32[]{:S(2)}) %collective-permute-start.1) | collective-permute-done | bytes 131104 | tf_op jit(solution)/shard_map/ppermute | solution.py:267
  8.7 0.0 copy-done
  8.7 1.3 %near_share.1 = (bf16[2,272,128]{2,1,0:T(8,128)(2,1)S(1)}, bf16[2,32,256]{2,1,0:T(8,128)(2,1)S(1)}, bf16[2,32,256]{2,1,0:T(8,128)(2,1)S(1)}, bf16[2,32,256]{2,1,0:T(8,128)(2,1)S(1)}, bf16[2,32,256]{2,1,0:T(8,128)(2,1)S(1)}) custom-call(s32[3]{0:T(128)S(1)} %pad_add_fusion.here, s32[8,16]{1,0:T(8,128)S(1)} %collective-permute-done.pattern, ...), custom_call_target="tpu_custom_call" | custom-call | flops 285212672 | bytes 1048576 | tf_op jit(solution)/shard_map/near_share/pallas_call | solution.py:306
  10.0 0.1 collective-permute-start.4
  10.1 1.6 %collective-permute-start.5 = (bf16[2,32,256]{2,1,0:T(8,128)(2,1)S(1)}, bf16[2,32,256]{2,1,0:T(8,128)(2,1)S(1)}, u32[]{:S(2)}, u32[]{:S(2)}) collective-permute-start(bf16[2,32,256]{2,1,0:T(8,128)(2,1)S(1)} %get-tuple-element.22), channel_id=1, source_target_pairs={{0,8},{4,12},{8,16},{12,20},{16,24},{20,28},{24,0},{28,4},{1,9},{5... | collective-permute-start | bytes 98312 | tf_op jit(solution)/shard_map/ppermute | solution.py:328
  11.7 2.6 %collective-permute-start.6 = (bf16[2,32,256]{2,1,0:T(8,128)(2,1)S(1)}, bf16[2,32,256]{2,1,0:T(8,128)(2,1)S(1)}, u32[]{:S(2)}, u32[]{:S(2)}) collective-permute-start(bf16[2,32,256]{2,1,0:T(8,128)(2,1)S(1)} %get-tuple-element.23), channel_id=1, source_target_pairs={{0,16},{4,20},{8,24},{12,28},{16,0},{20,4},{24,8},{28,12},{1,17},{... | collective-permute-start | bytes 98312 | tf_op jit(solution)/shard_map/ppermute | solution.py:328
  14.3 1.3 %collective-permute-start.7 = (bf16[2,32,256]{2,1,0:T(8,128)(2,1)S(1)}, bf16[2,32,256]{2,1,0:T(8,128)(2,1)S(1)}, u32[]{:S(2)}, u32[]{:S(2)}) collective-permute-start(bf16[2,32,256]{2,1,0:T(8,128)(2,1)S(1)} %get-tuple-element.24), channel_id=1, source_target_pairs={{0,24},{4,28},{8,0},{12,4},{16,8},{20,12},{24,16},{28,20},{1,25},{... | collective-permute-start | bytes 98312 | tf_op jit(solution)/shard_map/ppermute | solution.py:328
  15.6 0.0 copy-done.1
  15.6 1.1 %own_share.1.own = f32[2,272,256]{2,1,0:T(8,128)S(1)} custom-call(s32[3]{0:T(128)S(1)} %pad_add_fusion.here, s32[8,16]{1,0:T(8,128)S(1)} %bitcast.11, bf16[32,256,128]{2,1,0:T(8,128)(2,1)S(1)} %get-tuple-element.15.pert, f32[32,128]{1,0:T(8,128)S(1)} %get-tuple-element.16.weights, f32[32,128]{1,0:T(8,128)S(1)} %get-tuple-element.17.innov, ...), custom_call_target="tpu_custom_call" | custom-call | flops 285212672 | bytes 1048576 | tf_op jit(solution)/shard_map/own_share/pallas_call | solution.py:317
  16.7 0.0 collective-permute-done.3.before
  16.8 0.0 collective-permute-done.4.after
  16.8 2.4 %root.1 = (bf16[2,256,256]{2,1,0:T(8,128)(2,1)S(1)}, f32[2,16,256]{2,1,0:T(8,128)S(1)}) custom-call(f32[2,272,256]{2,1,0:T(8,128)S(1)} %own_share.1.own, bf16[2,272,128]{2,1,0:T(8,128)(2,1)S(1)} %collective-permute-done.3.before, bf16[2,272,128]{2,1,0:T(8,128)(2,1)S(1)} %collective-permute-done.4.after), custom_call_target="tpu_custom_call" | custom-call | flops 1006632960 | bytes 1048576 | tf_op jit(solution)/shard_map/root/pallas_call | solution.py:329
  19.2 0.0 collective-permute-done.5.rest_1_
  19.2 0.0 collective-permute-done.6.rest_2_
  19.2 0.0 collective-permute-done.7.rest_3_
  19.2 1.2 %apply.1 = bf16[256,256]{1,0:T(8,128)(2,1)S(1)} custom-call(s32[3]{0:T(128)S(1)} %pad_add_fusion.here, bf16[2,256,256]{2,1,0:T(8,128)(2,1)S(1)} %get-tuple-element.19.root, f32[2,16,256]{2,1,0:T(8,128)S(1)} %get-tuple-element.20.rows, bf16[2,32,256]{2,1,0:T(8,128)(2,1)S(1)} %get-tuple-element.21.rest_0_, ...), custom_call_target="tpu_custom_call" | custom-call | flops 33554432 | bytes 524288 | tf_op jit(solution)/shard_map/apply/pallas_call | solution.py:340
  20.5 11.4 %all_to_all.5 = bf16[8,32,256]{2,1,0:T(8,128)(2,1)S(1)} all-to-all(bf16[8,32,256]{2,1,0:T(8,128)(2,1)S(1)} %bitcast.8), channel_id=1, replica_groups=mesh['mem'=8,'lon'=4] {'mem'}, dimensions={0} | all-to-all | bytes 262144 | tf_op jit(solution)/shard_map/all_to_all | solution.py:352
  31.9 0.7 %copy.8 = bf16[8,4,8,256]{3,2,0,1:T(8,128)(2,1)} copy(bf16[8,4,8,256]{3,2,1,0:T(8,128)(2,1)S(1)} %bitcast.12) | data formatting | bytes 262144 | tf_op jit(solution)/shard_map/reshape | solution.py:355
Async XLA Ops:
  0.0 6.8 %collective-permute-start.2 = (s32[8,16]{1,0:T(8,128)}, s32[8,16]{1,0:T(8,128)S(1)}, u32[]{:S(2)}, u32[]{:S(2)}) collective-permute-start(s32[8,16]{1,0:T(8,128)} %bitcast.9), channel_id=1, source_target_pairs={{0,3},{1,2},{2,1},{3,0},{4,7},{5,6},{6,5},{7,4},{8,11},{9,10},{10,... | collective-permute-start | bytes 1544 | tf_op jit(solution)/shard_map/ppermute | solution.py:265
  2.4 5.6 %collective-permute-start = (s32[8,16]{1,0:T(8,128)}, s32[8,16]{1,0:T(8,128)S(1)}, u32[]{:S(2)}, u32[]{:S(2)}) collective-permute-start(s32[8,16]{1,0:T(8,128)} %bitcast.10), channel_id=1, source_target_pairs={{0,1},{1,0},{2,3},{3,2},{4,5},{5,4},{6,7},{7,6},{8,9},{9,8},{10,11... | collective-permute-start | bytes 1544 | tf_op jit(solution)/shard_map/ppermute | solution.py:266
  3.1 5.6 %collective-permute-start.1 = (bf16[32,2048]{1,0:T(8,128)(2,1)}, bf16[32,2048]{1,0:T(8,128)(2,1)S(1)}, u32[]{:S(2)}, u32[]{:S(2)}) collective-permute-start(bf16[32,2048]{1,0:T(8,128)(2,1)} %state.1), channel_id=1, source_target_pairs={{0,4},{4,0},{8,12},{12,8},{16,20},{20,16},{24,28},{28,24},{1,5},{5... | collective-permute-start | bytes 393224 | tf_op jit(solution)/shard_map/ppermute | solution.py:267
  4.7 4.1 %copy-start = (bf16[32,2048]{1,0:T(8,128)(2,1)S(1)}, bf16[32,2048]{1,0:T(8,128)(2,1)}, u32[]{:S(2)}) copy-start(bf16[32,2048]{1,0:T(8,128)(2,1)} %state.1) | copy-start | bytes 393220
  6.8 8.8 %copy-start.1 = (s32[16,8]{0,1:T(8,128)S(1)}, s32[16,8]{0,1:T(8,128)}, u32[]{:S(2)}) copy-start(s32[16,8]{0,1:T(8,128)} %param.11) | copy-start | bytes 1540
  8.0 8.8 %collective-permute-start.3 = (bf16[2,272,128]{2,1,0:T(8,128)(2,1)S(1)}, bf16[2,272,128]{2,1,0:T(8,128)(2,1)S(1)}, u32[]{:S(2)}, u32[]{:S(2)}) collective-permute-start(bf16[2,272,128]{2,1,0:T(8,128)(2,1)S(1)} %far_share.1.sent), channel_id=1, source_target_pairs={{0,3},{1,2},{2,1},{3,0},{4,7},{5,6},{6,5},{7,4},{8,11},{9,10},{10,... | collective-permute-start | bytes 417800 | tf_op jit(solution)/shard_map/ppermute | solution.py:305
  10.0 6.8 %collective-permute-start.4 = (bf16[2,272,128]{2,1,0:T(8,128)(2,1)S(1)}, bf16[2,272,128]{2,1,0:T(8,128)(2,1)S(1)}, u32[]{:S(2)}, u32[]{:S(2)}) collective-permute-start(bf16[2,272,128]{2,1,0:T(8,128)(2,1)S(1)} %get-tuple-element.18.sent), channel_id=1, source_target_pairs={{0,1},{1,0},{2,3},{3,2},{4,5},{5,4},{6,7},{7,6},{8,9},{9,8},{10,11... | collective-permute-start | bytes 417800 | tf_op jit(solution)/shard_map/ppermute | solution.py:316
  10.1 9.2 %collective-permute-start.5 = (bf16[2,32,256]{2,1,0:T(8,128)(2,1)S(1)}, bf16[2,32,256]{2,1,0:T(8,128)(2,1)S(1)}, u32[]{:S(2)}, u32[]{:S(2)}) collective-permute-start(bf16[2,32,256]{2,1,0:T(8,128)(2,1)S(1)} %get-tuple-element.22), channel_id=1, source_target_pairs={{0,8},{4,12},{8,16},{12,20},{16,24},{20,28},{24,0},{28,4},{1,9},{5... | collective-permute-start | bytes 98312 | tf_op jit(solution)/shard_map/ppermute | solution.py:328
  11.7 7.5 %collective-permute-start.6 = (bf16[2,32,256]{2,1,0:T(8,128)(2,1)S(1)}, bf16[2,32,256]{2,1,0:T(8,128)(2,1)S(1)}, u32[]{:S(2)}, u32[]{:S(2)}) collective-permute-start(bf16[2,32,256]{2,1,0:T(8,128)(2,1)S(1)} %get-tuple-element.23), channel_id=1, source_target_pairs={{0,16},{4,20},{8,24},{12,28},{16,0},{20,4},{24,8},{28,12},{1,17},{... | collective-permute-start | bytes 98312 | tf_op jit(solution)/shard_map/ppermute | solution.py:328
  14.3 5.0 %collective-permute-start.7 = (bf16[2,32,256]{2,1,0:T(8,128)(2,1)S(1)}, bf16[2,32,256]{2,1,0:T(8,128)(2,1)S(1)}, u32[]{:S(2)}, u32[]{:S(2)}) collective-permute-start(bf16[2,32,256]{2,1,0:T(8,128)(2,1)S(1)} %get-tuple-element.24), channel_id=1, source_target_pairs={{0,24},{4,28},{8,0},{12,4},{16,8},{20,12},{24,16},{28,20},{1,25},{... | collective-permute-start | bytes 98312 | tf_op jit(solution)/shard_map/ppermute | solution.py:328

commit v3 on v2

--- a/solution.py
+++ b/solution.py
@@ -118,14 +118,14 @@
     out[patch, members:, :] = tail.astype(BF16)
 
 
-def far_kernel(patches, side, here, pattern, pert, weights, innov, out):
+def far_kernel(patches, here, side, pattern, pert, weights, innov, out):
     mine = out.shape[0]
     for patch in range(mine):
         row = here[0] * mine + patch
-        pack(share(pattern, row, here[side], patches, pert, weights, innov), out, patch)
-
-
-def near_kernel(patches, side, here, pattern, pert, weights, innov, state, paired, sent, out, *rest):
+        pack(share(pattern, row, side[0], patches, pert, weights, innov), out, patch)
+
+
+def near_kernel(patches, here, side, pattern, pert, weights, innov, state, paired, sent, out, *rest):
     slabs, sems = rest[:-1], rest[-1]
     span = slabs[0].shape[2]
     length = len(slabs)
@@ -139,7 +139,7 @@
     moves = [pltpu.make_async_copy(*move, sems.at[i]) for i, move in enumerate(moves)]
     for move in moves:
         move.start()
-    far_kernel(patches, side, here, pattern, pert, weights, innov, out)
+    far_kernel(patches, here, side, pattern, pert, weights, innov, out)
     for move in moves:
         move.wait()
 
@@ -220,8 +220,15 @@
         rows_out[p] = jnp.where(index == 0, gain, jnp.where(index == 1, lead[p], spread))
 
 
+def partner(here, shift, count):
+    assert count & (count - 1) == 0
+    return here ^ shift
+
+
 def apply_kernel(here, root, rows, *rest):
-    slabs, (out, columns) = rest[:-2], rest[-2:]
+    columns, out = rest[-2:]
+    count = (len(rest) - 2) * PAIR // (PAIR + 1)
+    slabs, pieces = rest[: count // PAIR], rest[count // PAIR : -2]
     mine, members, _ = root.shape
     points = out.shape[1] // mine
     length = len(slabs)
@@ -241,6 +248,21 @@
         )
         shift = mean + product(split(rows[p]), split(spread))[0:1]
         out[:, cols] = (shift + rows[p, 2:3, :points] * spread).astype(BF16)
+    for shift, piece in enumerate(pieces):
+        target = partner(here[0], shift, count)
+        piece[...] = out[pl.ds(pl.multiple_of(target * local, local), local), :]
+
+
+def layout_kernel(here, *rest):
+    pieces, (out, whole, sem) = rest[:-3], rest[-3:]
+    count = len(pieces)
+    _, span = pieces[0].shape
+    for shift, piece in enumerate(pieces):
+        source = partner(here[0], shift, count)
+        whole[:, pl.ds(pl.multiple_of(source * span, span), span)] = piece[...]
+    copy = pltpu.make_async_copy(whole, out, sem)
+    copy.start()
+    copy.wait()
 
 
 def body(state, hx, obs_value, obs_rinv, obs_count, loc_pattern):
@@ -253,7 +275,9 @@
     near = [(i, i + 1 - 2 * (i % 2)) for i in range(ring)]
     far = [(i, (i - 1 + 2 * (i % 2)) % ring) for i in range(ring)]
     odd = lax.axis_index("lon") % 2
-    here = jnp.stack([lax.axis_index("mem"), 2 * odd, 2 - 2 * odd]).astype(jnp.int32)
+    here, near_side, far_side = (
+        value.astype(jnp.int32).reshape(1) for value in (lax.axis_index("mem"), 2 * odd, 2 - 2 * odd)
+    )
     shape = jax.ShapeDtypeStruct
     padded = members + PAD
 
@@ -294,25 +318,25 @@
     slab = shape((PAIR, local, span), BF16)
     cost = pl.CostEstimate(flops=mine * gram, bytes_accessed=hx.size, transcendentals=0)
     to_far = pl.pallas_call(
-        functools.partial(far_kernel, patches, 2),
+        functools.partial(far_kernel, patches),
         out_shape=packed,
-        in_specs=[SMEM] * 2 + [VMEM] * 3,
+        in_specs=[SMEM] * 3 + [VMEM] * 3,
         out_specs=VMEM,
         compiler_params=limit,
         cost_estimate=cost,
         name="far_share",
-    )(here, far_pattern, pert, weights, innov)
+    )(here, far_side, far_pattern, pert, weights, innov)
     from_far = lax.ppermute(to_far, "lon", far)
     to_near, *slabs = pl.pallas_call(
-        functools.partial(near_kernel, patches, 1),
+        functools.partial(near_kernel, patches),
         out_shape=(packed,) + (slab,) * length,
-        in_specs=[SMEM] * 2 + [VMEM] * 3 + [HBM] * 2 + [pl.BlockSpec(memory_space=pl.ANY)],
+        in_specs=[SMEM] * 3 + [VMEM] * 3 + [HBM] * 2 + [pl.BlockSpec(memory_space=pl.ANY)],
         out_specs=(VMEM,) * (1 + length),
         scratch_shapes=[pltpu.SemaphoreType.DMA((PAIR * length,))],
         compiler_params=limit,
         cost_estimate=cost,
         name="near_share",
-    )(here, near_pattern, pert, weights, innov, state, paired, to_far)
+    )(here, near_side, near_pattern, pert, weights, innov, state, paired, to_far)
     from_near = lax.ppermute(to_near, "lon", near)
     own = pl.pallas_call(
         functools.partial(own_kernel, patches),
@@ -337,22 +361,31 @@
         ),
         name="root",
     )(own, from_far, from_near)
-    updated = pl.pallas_call(
+    pieces = pl.pallas_call(
         apply_kernel,
-        out_shape=shape((members, span), BF16),
+        out_shape=(shape((local, span), BF16),) * mem_total,
         in_specs=[SMEM] + [VMEM] * (2 + length),
-        out_specs=VMEM,
-        scratch_shapes=[pltpu.VMEM((members, span), BF16)],
+        out_specs=(VMEM,) * mem_total,
+        scratch_shapes=[pltpu.VMEM((members, span), BF16)] * 2,
         compiler_params=limit,
         cost_estimate=pl.CostEstimate(
             flops=2 * members**2 * span, bytes_accessed=2**19, transcendentals=0
         ),
         name="apply",
     )(here, root, rows, *slabs)
-    pieces = lax.all_to_all(
-        updated.reshape(mem_total, local, span), "mem", split_axis=0, concat_axis=0
-    )
-    return jnp.swapaxes(pieces, 0, 1).reshape(local, points)
+    pieces = list(pieces)
+    for shift in range(1, mem_total):
+        swap = [(i, partner(i, shift, mem_total)) for i in range(mem_total)]
+        pieces[shift] = lax.ppermute(pieces[shift], "mem", swap)
+    return pl.pallas_call(
+        layout_kernel,
+        out_shape=shape((local, points), BF16),
+        in_specs=[SMEM] + [VMEM] * mem_total,
+        out_specs=HBM,
+        scratch_shapes=[pltpu.VMEM((local, points), BF16), pltpu.SemaphoreType.DMA],
+        compiler_params=limit,
+        name="layout",
+    )(here, *pieces)
 
 
 def solution(mesh):

time: 32.7 us -> 36 us (1.10)
  starting transfers between devices: 10.3 us -> 22.5 us
  blocking collectives: 11.4 us -> 0 us
  waiting for transfers between devices: 0.66 us -> 3.8 us
  local copies, waits for them, and re-layouts: 0.67 us -> 0.01 us
    all_to_all x1 -> x0, blocking collectives: 11.4 us -> none  [body(): lax.all_to_all(updated.reshape(mem_total, local, span), 'mem', split_axis...]
    ppermute x0 -> x7, starting transfers between devices: none -> 11.2 us  [body(): pieces[shift] = lax.ppermute(pieces[shift], 'mem', swap)]
    ppermute x0 -> x7, waiting for transfers between devices: none -> 3.78 us  [body(): pieces[shift] = lax.ppermute(pieces[shift], 'mem', swap)]
    ppermute x1, starting transfers between devices: 2.41 us -> 0.68 us  [body(): far_pattern = lax.ppermute(pattern, 'lon', far)]
    ppermute x1, starting transfers between devices: 1.49 us -> 2.94 us  [body(): paired = lax.ppermute(state, 'mem', swap)]
    reshape x1 -> x0, local copies, waits for them, and re-layouts: 0.66 us -> none  [body(): return jnp.swapaxes(pieces, 0, 1).reshape(local, points)]
    ppermute x1, starting transfers between devices: 0.07 us -> 0.73 us  [body(): from_near = lax.ppermute(to_near, 'lon', near)]
    ppermute x1, waiting for transfers between devices: 0.64 us -> 0.01 us  [body(): paired = lax.ppermute(state, 'mem', swap)]
  transfers between devices with their start and end apart: 8 -> 15, of which waited for: 1 -> 2; matrix products, arithmetic and copies ran while one was open for 0% -> 0% of each run, Pallas kernels for 25% -> 23%
where the time goes in v3:
time: 36 us; the launch traced here: 35.9 us
  starting transfers between devices  22.5 us (62%)
  Pallas kernels  9.47 us (26%)
  waiting for transfers between devices  3.8 us (11%)
    ppermute x7, starting transfers between devices, body(): pieces[shift] = lax.ppermute(pieces[shift], 'mem', swap)  11.2 us
    ppermute x3, starting transfers between devices, body(): slabs[shift] = lax.ppermute(slabs[shift], 'mem', turn)  5.51 us
    ppermute x7, waiting for transfers between devices, body(): pieces[shift] = lax.ppermute(pieces[shift], 'mem', swap)  3.78 us
    ppermute x1, starting transfers between devices, body(): paired = lax.ppermute(state, 'mem', swap)  2.94 us
    pallas_call x1, Pallas kernels, body(): pl.pallas_call(root_kernel, out_shape=(shape((mine, members, members), BF...  2.45 us
    pallas_call x1, Pallas kernels, body(): pl.pallas_call(perturb_kernel, out_shape=(shape((blocks, members, width),...  2.15 us
    pallas_call x1, Pallas kernels, body(): pl.pallas_call(functools.partial(near_kernel, patches), out_shape=(packed...  1.28 us
    pallas_call x1, Pallas kernels, body(): pl.pallas_call(functools.partial(far_kernel, patches), out_shape=packed,...  1.12 us
  transfers between devices with their start and end apart: 15, of which 2 were waited for; matrix products, arithmetic and copies ran while one was open for 0% of the time, Pallas kernels for 23%

profile of v3, /device:TPU:0, one launch (start us, length us, event | category | flops | bytes accessed | tf_op | source)
XLA Modules:
  0.0 35.9 jit_solution(6083249467733286852)
XLA Ops:
  0.0 2.9 %collective-permute-start.1 = (bf16[32,2048]{1,0:T(8,128)(2,1)}, bf16[32,2048]{1,0:T(8,128)(2,1)S(1)}, u32[]{:S(2)}, u32[]{:S(2)}) collective-permute-start(bf16[32,2048]{1,0:T(8,128)(2,1)} %state.1), channel_id=1, source_target_pairs={{0,4},{4,0},{8,12},{12,8},{16,20},{20,16},{24,28},{28,24},{1,5},{5... | collective-permute-start | bytes 393224 | tf_op jit(solution)/shard_map/ppermute | solution.py:291
  2.9 0.7 %collective-permute-start.2 = (s32[8,16]{1,0:T(8,128)}, s32[8,16]{1,0:T(8,128)S(1)}, u32[]{:S(2)}, u32[]{:S(2)}) collective-permute-start(s32[8,16]{1,0:T(8,128)} %bitcast.4), channel_id=1, source_target_pairs={{0,3},{1,2},{2,1},{3,0},{4,7},{5,6},{6,5},{7,4},{8,11},{9,10},{10,... | collective-permute-start | bytes 1544 | tf_op jit(solution)/shard_map/ppermute | solution.py:289
  3.6 1.0 %collective-permute-start = (s32[8,16]{1,0:T(8,128)}, s32[8,16]{1,0:T(8,128)S(1)}, u32[]{:S(2)}, u32[]{:S(2)}) collective-permute-start(s32[8,16]{1,0:T(8,128)} %bitcast.5), channel_id=1, source_target_pairs={{0,1},{1,0},{2,3},{3,2},{4,5},{5,4},{6,7},{7,6},{8,9},{9,8},{10,11... | collective-permute-start | bytes 1544 | tf_op jit(solution)/shard_map/ppermute | solution.py:290
  4.6 0.0 copy-start
  4.6 2.2 %perturb.1 = (bf16[32,256,128]{2,1,0:T(8,128)(2,1)S(1)}, f32[32,128]{1,0:T(8,128)S(1)}, f32[32,128]{1,0:T(8,128)S(1)}) custom-call(s32[32]{0:T(128)} %count_all.1, bf16[32,256,128]{2,1,0:T(8,128)(2,1)} %hx.1, f32[32,128]{1,0:T(8,128)} %value_all.1, f32[32,128]{1,0:T(8,128)} %rinv_all.1), custom_call_target="tpu_custom_call" | custom-call | flops 4194304 | bytes 4194304 | tf_op jit(solution)/shard_map/perturb/pallas_call | solution.py:294
  6.7 0.0 collective-permute-done.2.pattern
  6.7 0.0 copy-start.1
  6.8 1.1 %far_share.1.sent = bf16[2,272,128]{2,1,0:T(8,128)(2,1)S(1)} custom-call(s32[1]{0:T(128)} %bitcast.here, s32[1]{0:T(128)} %bitcast.3.side, s32[8,16]{1,0:T(8,128)S(1)} %collective-permute-done.2.pattern, bf16[32,256,128]{2,1,0:T(8,128)(2,1)S(1)} %get-tuple-element.23.pert, f32[32,128]{1,0:T(8,128)S(1)} %get-tuple-element.24.weights, ...), custom_call_target="tpu_custom_call" | custom-call | flops 285212672 | bytes 1048576 | tf_op jit(solution)/shard_map/far_share/pallas_call | solution.py:320
  7.9 0.5 %collective-permute-start.3 = (bf16[2,272,128]{2,1,0:T(8,128)(2,1)S(1)}, bf16[2,272,128]{2,1,0:T(8,128)(2,1)S(1)}, u32[]{:S(2)}, u32[]{:S(2)}) collective-permute-start(bf16[2,272,128]{2,1,0:T(8,128)(2,1)S(1)} %far_share.1.sent), channel_id=1, source_target_pairs={{0,3},{1,2},{2,1},{3,0},{4,7},{5,6},{6,5},{7,4},{8,11},{9,10},{10,... | collective-permute-start | bytes 417800 | tf_op jit(solution)/shard_map/ppermute | solution.py:329
  8.3 0.0 collective-permute-done.pattern
  8.3 0.0 collective-permute-done.1.paired
  8.4 0.0 copy-done
  8.4 1.3 %near_share.1 = (bf16[2,272,128]{2,1,0:T(8,128)(2,1)S(1)}, bf16[2,32,256]{2,1,0:T(8,128)(2,1)S(1)}, bf16[2,32,256]{2,1,0:T(8,128)(2,1)S(1)}, bf16[2,32,256]{2,1,0:T(8,128)(2,1)S(1)}, bf16[2,32,256]{2,1,0:T(8,128)(2,1)S(1)}) custom-call(s32[1]{0:T(128)} %bitcast.here, s32[1]{0:T(128)} %bitcast.2.side, s32[8,16]{1,0:T(8,128)S(1)} %collective-permute-done.pattern, ...), custom_call_target="tpu_custom_call" | custom-call | flops 285212672 | bytes 1048576 | tf_op jit(solution)/shard_map/near_share/pallas_call | solution.py:330
  9.6 0.7 %collective-permute-start.4 = (bf16[2,272,128]{2,1,0:T(8,128)(2,1)S(1)}, bf16[2,272,128]{2,1,0:T(8,128)(2,1)S(1)}, u32[]{:S(2)}, u32[]{:S(2)}) collective-permute-start(bf16[2,272,128]{2,1,0:T(8,128)(2,1)S(1)} %get-tuple-element.26.sent), channel_id=1, source_target_pairs={{0,1},{1,0},{2,3},{3,2},{4,5},{5,4},{6,7},{7,6},{8,9},{9,8},{10,11... | collective-permute-start | bytes 417800 | tf_op jit(solution)/shard_map/ppermute | solution.py:340
  10.4 1.6 %collective-permute-start.5 = (bf16[2,32,256]{2,1,0:T(8,128)(2,1)S(1)}, bf16[2,32,256]{2,1,0:T(8,128)(2,1)S(1)}, u32[]{:S(2)}, u32[]{:S(2)}) collective-permute-start(bf16[2,32,256]{2,1,0:T(8,128)(2,1)S(1)} %get-tuple-element.30), channel_id=1, source_target_pairs={{0,8},{4,12},{8,16},{12,20},{16,24},{20,28},{24,0},{28,4},{1,9},{5... | collective-permute-start | bytes 98312 | tf_op jit(solution)/shard_map/ppermute | solution.py:352
  12.0 2.6 %collective-permute-start.6 = (bf16[2,32,256]{2,1,0:T(8,128)(2,1)S(1)}, bf16[2,32,256]{2,1,0:T(8,128)(2,1)S(1)}, u32[]{:S(2)}, u32[]{:S(2)}) collective-permute-start(bf16[2,32,256]{2,1,0:T(8,128)(2,1)S(1)} %get-tuple-element.31), channel_id=1, source_target_pairs={{0,16},{4,20},{8,24},{12,28},{16,0},{20,4},{24,8},{28,12},{1,17},{... | collective-permute-start | bytes 98312 | tf_op jit(solution)/shard_map/ppermute | solution.py:352
  14.5 1.3 %collective-permute-start.7 = (bf16[2,32,256]{2,1,0:T(8,128)(2,1)S(1)}, bf16[2,32,256]{2,1,0:T(8,128)(2,1)S(1)}, u32[]{:S(2)}, u32[]{:S(2)}) collective-permute-start(bf16[2,32,256]{2,1,0:T(8,128)(2,1)S(1)} %get-tuple-element.32), channel_id=1, source_target_pairs={{0,24},{4,28},{8,0},{12,4},{16,8},{20,12},{24,16},{28,20},{1,25},{... | collective-permute-start | bytes 98312 | tf_op jit(solution)/shard_map/ppermute | solution.py:352
  15.9 0.0 copy-done.1
  15.9 1.1 %own_share.1.own = f32[2,272,256]{2,1,0:T(8,128)S(1)} custom-call(s32[1]{0:T(128)} %bitcast.here, s32[8,16]{1,0:T(8,128)S(1)} %bitcast.6, bf16[32,256,128]{2,1,0:T(8,128)(2,1)S(1)} %get-tuple-element.23.pert, f32[32,128]{1,0:T(8,128)S(1)} %get-tuple-element.24.weights, f32[32,128]{1,0:T(8,128)S(1)} %get-tuple-element.25.innov, ...), custom_call_target="tpu_custom_call" | custom-call | flops 285212672 | bytes 1048576 | tf_op jit(solution)/shard_map/own_share/pallas_call | solution.py:341
  17.0 0.0 collective-permute-done.3.before
  17.0 0.0 collective-permute-done.4.after
  17.0 2.4 %root.1 = (bf16[2,256,256]{2,1,0:T(8,128)(2,1)S(1)}, f32[2,16,256]{2,1,0:T(8,128)S(1)}) custom-call(f32[2,272,256]{2,1,0:T(8,128)S(1)} %own_share.1.own, bf16[2,272,128]{2,1,0:T(8,128)(2,1)S(1)} %collective-permute-done.3.before, bf16[2,272,128]{2,1,0:T(8,128)(2,1)S(1)} %collective-permute-done.4.after), custom_call_target="tpu_custom_call" | custom-call | flops 1006632960 | bytes 1048576 | tf_op jit(solution)/shard_map/root/pallas_call | solution.py:353
  19.5 0.0 collective-permute-done.5.rest_1_
  19.5 0.0 collective-permute-done.6.rest_2_
  19.5 0.0 collective-permute-done.7.rest_3_
  19.5 0.7 %apply.1 = (bf16[32,256]{1,0:T(8,128)(2,1)S(1)}, bf16[32,256]{1,0:T(8,128)(2,1)S(1)}, bf16[32,256]{1,0:T(8,128)(2,1)S(1)}, bf16[32,256]{1,0:T(8,128)(2,1)S(1)}, ...) custom-call(s32[1]{0:T(128)} %bitcast.here, ...), custom_call_target="tpu_custom_call" | custom-call | flops 33554432 | bytes 524288 | tf_op jit(solution)/shard_map/apply/pallas_call | solution.py:364
  20.2 0.6 %collective-permute-start.8 = (bf16[32,256]{1,0:T(8,128)(2,1)S(1)}, bf16[32,256]{1,0:T(8,128)(2,1)S(1)}, u32[]{:S(2)}, u32[]{:S(2)}) collective-permute-start(bf16[32,256]{1,0:T(8,128)(2,1)S(1)} %get-tuple-element.34), channel_id=1, source_target_pairs={{0,4},{4,0},{8,12},{12,8},{16,20},{20,16},{24,28},{28,24},{1,5},{5... | collective-permute-start | bytes 49160 | tf_op jit(solution)/shard_map/ppermute | solution.py:379
  20.8 0.7 %collective-permute-start.9 = (bf16[32,256]{1,0:T(8,128)(2,1)S(1)}, bf16[32,256]{1,0:T(8,128)(2,1)S(1)}, u32[]{:S(2)}, u32[]{:S(2)}) collective-permute-start(bf16[32,256]{1,0:T(8,128)(2,1)S(1)} %get-tuple-element.35), channel_id=1, source_target_pairs={{0,8},{4,12},{8,0},{12,4},{16,24},{20,28},{24,16},{28,20},{1,9},{5... | collective-permute-start | bytes 49160 | tf_op jit(solution)/shard_map/ppermute | solution.py:379
  21.5 2.3 %collective-permute-start.10 = (bf16[32,256]{1,0:T(8,128)(2,1)S(1)}, bf16[32,256]{1,0:T(8,128)(2,1)S(1)}, u32[]{:S(2)}, u32[]{:S(2)}) collective-permute-start(bf16[32,256]{1,0:T(8,128)(2,1)S(1)} %get-tuple-element.36), channel_id=1, source_target_pairs={{0,12},{4,8},{8,4},{12,0},{16,28},{20,24},{24,20},{28,16},{1,13},{... | collective-permute-start | bytes 49160 | tf_op jit(solution)/shard_map/ppermute | solution.py:379
  23.7 0.6 %collective-permute-start.11 = (bf16[32,256]{1,0:T(8,128)(2,1)S(1)}, bf16[32,256]{1,0:T(8,128)(2,1)S(1)}, u32[]{:S(2)}, u32[]{:S(2)}) collective-permute-start(bf16[32,256]{1,0:T(8,128)(2,1)S(1)} %get-tuple-element.37), channel_id=1, source_target_pairs={{0,16},{4,20},{8,24},{12,28},{16,0},{20,4},{24,8},{28,12},{1,17},{... | collective-permute-start | bytes 49160 | tf_op jit(solution)/shard_map/ppermute | solution.py:379
  24.4 2.3 %collective-permute-start.12 = (bf16[32,256]{1,0:T(8,128)(2,1)S(1)}, bf16[32,256]{1,0:T(8,128)(2,1)S(1)}, u32[]{:S(2)}, u32[]{:S(2)}) collective-permute-start(bf16[32,256]{1,0:T(8,128)(2,1)S(1)} %get-tuple-element.38), channel_id=1, source_target_pairs={{0,20},{4,16},{8,28},{12,24},{16,4},{20,0},{24,12},{28,8},{1,21},{... | collective-permute-start | bytes 49160 | tf_op jit(solution)/shard_map/ppermute | solution.py:379
  26.6 0.0 collective-permute-done.8.rest_1_
  26.6 2.1 %collective-permute-start.13 = (bf16[32,256]{1,0:T(8,128)(2,1)S(1)}, bf16[32,256]{1,0:T(8,128)(2,1)S(1)}, u32[]{:S(2)}, u32[]{:S(2)}) collective-permute-start(bf16[32,256]{1,0:T(8,128)(2,1)S(1)} %get-tuple-element.39), channel_id=1, source_target_pairs={{0,24},{4,28},{8,16},{12,20},{16,8},{20,12},{24,0},{28,4},{1,25},{... | collective-permute-start | bytes 49160 | tf_op jit(solution)/shard_map/ppermute | solution.py:379
  28.7 0.0 collective-permute-done.9.rest_2_
  28.7 2.7 %collective-permute-start.14 = (bf16[32,256]{1,0:T(8,128)(2,1)S(1)}, bf16[32,256]{1,0:T(8,128)(2,1)S(1)}, u32[]{:S(2)}, u32[]{:S(2)}) collective-permute-start(bf16[32,256]{1,0:T(8,128)(2,1)S(1)} %get-tuple-element.40), channel_id=1, source_target_pairs={{0,28},{4,24},{8,20},{12,16},{16,12},{20,8},{24,4},{28,0},{1,29},{... | collective-permute-start | bytes 49160 | tf_op jit(solution)/shard_map/ppermute | solution.py:379
  31.4 0.0 collective-permute-done.10.rest_3_
  31.4 0.0 collective-permute-done.11.rest_4_
  31.4 0.0 collective-permute-done.12.rest_5_
  31.4 0.8 %collective-permute-done.13.rest_6_ = bf16[32,256]{1,0:T(8,128)(2,1)S(1)} collective-permute-done((bf16[32,256]{1,0:T(8,128)(2,1)S(1)}, bf16[32,256]{1,0:T(8,128)(2,1)S(1)}, u32[]{:S(2)}, u32[]{:S(2)}) %collective-permute-start.13) | collective-permute-done | bytes 16416 | tf_op jit(solution)/shard_map/ppermute | solution.py:379
  32.2 3.0 %collective-permute-done.14.rest_7_ = bf16[32,256]{1,0:T(8,128)(2,1)S(1)} collective-permute-done((bf16[32,256]{1,0:T(8,128)(2,1)S(1)}, bf16[32,256]{1,0:T(8,128)(2,1)S(1)}, u32[]{:S(2)}, u32[]{:S(2)}) %collective-permute-start.14) | collective-permute-done | bytes 16416 | tf_op jit(solution)/shard_map/ppermute | solution.py:379
  35.2 0.7 %layout.1 = bf16[32,2048]{1,0:T(8,128)(2,1)} custom-call(s32[1]{0:T(128)} %bitcast.here, bf16[32,256]{1,0:T(8,128)(2,1)S(1)} %get-tuple-element.33.rest_0_, bf16[32,256]{1,0:T(8,128)(2,1)S(1)} %collective-permute-done.8.rest_1_, bf16[32,256]{1,0:T(8,128)(2,1)S(1)} %collective-permute-done.9.rest_2_, bf16[32,256]{1,0:T(8,128)(2,1)S(1)} %collective-permute-done.10.rest_3_, ...), custom_call_target="tpu_custom_call" | custom-call | tf_op jit(solution)/shard_map/layout/pallas_call | solution.py:380
Async XLA Ops:
  0.0 8.4 %collective-permute-start.1 = (bf16[32,2048]{1,0:T(8,128)(2,1)}, bf16[32,2048]{1,0:T(8,128)(2,1)S(1)}, u32[]{:S(2)}, u32[]{:S(2)}) collective-permute-start(bf16[32,2048]{1,0:T(8,128)(2,1)} %state.1), channel_id=1, source_target_pairs={{0,4},{4,0},{8,12},{12,8},{16,20},{20,16},{24,28},{28,24},{1,5},{5... | collective-permute-start | bytes 393224 | tf_op jit(solution)/shard_map/ppermute | solution.py:291
  2.9 3.8 %collective-permute-start.2 = (s32[8,16]{1,0:T(8,128)}, s32[8,16]{1,0:T(8,128)S(1)}, u32[]{:S(2)}, u32[]{:S(2)}) collective-permute-start(s32[8,16]{1,0:T(8,128)} %bitcast.4), channel_id=1, source_target_pairs={{0,3},{1,2},{2,1},{3,0},{4,7},{5,6},{6,5},{7,4},{8,11},{9,10},{10,... | collective-permute-start | bytes 1544 | tf_op jit(solution)/shard_map/ppermute | solution.py:289
  3.6 4.7 %collective-permute-start = (s32[8,16]{1,0:T(8,128)}, s32[8,16]{1,0:T(8,128)S(1)}, u32[]{:S(2)}, u32[]{:S(2)}) collective-permute-start(s32[8,16]{1,0:T(8,128)} %bitcast.5), channel_id=1, source_target_pairs={{0,1},{1,0},{2,3},{3,2},{4,5},{5,4},{6,7},{7,6},{8,9},{9,8},{10,11... | collective-permute-start | bytes 1544 | tf_op jit(solution)/shard_map/ppermute | solution.py:290
  4.6 3.8 %copy-start = (bf16[32,2048]{1,0:T(8,128)(2,1)S(1)}, bf16[32,2048]{1,0:T(8,128)(2,1)}, u32[]{:S(2)}) copy-start(bf16[32,2048]{1,0:T(8,128)(2,1)} %state.1) | copy-start | bytes 393220
  6.7 9.1 %copy-start.1 = (s32[16,8]{0,1:T(8,128)S(1)}, s32[16,8]{0,1:T(8,128)}, u32[]{:S(2)}) copy-start(s32[16,8]{0,1:T(8,128)} %param.11) | copy-start | bytes 1540
  7.9 9.1 %collective-permute-start.3 = (bf16[2,272,128]{2,1,0:T(8,128)(2,1)S(1)}, bf16[2,272,128]{2,1,0:T(8,128)(2,1)S(1)}, u32[]{:S(2)}, u32[]{:S(2)}) collective-permute-start(bf16[2,272,128]{2,1,0:T(8,128)(2,1)S(1)} %far_share.1.sent), channel_id=1, source_target_pairs={{0,3},{1,2},{2,1},{3,0},{4,7},{5,6},{6,5},{7,4},{8,11},{9,10},{10,... | collective-permute-start | bytes 417800 | tf_op jit(solution)/shard_map/ppermute | solution.py:329
  9.6 7.4 %collective-permute-start.4 = (bf16[2,272,128]{2,1,0:T(8,128)(2,1)S(1)}, bf16[2,272,128]{2,1,0:T(8,128)(2,1)S(1)}, u32[]{:S(2)}, u32[]{:S(2)}) collective-permute-start(bf16[2,272,128]{2,1,0:T(8,128)(2,1)S(1)} %get-tuple-element.26.sent), channel_id=1, source_target_pairs={{0,1},{1,0},{2,3},{3,2},{4,5},{5,4},{6,7},{7,6},{8,9},{9,8},{10,11... | collective-permute-start | bytes 417800 | tf_op jit(solution)/shard_map/ppermute | solution.py:340
  10.4 9.1 %collective-permute-start.5 = (bf16[2,32,256]{2,1,0:T(8,128)(2,1)S(1)}, bf16[2,32,256]{2,1,0:T(8,128)(2,1)S(1)}, u32[]{:S(2)}, u32[]{:S(2)}) collective-permute-start(bf16[2,32,256]{2,1,0:T(8,128)(2,1)S(1)} %get-tuple-element.30), channel_id=1, source_target_pairs={{0,8},{4,12},{8,16},{12,20},{16,24},{20,28},{24,0},{28,4},{1,9},{5... | collective-permute-start | bytes 98312 | tf_op jit(solution)/shard_map/ppermute | solution.py:352
  12.0 7.5 %collective-permute-start.6 = (bf16[2,32,256]{2,1,0:T(8,128)(2,1)S(1)}, bf16[2,32,256]{2,1,0:T(8,128)(2,1)S(1)}, u32[]{:S(2)}, u32[]{:S(2)}) collective-permute-start(bf16[2,32,256]{2,1,0:T(8,128)(2,1)S(1)} %get-tuple-element.31), channel_id=1, source_target_pairs={{0,16},{4,20},{8,24},{12,28},{16,0},{20,4},{24,8},{28,12},{1,17},{... | collective-permute-start | bytes 98312 | tf_op jit(solution)/shard_map/ppermute | solution.py:352
  14.5 4.9 %collective-permute-start.7 = (bf16[2,32,256]{2,1,0:T(8,128)(2,1)S(1)}, bf16[2,32,256]{2,1,0:T(8,128)(2,1)S(1)}, u32[]{:S(2)}, u32[]{:S(2)}) collective-permute-start(bf16[2,32,256]{2,1,0:T(8,128)(2,1)S(1)} %get-tuple-element.32), channel_id=1, source_target_pairs={{0,24},{4,28},{8,0},{12,4},{16,8},{20,12},{24,16},{28,20},{1,25},{... | collective-permute-start | bytes 98312 | tf_op jit(solution)/shard_map/ppermute | solution.py:352
  20.2 6.5 %collective-permute-start.8 = (bf16[32,256]{1,0:T(8,128)(2,1)S(1)}, bf16[32,256]{1,0:T(8,128)(2,1)S(1)}, u32[]{:S(2)}, u32[]{:S(2)}) collective-permute-start(bf16[32,256]{1,0:T(8,128)(2,1)S(1)} %get-tuple-element.34), channel_id=1, source_target_pairs={{0,4},{4,0},{8,12},{12,8},{16,20},{20,16},{24,28},{28,24},{1,5},{5... | collective-permute-start | bytes 49160 | tf_op jit(solution)/shard_map/ppermute | solution.py:379
  20.8 8.0 %collective-permute-start.9 = (bf16[32,256]{1,0:T(8,128)(2,1)S(1)}, bf16[32,256]{1,0:T(8,128)(2,1)S(1)}, u32[]{:S(2)}, u32[]{:S(2)}) collective-permute-start(bf16[32,256]{1,0:T(8,128)(2,1)S(1)} %get-tuple-element.35), channel_id=1, source_target_pairs={{0,8},{4,12},{8,0},{12,4},{16,24},{20,28},{24,16},{28,20},{1,9},{5... | collective-permute-start | bytes 49160 | tf_op jit(solution)/shard_map/ppermute | solution.py:379
  21.5 9.9 %collective-permute-start.10 = (bf16[32,256]{1,0:T(8,128)(2,1)S(1)}, bf16[32,256]{1,0:T(8,128)(2,1)S(1)}, u32[]{:S(2)}, u32[]{:S(2)}) collective-permute-start(bf16[32,256]{1,0:T(8,128)(2,1)S(1)} %get-tuple-element.36), channel_id=1, source_target_pairs={{0,12},{4,8},{8,4},{12,0},{16,28},{20,24},{24,20},{28,16},{1,13},{... | collective-permute-start | bytes 49160 | tf_op jit(solution)/shard_map/ppermute | solution.py:379
  23.7 7.7 %collective-permute-start.11 = (bf16[32,256]{1,0:T(8,128)(2,1)S(1)}, bf16[32,256]{1,0:T(8,128)(2,1)S(1)}, u32[]{:S(2)}, u32[]{:S(2)}) collective-permute-start(bf16[32,256]{1,0:T(8,128)(2,1)S(1)} %get-tuple-element.37), channel_id=1, source_target_pairs={{0,16},{4,20},{8,24},{12,28},{16,0},{20,4},{24,8},{28,12},{1,17},{... | collective-permute-start | bytes 49160 | tf_op jit(solution)/shard_map/ppermute | solution.py:379
  24.4 7.0 %collective-permute-start.12 = (bf16[32,256]{1,0:T(8,128)(2,1)S(1)}, bf16[32,256]{1,0:T(8,128)(2,1)S(1)}, u32[]{:S(2)}, u32[]{:S(2)}) collective-permute-start(bf16[32,256]{1,0:T(8,128)(2,1)S(1)} %get-tuple-element.38), channel_id=1, source_target_pairs={{0,20},{4,16},{8,28},{12,24},{16,4},{20,0},{24,12},{28,8},{1,21},{... | collective-permute-start | bytes 49160 | tf_op jit(solution)/shard_map/ppermute | solution.py:379
  26.6 5.5 %collective-permute-start.13 = (bf16[32,256]{1,0:T(8,128)(2,1)S(1)}, bf16[32,256]{1,0:T(8,128)(2,1)S(1)}, u32[]{:S(2)}, u32[]{:S(2)}) collective-permute-start(bf16[32,256]{1,0:T(8,128)(2,1)S(1)} %get-tuple-element.39), channel_id=1, source_target_pairs={{0,24},{4,28},{8,16},{12,20},{16,8},{20,12},{24,0},{28,4},{1,25},{... | collective-permute-start | bytes 49160 | tf_op jit(solution)/shard_map/ppermute | solution.py:379
  28.7 6.4 %collective-permute-start.14 = (bf16[32,256]{1,0:T(8,128)(2,1)S(1)}, bf16[32,256]{1,0:T(8,128)(2,1)S(1)}, u32[]{:S(2)}, u32[]{:S(2)}) collective-permute-start(bf16[32,256]{1,0:T(8,128)(2,1)S(1)} %get-tuple-element.40), channel_id=1, source_target_pairs={{0,28},{4,24},{8,20},{12,16},{16,12},{20,8},{24,4},{28,0},{1,29},{... | collective-permute-start | bytes 49160 | tf_op jit(solution)/shard_map/ppermute | solution.py:379

commit v4 on v2

--- a/solution.py
+++ b/solution.py
@@ -90,11 +90,26 @@
         innov[block : block + 1, :] = gap
 
 
-def own_kernel(patches, here, pattern, pert, weights, innov, sent, own):
+def own_kernel(
+    patches, here, pattern, pert, weights, innov, state, paired, sent, own, slabs, sems
+):
     mine = own.shape[0]
+    length, _, _, span = slabs.shape
+    place = here[0] % PAIR
+    moves = []
+    for layer in range(length):
+        start = (layer * PAIR + place) * span
+        cols = pl.ds(pl.multiple_of(start, span), span)
+        moves.append((state.at[:, cols], slabs.at[layer, place]))
+        moves.append((paired.at[:, cols], slabs.at[layer, 1 - place]))
+    moves = [pltpu.make_async_copy(*move, sems.at[i]) for i, move in enumerate(moves)]
+    for move in moves:
+        move.start()
     for patch in range(mine):
         row = here[0] * mine + patch
         own[patch] = share(pattern, row, 1, patches, pert, weights, innov)
+    for move in moves:
+        move.wait()
 
 
 def pack(part, out, patch):
@@ -118,30 +133,12 @@
     out[patch, members:, :] = tail.astype(BF16)
 
 
-def far_kernel(patches, side, here, pattern, pert, weights, innov, out):
+def neighbour_kernel(patches, here, side, pattern, pert, weights, innov, *rest):
+    out = rest[-1]
     mine = out.shape[0]
     for patch in range(mine):
         row = here[0] * mine + patch
-        pack(share(pattern, row, here[side], patches, pert, weights, innov), out, patch)
-
-
-def near_kernel(patches, side, here, pattern, pert, weights, innov, state, paired, sent, out, *rest):
-    slabs, sems = rest[:-1], rest[-1]
-    span = slabs[0].shape[2]
-    length = len(slabs)
-    layer, place = here[0] // PAIR, here[0] % PAIR
-    moves = []
-    for shift, slab in enumerate(slabs):
-        target = lax.rem(layer + shift, length) * PAIR + place
-        cols = pl.ds(pl.multiple_of(target * span, span), span)
-        moves.append((state.at[:, cols], slab.at[place]))
-        moves.append((paired.at[:, cols], slab.at[1 - place]))
-    moves = [pltpu.make_async_copy(*move, sems.at[i]) for i, move in enumerate(moves)]
-    for move in moves:
-        move.start()
-    far_kernel(patches, side, here, pattern, pert, weights, innov, out)
-    for move in moves:
-        move.wait()
+        pack(share(pattern, row, side[0], patches, pert, weights, innov), out, patch)
 
 
 def total(value):
@@ -220,20 +217,12 @@
         rows_out[p] = jnp.where(index == 0, gain, jnp.where(index == 1, lead[p], spread))
 
 
-def apply_kernel(here, root, rows, *rest):
-    slabs, (out, columns) = rest[:-2], rest[-2:]
+def apply_kernel(root, rows, state, out):
     mine, members, _ = root.shape
     points = out.shape[1] // mine
-    length = len(slabs)
-    _, local, _ = slabs[0].shape
-    for shift, slab in enumerate(slabs):
-        source = lax.rem(here[0] // PAIR - shift + length, length)
-        for i in range(PAIR):
-            place = pl.ds(pl.multiple_of((source * PAIR + i) * local, local), local)
-            columns[place, :] = slab[i]
     for p in range(mine):
         cols = slice(p * points, (p + 1) * points)
-        member = columns[:, cols].astype(F32)
+        member = state[:, cols].astype(F32)
         mean = jnp.sum(member, axis=0, keepdims=True) / members
         deviation = member - mean
         spread = rows[p, 1:2, :points] * deviation + jnp.dot(
@@ -253,7 +242,9 @@
     near = [(i, i + 1 - 2 * (i % 2)) for i in range(ring)]
     far = [(i, (i - 1 + 2 * (i % 2)) % ring) for i in range(ring)]
     odd = lax.axis_index("lon") % 2
-    here = jnp.stack([lax.axis_index("mem"), 2 * odd, 2 - 2 * odd]).astype(jnp.int32)
+    here, near_side, far_side = (
+        value.astype(jnp.int32).reshape(1) for value in (lax.axis_index("mem"), 2 * odd, 2 - 2 * odd)
+    )
     shape = jax.ShapeDtypeStruct
     padded = members + PAD
 
@@ -264,7 +255,6 @@
     pattern = loc_pattern.T
     far_pattern = lax.ppermute(pattern, "lon", far)
     near_pattern = lax.ppermute(pattern, "lon", near)
-    paired = lax.ppermute(state, "mem", swap)
     limit = pltpu.CompilerParams(vmem_limit_bytes=16 * 1024 * 1024)
     gram = 2 * padded * members * uses * width
     pert, weights, innov = pl.pallas_call(
@@ -291,41 +281,42 @@
         name="perturb",
     )(*(stay(value) for value in (obs_count, hx, obs_value, obs_rinv)))
     packed = shape((mine, padded, members // 2), BF16)
-    slab = shape((PAIR, local, span), BF16)
     cost = pl.CostEstimate(flops=mine * gram, bytes_accessed=hx.size, transcendentals=0)
-    to_far = pl.pallas_call(
-        functools.partial(far_kernel, patches, 2),
-        out_shape=packed,
-        in_specs=[SMEM] * 2 + [VMEM] * 3,
-        out_specs=VMEM,
-        compiler_params=limit,
-        cost_estimate=cost,
-        name="far_share",
-    )(here, far_pattern, pert, weights, innov)
+
+    def shares(side, theirs, *earlier):
+        return pl.pallas_call(
+            functools.partial(neighbour_kernel, patches),
+            out_shape=packed,
+            in_specs=[SMEM] * 3 + [VMEM] * 3 + [pl.BlockSpec(memory_space=pl.ANY)] * len(earlier),
+            out_specs=VMEM,
+            compiler_params=limit,
+            cost_estimate=cost,
+            name="neighbour_share",
+        )(here, side, theirs, pert, weights, innov, *earlier)
+
+    to_far = shares(far_side, far_pattern)
     from_far = lax.ppermute(to_far, "lon", far)
-    to_near, *slabs = pl.pallas_call(
-        functools.partial(near_kernel, patches, 1),
-        out_shape=(packed,) + (slab,) * length,
+    later, _ = lax.optimization_barrier((state, to_far))
+    paired = lax.ppermute(later, "mem", swap)
+    to_near = shares(near_side, near_pattern, to_far)
+    from_near = lax.ppermute(to_near, "lon", near)
+    own, slabs = pl.pallas_call(
+        functools.partial(own_kernel, patches),
+        out_shape=(
+            shape((mine, padded, members), F32),
+            shape((length, PAIR, local, span), BF16),
+        ),
         in_specs=[SMEM] * 2 + [VMEM] * 3 + [HBM] * 2 + [pl.BlockSpec(memory_space=pl.ANY)],
-        out_specs=(VMEM,) * (1 + length),
+        out_specs=(VMEM,) * 2,
         scratch_shapes=[pltpu.SemaphoreType.DMA((PAIR * length,))],
         compiler_params=limit,
         cost_estimate=cost,
-        name="near_share",
-    )(here, near_pattern, pert, weights, innov, state, paired, to_far)
-    from_near = lax.ppermute(to_near, "lon", near)
-    own = pl.pallas_call(
-        functools.partial(own_kernel, patches),
-        out_shape=shape((mine, padded, members), F32),
-        in_specs=[SMEM] * 2 + [VMEM] * 3 + [pl.BlockSpec(memory_space=pl.ANY)],
-        out_specs=VMEM,
-        compiler_params=limit,
-        cost_estimate=cost,
         name="own_share",
-    )(here, pattern, pert, weights, innov, to_near)
-    for shift in range(1, length):
-        turn = [(i, (i + shift * PAIR) % mem_total) for i in range(mem_total)]
-        slabs[shift] = lax.ppermute(slabs[shift], "mem", turn)
+    )(here, pattern, pert, weights, innov, state, paired, to_near)
+    layers = [[i * PAIR + j for i in range(length)] for j in range(PAIR)]
+    columns = lax.all_to_all(
+        slabs, "mem", split_axis=0, concat_axis=0, axis_index_groups=layers
+    ).reshape(members, span)
     root, rows = pl.pallas_call(
         root_kernel,
         out_shape=(shape((mine, members, members), BF16), shape((mine, PAD, members), F32)),
@@ -340,15 +331,14 @@
     updated = pl.pallas_call(
         apply_kernel,
         out_shape=shape((members, span), BF16),
-        in_specs=[SMEM] + [VMEM] * (2 + length),
+        in_specs=[VMEM] * 3,
         out_specs=VMEM,
-        scratch_shapes=[pltpu.VMEM((members, span), BF16)],
         compiler_params=limit,
         cost_estimate=pl.CostEstimate(
             flops=2 * members**2 * span, bytes_accessed=2**19, transcendentals=0
         ),
         name="apply",
-    )(here, root, rows, *slabs)
+    )(root, rows, columns)
     pieces = lax.all_to_all(
         updated.reshape(mem_total, local, span), "mem", split_axis=0, concat_axis=0
     )

time: 32.7 us -> 37.1 us (1.13)
  waiting for transfers between devices: 0.66 us -> 4.96 us
  starting transfers between devices: 10.3 us -> 11 us
  blocking collectives: 11.4 us -> 10.8 us
    ppermute x4 -> x1, starting transfers between devices: 7.06 us -> 1.67 us  [body(): paired = lax.ppermute(later, 'mem', swap)]
    all_to_all x0 -> x1, starting transfers between devices: none -> 4.87 us  [body(): lax.all_to_all(slabs, 'mem', split_axis=0, concat_axis=0, axis_index_grou...]
    all_to_all x0 -> x1, waiting for transfers between devices: none -> 3.62 us  [body(): lax.all_to_all(slabs, 'mem', split_axis=0, concat_axis=0, axis_index_grou...]
    ppermute x1, starting transfers between devices: 0.07 us -> 1.38 us  [body(): from_far = lax.ppermute(to_far, 'lon', far)]
    ppermute x1, waiting for transfers between devices: 0.01 us -> 0.89 us  [body(): near_pattern = lax.ppermute(pattern, 'lon', near)]
    all_to_all x1, blocking collectives: 11.4 us -> 10.8 us  [body(): lax.all_to_all(updated.reshape(mem_total, local, span), 'mem', split_axis...]
    pallas_call x3, Pallas kernels: 3.5 us -> 4.14 us  [the longest x2 2.23 us: shares(): pl.pallas_call(functools.partial(neighbour_kernel, patches), out_shape=pa...]
    pallas_call x1, Pallas kernels: 1.21 us -> 0.64 us  [body(): pl.pallas_call(apply_kernel, out_shape=shape((members, span), BF16), in_s...]
  transfers between devices with their start and end apart: 8 -> 6, of which waited for: 1 -> 3; matrix products, arithmetic and copies ran while one was open for 0% -> 0% of each run, Pallas kernels for 25% -> 21%
where the time goes in v4:
time: 37.1 us; the launch traced here: 36.8 us
  starting transfers between devices  11 us (30%)
  blocking collectives  10.8 us (29%)
  Pallas kernels  9.37 us (25%)
  waiting for transfers between devices  4.96 us (13%)
  local copies, waits for them, and re-layouts  0.67 us (2%)
    all_to_all x1, blocking collectives, body(): lax.all_to_all(updated.reshape(mem_total, local, span), 'mem', split_axis...  10.8 us
    all_to_all x1, starting transfers between devices, body(): lax.all_to_all(slabs, 'mem', split_axis=0, concat_axis=0, axis_index_grou...  4.87 us
    all_to_all x1, waiting for transfers between devices, body(): lax.all_to_all(slabs, 'mem', split_axis=0, concat_axis=0, axis_index_grou...  3.62 us
    pallas_call x1, Pallas kernels, body(): pl.pallas_call(root_kernel, out_shape=(shape((mine, members, members), BF...  2.45 us
    ppermute x1, starting transfers between devices, body(): far_pattern = lax.ppermute(pattern, 'lon', far)  2.41 us
    pallas_call x2, Pallas kernels, shares(): pl.pallas_call(functools.partial(neighbour_kernel, patches), out_shape=pa...  2.23 us
    pallas_call x1, Pallas kernels, body(): pl.pallas_call(perturb_kernel, out_shape=(shape((blocks, members, width),...  2.14 us
    pallas_call x1, Pallas kernels, body(): pl.pallas_call(functools.partial(own_kernel, patches), out_shape=(shape((...  1.91 us
  transfers between devices with their start and end apart: 6, of which 3 were waited for; matrix products, arithmetic and copies ran while one was open for 0% of the time, Pallas kernels for 21%

profile of v4, /device:TPU:0, one launch (start us, length us, event | category | flops | bytes accessed | tf_op | source)
XLA Modules:
  0.0 36.8 jit_solution(16956962391447389312)
XLA Ops:
  0.0 2.4 %collective-permute-start = (s32[8,16]{1,0:T(8,128)}, s32[8,16]{1,0:T(8,128)S(1)}, u32[]{:S(2)}, u32[]{:S(2)}) collective-permute-start(s32[8,16]{1,0:T(8,128)} %bitcast.11), channel_id=1, source_target_pairs={{0,3},{1,2},{2,1},{3,0},{4,7},{5,6},{6,5},{7,4},{8,11},{9,10},{10,... | collective-permute-start | bytes 1544 | tf_op jit(solution)/shard_map/ppermute | solution.py:256
  2.4 0.0 copy-start
  2.4 0.0 copy-start.1
  2.4 2.1 %perturb.1 = (bf16[32,256,128]{2,1,0:T(8,128)(2,1)S(1)}, f32[32,128]{1,0:T(8,128)S(1)}, f32[32,128]{1,0:T(8,128)S(1)}) custom-call(s32[32]{0:T(128)} %count_all.1, bf16[32,256,128]{2,1,0:T(8,128)(2,1)} %hx.1, f32[32,128]{1,0:T(8,128)} %value_all.1, f32[32,128]{1,0:T(8,128)} %rinv_all.1), custom_call_target="tpu_custom_call" | custom-call | flops 4194304 | bytes 4194304 | tf_op jit(solution)/shard_map/perturb/pallas_call | solution.py:260
  4.6 0.0 collective-permute-done.pattern
  4.6 1.1 %neighbour_share.2.rest_0_ = bf16[2,272,128]{2,1,0:T(8,128)(2,1)S(1)} custom-call(s32[1]{0:T(128)} %bitcast.here, s32[1]{0:T(128)} %bitcast.2.side, s32[8,16]{1,0:T(8,128)S(1)} %collective-permute-done.pattern, bf16[32,256,128]{2,1,0:T(8,128)(2,1)S(1)} %get-tuple-element.13.pert, f32[32,128]{1,0:T(8,128)S(1)} %get-tuple-element.14.weights, ...), custom_call_target="tpu_custom_call" | custom-call | flops 285212672 | bytes 1048576 | tf_op jit(solution)/shard_map/neighbour_share/pallas_call | solution.py:287
  5.7 0.0 copy-done
  5.7 1.7 %collective-permute-start.1 = (bf16[32,2048]{1,0:T(8,128)(2,1)S(1)}, bf16[32,2048]{1,0:T(8,128)(2,1)S(1)}, u32[]{:S(2)}, u32[]{:S(2)}) collective-permute-start(bf16[32,2048]{1,0:T(8,128)(2,1)S(1)} %copy-done), channel_id=1, source_target_pairs={{0,4},{4,0},{8,12},{12,8},{16,20},{20,16},{24,28},{28,24},{1,5},{5... | collective-permute-start | bytes 393224 | tf_op jit(solution)/shard_map/ppermute | solution.py:300
  7.4 0.0 copy-done.1
  7.4 0.3 collective-permute-start.2
  7.7 0.9 %collective-permute-done.2.pattern = s32[8,16]{1,0:T(8,128)S(1)} collective-permute-done((s32[8,16]{1,0:T(8,128)S(1)}, s32[8,16]{1,0:T(8,128)S(1)}, u32[]{:S(2)}, u32[]{:S(2)}) %collective-permute-start.2) | collective-permute-done | bytes 544 | tf_op jit(solution)/shard_map/ppermute | solution.py:257
  8.5 1.1 %neighbour_share.3.sent = bf16[2,272,128]{2,1,0:T(8,128)(2,1)S(1)} custom-call(s32[1]{0:T(128)} %bitcast.here, s32[1]{0:T(128)} %bitcast.3.side, s32[8,16]{1,0:T(8,128)S(1)} %collective-permute-done.2.pattern, bf16[32,256,128]{2,1,0:T(8,128)(2,1)S(1)} %get-tuple-element.13.pert, f32[32,128]{1,0:T(8,128)S(1)} %get-tuple-element.14.weights, ...), custom_call_target="tpu_custom_call" | custom-call | flops 285212672 | bytes 1048576 | tf_op jit(solution)/shard_map/neighbour_share/pallas_call | solution.py:287
  9.7 0.3 collective-permute-start.4
  10.0 1.4 %collective-permute-start.3 = (bf16[2,272,128]{2,1,0:T(8,128)(2,1)S(1)}, bf16[2,272,128]{2,1,0:T(8,128)(2,1)S(1)}, u32[]{:S(2)}, u32[]{:S(2)}) collective-permute-start(bf16[2,272,128]{2,1,0:T(8,128)(2,1)S(1)} %neighbour_share.2.rest_0_), channel_id=1, source_target_pairs={{0,3},{1,2},{2,1},{3,0},{4,7},{5,6},{6,5},{7,4},{8,11},{9,10},{10,... | collective-permute-start | bytes 417800 | tf_op jit(solution)/shard_map/ppermute | solution.py:298
  11.4 0.5 %collective-permute-done.1.paired = bf16[32,2048]{1,0:T(8,128)(2,1)S(1)} collective-permute-done((bf16[32,2048]{1,0:T(8,128)(2,1)S(1)}, bf16[32,2048]{1,0:T(8,128)(2,1)S(1)}, u32[]{:S(2)}, u32[]{:S(2)}) %collective-permute-start.1) | collective-permute-done | bytes 131104 | tf_op jit(solution)/shard_map/ppermute | solution.py:300
  11.8 1.9 %own_share.1 = (f32[2,272,256]{2,1,0:T(8,128)S(1)}, bf16[4,2,32,256]{3,2,1,0:T(8,128)(2,1)}) custom-call(s32[1]{0:T(128)} %bitcast.here, s32[8,16]{1,0:T(8,128)S(1)} %bitcast.13, bf16[32,256,128]{2,1,0:T(8,128)(2,1)S(1)} %get-tuple-element.13.pert, f32[32,128]{1,0:T(8,128)S(1)} %get-tuple-element.14.weights, f32[32,128]{1,0:T(8,128)S(1)} %get-tuple-element.15.innov, ...), custom_call_target="tpu_custom_call" | custom-call | flops 285212672 | bytes 1048576 | tf_op jit(solution)/shard_map/own_share/pallas_call | solution.py:303
  13.8 4.9 %all-to-all-start = ((bf16[4,2,32,256]{3,2,1,0:T(8,128)(2,1)}), bf16[4,2,32,256]{3,2,1,0:T(8,128)(2,1)S(1)}, u32[]{:S(2)}, u32[]{:S(2)}) async-start(bf16[4,2,32,256]{3,2,1,0:T(8,128)(2,1)} %get-tuple-element.20), calls=%async_computation | async-start | bytes 262144 | tf_op jit(solution)/shard_map/all_to_all | solution.py:317
  18.6 0.0 collective-permute-done.4.after
  18.6 0.0 collective-permute-done.3.before
  18.6 2.4 %root.1 = (bf16[2,256,256]{2,1,0:T(8,128)(2,1)S(1)}, f32[2,16,256]{2,1,0:T(8,128)S(1)}) custom-call(f32[2,272,256]{2,1,0:T(8,128)S(1)} %get-tuple-element.17.own, bf16[2,272,128]{2,1,0:T(8,128)(2,1)S(1)} %collective-permute-done.3.before, bf16[2,272,128]{2,1,0:T(8,128)(2,1)S(1)} %collective-permute-done.4.after), custom_call_target="tpu_custom_call" | custom-call | flops 1006632960 | bytes 1048576 | tf_op jit(solution)/shard_map/root/pallas_call | solution.py:320
  21.1 3.6 %all-to-all-done = bf16[4,2,32,256]{3,2,1,0:T(8,128)(2,1)S(1)} async-done(((bf16[4,2,32,256]{3,2,1,0:T(8,128)(2,1)}), bf16[4,2,32,256]{3,2,1,0:T(8,128)(2,1)S(1)}, u32[]{:S(2)}, u32[]{:S(2)}) %all-to-all-start) | async-done | bytes 131104 | tf_op jit(solution)/shard_map/all_to_all | solution.py:317
  24.7 0.6 %apply.1 = bf16[256,256]{1,0:T(8,128)(2,1)S(1)} custom-call(bf16[2,256,256]{2,1,0:T(8,128)(2,1)S(1)} %get-tuple-element.18.root, f32[2,16,256]{2,1,0:T(8,128)S(1)} %get-tuple-element.19.rows, bf16[256,256]{1,0:T(8,128)(2,1)S(1)} %bitcast.9), custom_call_target="tpu_custom_call" | custom-call | flops 33554432 | bytes 524288 | tf_op jit(solution)/shard_map/apply/pallas_call | solution.py:331
  25.4 10.8 %all_to_all.10 = bf16[8,32,256]{2,1,0:T(8,128)(2,1)S(1)} all-to-all(bf16[8,32,256]{2,1,0:T(8,128)(2,1)S(1)} %bitcast.10), channel_id=1, replica_groups=mesh['mem'=8,'lon'=4] {'mem'}, dimensions={0} | all-to-all | bytes 262144 | tf_op jit(solution)/shard_map/all_to_all | solution.py:342
  36.1 0.7 %copy.8 = bf16[8,4,8,256]{3,2,0,1:T(8,128)(2,1)} copy(bf16[8,4,8,256]{3,2,1,0:T(8,128)(2,1)S(1)} %bitcast.14) | data formatting | bytes 262144 | tf_op jit(solution)/shard_map/reshape | solution.py:345
Async XLA Ops:
  0.0 4.6 %collective-permute-start = (s32[8,16]{1,0:T(8,128)}, s32[8,16]{1,0:T(8,128)S(1)}, u32[]{:S(2)}, u32[]{:S(2)}) collective-permute-start(s32[8,16]{1,0:T(8,128)} %bitcast.11), channel_id=1, source_target_pairs={{0,3},{1,2},{2,1},{3,0},{4,7},{5,6},{6,5},{7,4},{8,11},{9,10},{10,... | collective-permute-start | bytes 1544 | tf_op jit(solution)/shard_map/ppermute | solution.py:256
  2.4 3.3 %copy-start = (bf16[32,2048]{1,0:T(8,128)(2,1)S(1)}, bf16[32,2048]{1,0:T(8,128)(2,1)}, u32[]{:S(2)}) copy-start(bf16[32,2048]{1,0:T(8,128)(2,1)} %state.1) | copy-start | bytes 393220
  2.4 5.0 %copy-start.1 = (s32[16,8]{0,1:T(8,128)S(1)}, s32[16,8]{0,1:T(8,128)}, u32[]{:S(2)}) copy-start(s32[16,8]{0,1:T(8,128)} %param.11) | copy-start | bytes 1540
  5.7 6.1 %collective-permute-start.1 = (bf16[32,2048]{1,0:T(8,128)(2,1)S(1)}, bf16[32,2048]{1,0:T(8,128)(2,1)S(1)}, u32[]{:S(2)}, u32[]{:S(2)}) collective-permute-start(bf16[32,2048]{1,0:T(8,128)(2,1)S(1)} %copy-done), channel_id=1, source_target_pairs={{0,4},{4,0},{8,12},{12,8},{16,20},{20,16},{24,28},{28,24},{1,5},{5... | collective-permute-start | bytes 393224 | tf_op jit(solution)/shard_map/ppermute | solution.py:300
  7.4 1.2 %collective-permute-start.2 = (s32[8,16]{1,0:T(8,128)S(1)}, s32[8,16]{1,0:T(8,128)S(1)}, u32[]{:S(2)}, u32[]{:S(2)}) collective-permute-start(s32[8,16]{1,0:T(8,128)S(1)} %bitcast.12), channel_id=1, source_target_pairs={{0,1},{1,0},{2,3},{3,2},{4,5},{5,4},{6,7},{7,6},{8,9},{9,8},{10,11... | collective-permute-start | bytes 1544 | tf_op jit(solution)/shard_map/ppermute | solution.py:257
  9.7 9.0 %collective-permute-start.4 = (bf16[2,272,128]{2,1,0:T(8,128)(2,1)S(1)}, bf16[2,272,128]{2,1,0:T(8,128)(2,1)S(1)}, u32[]{:S(2)}, u32[]{:S(2)}) collective-permute-start(bf16[2,272,128]{2,1,0:T(8,128)(2,1)S(1)} %neighbour_share.3.sent), channel_id=1, source_target_pairs={{0,1},{1,0},{2,3},{3,2},{4,5},{5,4},{6,7},{7,6},{8,9},{9,8},{10,11... | collective-permute-start | bytes 417800 | tf_op jit(solution)/shard_map/ppermute | solution.py:302
  10.0 8.6 %collective-permute-start.3 = (bf16[2,272,128]{2,1,0:T(8,128)(2,1)S(1)}, bf16[2,272,128]{2,1,0:T(8,128)(2,1)S(1)}, u32[]{:S(2)}, u32[]{:S(2)}) collective-permute-start(bf16[2,272,128]{2,1,0:T(8,128)(2,1)S(1)} %neighbour_share.2.rest_0_), channel_id=1, source_target_pairs={{0,3},{1,2},{2,1},{3,0},{4,7},{5,6},{6,5},{7,4},{8,11},{9,10},{10,... | collective-permute-start | bytes 417800 | tf_op jit(solution)/shard_map/ppermute | solution.py:298
  13.8 10.9 %all-to-all-start = ((bf16[4,2,32,256]{3,2,1,0:T(8,128)(2,1)}), bf16[4,2,32,256]{3,2,1,0:T(8,128)(2,1)S(1)}, u32[]{:S(2)}, u32[]{:S(2)}) async-start(bf16[4,2,32,256]{3,2,1,0:T(8,128)(2,1)} %get-tuple-element.20), calls=%async_computation | async-start | bytes 262144 | tf_op jit(solution)/shard_map/all_to_all | solution.py:317

commit v5 on v2

--- a/solution.py
+++ b/solution.py
@@ -118,28 +118,28 @@
     out[patch, members:, :] = tail.astype(BF16)
 
 
-def far_kernel(patches, side, here, pattern, pert, weights, innov, out):
+def far_kernel(patches, here, side, pattern, pert, weights, innov, out):
     mine = out.shape[0]
     for patch in range(mine):
         row = here[0] * mine + patch
-        pack(share(pattern, row, here[side], patches, pert, weights, innov), out, patch)
-
-
-def near_kernel(patches, side, here, pattern, pert, weights, innov, state, paired, sent, out, *rest):
+        pack(share(pattern, row, side[0], patches, pert, weights, innov), out, patch)
+
+
+def near_kernel(patches, here, side, pattern, pert, weights, innov, state, paired, sent, out, *rest):
     slabs, sems = rest[:-1], rest[-1]
     span = slabs[0].shape[2]
     length = len(slabs)
     layer, place = here[0] // PAIR, here[0] % PAIR
     moves = []
     for shift, slab in enumerate(slabs):
-        target = lax.rem(layer + shift, length) * PAIR + place
+        target = (layer ^ shift) * PAIR + place
         cols = pl.ds(pl.multiple_of(target * span, span), span)
         moves.append((state.at[:, cols], slab.at[place]))
         moves.append((paired.at[:, cols], slab.at[1 - place]))
     moves = [pltpu.make_async_copy(*move, sems.at[i]) for i, move in enumerate(moves)]
     for move in moves:
         move.start()
-    far_kernel(patches, side, here, pattern, pert, weights, innov, out)
+    far_kernel(patches, here, side, pattern, pert, weights, innov, out)
     for move in moves:
         move.wait()
 
@@ -227,7 +227,7 @@
     length = len(slabs)
     _, local, _ = slabs[0].shape
     for shift, slab in enumerate(slabs):
-        source = lax.rem(here[0] // PAIR - shift + length, length)
+        source = (here[0] // PAIR) ^ shift
         for i in range(PAIR):
             place = pl.ds(pl.multiple_of((source * PAIR + i) * local, local), local)
             columns[place, :] = slab[i]
@@ -253,13 +253,16 @@
     near = [(i, i + 1 - 2 * (i % 2)) for i in range(ring)]
     far = [(i, (i - 1 + 2 * (i % 2)) % ring) for i in range(ring)]
     odd = lax.axis_index("lon") % 2
-    here = jnp.stack([lax.axis_index("mem"), 2 * odd, 2 - 2 * odd]).astype(jnp.int32)
+    here, near_side, far_side = (
+        value.astype(jnp.int32).reshape(1) for value in (lax.axis_index("mem"), 2 * odd, 2 - 2 * odd)
+    )
     shape = jax.ShapeDtypeStruct
     padded = members + PAD
 
     span = points // mem_total
     length = mem_total // PAIR
-    swap = [(i, i + 1 - 2 * (i % PAIR)) for i in range(mem_total)]
+    swap = [(i, i ^ 1) for i in range(mem_total)]
+    assert mem_total & (mem_total - 1) == 0
 
     pattern = loc_pattern.T
     far_pattern = lax.ppermute(pattern, "lon", far)
@@ -294,25 +297,25 @@
     slab = shape((PAIR, local, span), BF16)
     cost = pl.CostEstimate(flops=mine * gram, bytes_accessed=hx.size, transcendentals=0)
     to_far = pl.pallas_call(
-        functools.partial(far_kernel, patches, 2),
+        functools.partial(far_kernel, patches),
         out_shape=packed,
-        in_specs=[SMEM] * 2 + [VMEM] * 3,
+        in_specs=[SMEM] * 3 + [VMEM] * 3,
         out_specs=VMEM,
         compiler_params=limit,
         cost_estimate=cost,
         name="far_share",
-    )(here, far_pattern, pert, weights, innov)
+    )(here, far_side, far_pattern, pert, weights, innov)
     from_far = lax.ppermute(to_far, "lon", far)
     to_near, *slabs = pl.pallas_call(
-        functools.partial(near_kernel, patches, 1),
+        functools.partial(near_kernel, patches),
         out_shape=(packed,) + (slab,) * length,
-        in_specs=[SMEM] * 2 + [VMEM] * 3 + [HBM] * 2 + [pl.BlockSpec(memory_space=pl.ANY)],
+        in_specs=[SMEM] * 3 + [VMEM] * 3 + [HBM] * 2 + [pl.BlockSpec(memory_space=pl.ANY)],
         out_specs=(VMEM,) * (1 + length),
         scratch_shapes=[pltpu.SemaphoreType.DMA((PAIR * length,))],
         compiler_params=limit,
         cost_estimate=cost,
         name="near_share",
-    )(here, near_pattern, pert, weights, innov, state, paired, to_far)
+    )(here, near_side, near_pattern, pert, weights, innov, state, paired, to_far)
     from_near = lax.ppermute(to_near, "lon", near)
     own = pl.pallas_call(
         functools.partial(own_kernel, patches),
@@ -324,8 +327,8 @@
         name="own_share",
     )(here, pattern, pert, weights, innov, to_near)
     for shift in range(1, length):
-        turn = [(i, (i + shift * PAIR) % mem_total) for i in range(mem_total)]
-        slabs[shift] = lax.ppermute(slabs[shift], "mem", turn)
+        trade = [(i, i ^ (shift * PAIR)) for i in range(mem_total)]
+        slabs[shift] = lax.ppermute(slabs[shift], "mem", trade)
     root, rows = pl.pallas_call(
         root_kernel,
         out_shape=(shape((mine, members, members), BF16), shape((mine, PAD, members), F32)),

time: 32.7 us -> 31.9 us (0.976)
  blocking collectives: 11.4 us -> 10.1 us
  waiting for transfers between devices: 0.66 us -> 1.91 us
  Pallas kernels: 9.32 us -> 8.76 us
    ppermute x3, waiting for transfers between devices: 0.01 us -> 1.9 us  [body(): slabs[shift] = lax.ppermute(slabs[shift], 'mem', trade)]
    ppermute x1, starting transfers between devices: 2.41 us -> 0.68 us  [body(): far_pattern = lax.ppermute(pattern, 'lon', far)]
    ppermute x1, starting transfers between devices: 1.49 us -> 2.94 us  [body(): paired = lax.ppermute(state, 'mem', swap)]
    all_to_all x1, blocking collectives: 11.4 us -> 10.1 us  [body(): lax.all_to_all(updated.reshape(mem_total, local, span), 'mem', split_axis...]
    ppermute x3, starting transfers between devices: 5.57 us -> 4.39 us  [body(): slabs[shift] = lax.ppermute(slabs[shift], 'mem', trade)]
    ppermute x1, starting transfers between devices: 0.07 us -> 0.73 us  [body(): from_near = lax.ppermute(to_near, 'lon', near)]
    ppermute x1, waiting for transfers between devices: 0.64 us -> 0.01 us  [body(): paired = lax.ppermute(state, 'mem', swap)]
    pallas_call x1, Pallas kernels: 1.21 us -> 0.66 us  [body(): pl.pallas_call(apply_kernel, out_shape=shape((members, span), BF16), in_s...]
  transfers between devices with their start and end apart: 8 -> 8, of which waited for: 1 -> 1; matrix products, arithmetic and copies ran while one was open for 0% -> 0% of each run, Pallas kernels for 25% -> 26%
where the time goes in v5:
time: 31.9 us; the launch traced here: 31.7 us
  starting transfers between devices  10.1 us (32%)
  blocking collectives  10.1 us (32%)
  Pallas kernels  8.76 us (27%)
  waiting for transfers between devices  1.91 us (6%)
  local copies, waits for them, and re-layouts  0.67 us (2%)
    all_to_all x1, blocking collectives, body(): lax.all_to_all(updated.reshape(mem_total, local, span), 'mem', split_axis...  10.1 us
    ppermute x3, starting transfers between devices, body(): slabs[shift] = lax.ppermute(slabs[shift], 'mem', trade)  4.39 us
    ppermute x1, starting transfers between devices, body(): paired = lax.ppermute(state, 'mem', swap)  2.94 us
    pallas_call x1, Pallas kernels, body(): pl.pallas_call(root_kernel, out_shape=(shape((mine, members, members), BF...  2.45 us
    pallas_call x1, Pallas kernels, body(): pl.pallas_call(perturb_kernel, out_shape=(shape((blocks, members, width),...  2.15 us
    ppermute x3, waiting for transfers between devices, body(): slabs[shift] = lax.ppermute(slabs[shift], 'mem', trade)  1.9 us
    pallas_call x1, Pallas kernels, body(): pl.pallas_call(functools.partial(near_kernel, patches), out_shape=(packed...  1.27 us
    pallas_call x1, Pallas kernels, body(): pl.pallas_call(functools.partial(far_kernel, patches), out_shape=packed,...  1.12 us
  transfers between devices with their start and end apart: 8, of which 1 were waited for; matrix products, arithmetic and copies ran while one was open for 0% of the time, Pallas kernels for 26%

profile of v5, /device:TPU:0, one launch (start us, length us, event | category | flops | bytes accessed | tf_op | source)
XLA Modules:
  0.0 31.7 jit_solution(17426346706034198847)
XLA Ops:
  0.0 2.9 %collective-permute-start.1 = (bf16[32,2048]{1,0:T(8,128)(2,1)}, bf16[32,2048]{1,0:T(8,128)(2,1)S(1)}, u32[]{:S(2)}, u32[]{:S(2)}) collective-permute-start(bf16[32,2048]{1,0:T(8,128)(2,1)} %state.1), channel_id=1, source_target_pairs={{0,4},{4,0},{8,12},{12,8},{16,20},{20,16},{24,28},{28,24},{1,5},{5... | collective-permute-start | bytes 393224 | tf_op jit(solution)/shard_map/ppermute | solution.py:270
  2.9 0.7 %collective-permute-start.2 = (s32[8,16]{1,0:T(8,128)}, s32[8,16]{1,0:T(8,128)S(1)}, u32[]{:S(2)}, u32[]{:S(2)}) collective-permute-start(s32[8,16]{1,0:T(8,128)} %bitcast.9), channel_id=1, source_target_pairs={{0,3},{1,2},{2,1},{3,0},{4,7},{5,6},{6,5},{7,4},{8,11},{9,10},{10,... | collective-permute-start | bytes 1544 | tf_op jit(solution)/shard_map/ppermute | solution.py:268
  3.6 1.0 %collective-permute-start = (s32[8,16]{1,0:T(8,128)}, s32[8,16]{1,0:T(8,128)S(1)}, u32[]{:S(2)}, u32[]{:S(2)}) collective-permute-start(s32[8,16]{1,0:T(8,128)} %bitcast.10), channel_id=1, source_target_pairs={{0,1},{1,0},{2,3},{3,2},{4,5},{5,4},{6,7},{7,6},{8,9},{9,8},{10,11... | collective-permute-start | bytes 1544 | tf_op jit(solution)/shard_map/ppermute | solution.py:269
  4.6 0.0 copy-start
  4.6 2.2 %perturb.1 = (bf16[32,256,128]{2,1,0:T(8,128)(2,1)S(1)}, f32[32,128]{1,0:T(8,128)S(1)}, f32[32,128]{1,0:T(8,128)S(1)}) custom-call(s32[32]{0:T(128)} %count_all.1, bf16[32,256,128]{2,1,0:T(8,128)(2,1)} %hx.1, f32[32,128]{1,0:T(8,128)} %value_all.1, f32[32,128]{1,0:T(8,128)} %rinv_all.1), custom_call_target="tpu_custom_call" | custom-call | flops 4194304 | bytes 4194304 | tf_op jit(solution)/shard_map/perturb/pallas_call | solution.py:273
  6.7 0.0 collective-permute-done.2.pattern
  6.7 0.0 copy-start.1
  6.8 1.1 %far_share.1.sent = bf16[2,272,128]{2,1,0:T(8,128)(2,1)S(1)} custom-call(s32[1]{0:T(128)} %bitcast.here, s32[1]{0:T(128)} %bitcast.3.side, s32[8,16]{1,0:T(8,128)S(1)} %collective-permute-done.2.pattern, bf16[32,256,128]{2,1,0:T(8,128)(2,1)S(1)} %get-tuple-element.15.pert, f32[32,128]{1,0:T(8,128)S(1)} %get-tuple-element.16.weights, ...), custom_call_target="tpu_custom_call" | custom-call | flops 285212672 | bytes 1048576 | tf_op jit(solution)/shard_map/far_share/pallas_call | solution.py:299
  7.9 0.5 %collective-permute-start.3 = (bf16[2,272,128]{2,1,0:T(8,128)(2,1)S(1)}, bf16[2,272,128]{2,1,0:T(8,128)(2,1)S(1)}, u32[]{:S(2)}, u32[]{:S(2)}) collective-permute-start(bf16[2,272,128]{2,1,0:T(8,128)(2,1)S(1)} %far_share.1.sent), channel_id=1, source_target_pairs={{0,3},{1,2},{2,1},{3,0},{4,7},{5,6},{6,5},{7,4},{8,11},{9,10},{10,... | collective-permute-start | bytes 417800 | tf_op jit(solution)/shard_map/ppermute | solution.py:308
  8.3 0.0 collective-permute-done.pattern
  8.3 0.0 collective-permute-done.1.paired
  8.4 0.0 copy-done
  8.4 1.3 %near_share.1 = (bf16[2,272,128]{2,1,0:T(8,128)(2,1)S(1)}, bf16[2,32,256]{2,1,0:T(8,128)(2,1)S(1)}, bf16[2,32,256]{2,1,0:T(8,128)(2,1)S(1)}, bf16[2,32,256]{2,1,0:T(8,128)(2,1)S(1)}, bf16[2,32,256]{2,1,0:T(8,128)(2,1)S(1)}) custom-call(s32[1]{0:T(128)} %bitcast.here, s32[1]{0:T(128)} %bitcast.2.side, s32[8,16]{1,0:T(8,128)S(1)} %collective-permute-done.pattern, ...), custom_call_target="tpu_custom_call" | custom-call | flops 285212672 | bytes 1048576 | tf_op jit(solution)/shard_map/near_share/pallas_call | solution.py:309
  9.6 0.7 %collective-permute-start.4 = (bf16[2,272,128]{2,1,0:T(8,128)(2,1)S(1)}, bf16[2,272,128]{2,1,0:T(8,128)(2,1)S(1)}, u32[]{:S(2)}, u32[]{:S(2)}) collective-permute-start(bf16[2,272,128]{2,1,0:T(8,128)(2,1)S(1)} %get-tuple-element.18.sent), channel_id=1, source_target_pairs={{0,1},{1,0},{2,3},{3,2},{4,5},{5,4},{6,7},{7,6},{8,9},{9,8},{10,11... | collective-permute-start | bytes 417800 | tf_op jit(solution)/shard_map/ppermute | solution.py:319
  10.4 1.6 %collective-permute-start.5 = (bf16[2,32,256]{2,1,0:T(8,128)(2,1)S(1)}, bf16[2,32,256]{2,1,0:T(8,128)(2,1)S(1)}, u32[]{:S(2)}, u32[]{:S(2)}) collective-permute-start(bf16[2,32,256]{2,1,0:T(8,128)(2,1)S(1)} %get-tuple-element.22), channel_id=1, source_target_pairs={{0,8},{4,12},{8,0},{12,4},{16,24},{20,28},{24,16},{28,20},{1,9},{5... | collective-permute-start | bytes 98312 | tf_op jit(solution)/shard_map/ppermute | solution.py:331
  11.9 2.6 %collective-permute-start.6 = (bf16[2,32,256]{2,1,0:T(8,128)(2,1)S(1)}, bf16[2,32,256]{2,1,0:T(8,128)(2,1)S(1)}, u32[]{:S(2)}, u32[]{:S(2)}) collective-permute-start(bf16[2,32,256]{2,1,0:T(8,128)(2,1)S(1)} %get-tuple-element.23), channel_id=1, source_target_pairs={{0,16},{4,20},{8,24},{12,28},{16,0},{20,4},{24,8},{28,12},{1,17},{... | collective-permute-start | bytes 98312 | tf_op jit(solution)/shard_map/ppermute | solution.py:331
  14.5 0.2 collective-permute-start.7
  14.8 0.0 copy-done.1
  14.8 1.1 %own_share.1.own = f32[2,272,256]{2,1,0:T(8,128)S(1)} custom-call(s32[1]{0:T(128)} %bitcast.here, s32[8,16]{1,0:T(8,128)S(1)} %bitcast.11, bf16[32,256,128]{2,1,0:T(8,128)(2,1)S(1)} %get-tuple-element.15.pert, f32[32,128]{1,0:T(8,128)S(1)} %get-tuple-element.16.weights, f32[32,128]{1,0:T(8,128)S(1)} %get-tuple-element.17.innov, ...), custom_call_target="tpu_custom_call" | custom-call | flops 285212672 | bytes 1048576 | tf_op jit(solution)/shard_map/own_share/pallas_call | solution.py:320
  15.9 0.0 collective-permute-done.3.before
  15.9 0.0 collective-permute-done.4.after
  15.9 2.5 %root.1 = (bf16[2,256,256]{2,1,0:T(8,128)(2,1)S(1)}, f32[2,16,256]{2,1,0:T(8,128)S(1)}) custom-call(f32[2,272,256]{2,1,0:T(8,128)S(1)} %own_share.1.own, bf16[2,272,128]{2,1,0:T(8,128)(2,1)S(1)} %collective-permute-done.3.before, bf16[2,272,128]{2,1,0:T(8,128)(2,1)S(1)} %collective-permute-done.4.after), custom_call_target="tpu_custom_call" | custom-call | flops 1006632960 | bytes 1048576 | tf_op jit(solution)/shard_map/root/pallas_call | solution.py:332
  18.3 0.0 collective-permute-done.5.rest_1_
  18.3 0.0 collective-permute-done.6.rest_2_
  18.4 1.9 %collective-permute-done.7.rest_3_ = bf16[2,32,256]{2,1,0:T(8,128)(2,1)S(1)} collective-permute-done((bf16[2,32,256]{2,1,0:T(8,128)(2,1)S(1)}, bf16[2,32,256]{2,1,0:T(8,128)(2,1)S(1)}, u32[]{:S(2)}, u32[]{:S(2)}) %collective-permute-start.7) | collective-permute-done | bytes 32800 | tf_op jit(solution)/shard_map/ppermute | solution.py:331
  20.2 0.7 %apply.1 = bf16[256,256]{1,0:T(8,128)(2,1)S(1)} custom-call(s32[1]{0:T(128)} %bitcast.here, bf16[2,256,256]{2,1,0:T(8,128)(2,1)S(1)} %get-tuple-element.19.root, f32[2,16,256]{2,1,0:T(8,128)S(1)} %get-tuple-element.20.rows, bf16[2,32,256]{2,1,0:T(8,128)(2,1)S(1)} %get-tuple-element.21.rest_0_, bf16[2,32,256]{2,1,0:T(8,128)(2,1)S(1)} %collective-permute-done.5.rest_1_, ...), custom_call_target="tpu_custom_call" | custom-call | flops 33554432 | bytes 524288 | tf_op jit(solution)/shard_map/apply/pallas_call | solution.py:343
  20.9 10.1 %all_to_all.5 = bf16[8,32,256]{2,1,0:T(8,128)(2,1)S(1)} all-to-all(bf16[8,32,256]{2,1,0:T(8,128)(2,1)S(1)} %bitcast.8), channel_id=1, replica_groups=mesh['mem'=8,'lon'=4] {'mem'}, dimensions={0} | all-to-all | bytes 262144 | tf_op jit(solution)/shard_map/all_to_all | solution.py:355
  31.1 0.7 %copy.8 = bf16[8,4,8,256]{3,2,0,1:T(8,128)(2,1)} copy(bf16[8,4,8,256]{3,2,1,0:T(8,128)(2,1)S(1)} %bitcast.12) | data formatting | bytes 262144 | tf_op jit(solution)/shard_map/reshape | solution.py:358
Async XLA Ops:
  0.0 8.4 %collective-permute-start.1 = (bf16[32,2048]{1,0:T(8,128)(2,1)}, bf16[32,2048]{1,0:T(8,128)(2,1)S(1)}, u32[]{:S(2)}, u32[]{:S(2)}) collective-permute-start(bf16[32,2048]{1,0:T(8,128)(2,1)} %state.1), channel_id=1, source_target_pairs={{0,4},{4,0},{8,12},{12,8},{16,20},{20,16},{24,28},{28,24},{1,5},{5... | collective-permute-start | bytes 393224 | tf_op jit(solution)/shard_map/ppermute | solution.py:270
  2.9 3.8 %collective-permute-start.2 = (s32[8,16]{1,0:T(8,128)}, s32[8,16]{1,0:T(8,128)S(1)}, u32[]{:S(2)}, u32[]{:S(2)}) collective-permute-start(s32[8,16]{1,0:T(8,128)} %bitcast.9), channel_id=1, source_target_pairs={{0,3},{1,2},{2,1},{3,0},{4,7},{5,6},{6,5},{7,4},{8,11},{9,10},{10,... | collective-permute-start | bytes 1544 | tf_op jit(solution)/shard_map/ppermute | solution.py:268
  3.6 4.7 %collective-permute-start = (s32[8,16]{1,0:T(8,128)}, s32[8,16]{1,0:T(8,128)S(1)}, u32[]{:S(2)}, u32[]{:S(2)}) collective-permute-start(s32[8,16]{1,0:T(8,128)} %bitcast.10), channel_id=1, source_target_pairs={{0,1},{1,0},{2,3},{3,2},{4,5},{5,4},{6,7},{7,6},{8,9},{9,8},{10,11... | collective-permute-start | bytes 1544 | tf_op jit(solution)/shard_map/ppermute | solution.py:269
  4.6 3.8 %copy-start = (bf16[32,2048]{1,0:T(8,128)(2,1)S(1)}, bf16[32,2048]{1,0:T(8,128)(2,1)}, u32[]{:S(2)}) copy-start(bf16[32,2048]{1,0:T(8,128)(2,1)} %state.1) | copy-start | bytes 393220
  6.7 8.0 %copy-start.1 = (s32[16,8]{0,1:T(8,128)S(1)}, s32[16,8]{0,1:T(8,128)}, u32[]{:S(2)}) copy-start(s32[16,8]{0,1:T(8,128)} %param.11) | copy-start | bytes 1540
  7.9 8.0 %collective-permute-start.3 = (bf16[2,272,128]{2,1,0:T(8,128)(2,1)S(1)}, bf16[2,272,128]{2,1,0:T(8,128)(2,1)S(1)}, u32[]{:S(2)}, u32[]{:S(2)}) collective-permute-start(bf16[2,272,128]{2,1,0:T(8,128)(2,1)S(1)} %far_share.1.sent), channel_id=1, source_target_pairs={{0,3},{1,2},{2,1},{3,0},{4,7},{5,6},{6,5},{7,4},{8,11},{9,10},{10,... | collective-permute-start | bytes 417800 | tf_op jit(solution)/shard_map/ppermute | solution.py:308
  9.6 6.2 %collective-permute-start.4 = (bf16[2,272,128]{2,1,0:T(8,128)(2,1)S(1)}, bf16[2,272,128]{2,1,0:T(8,128)(2,1)S(1)}, u32[]{:S(2)}, u32[]{:S(2)}) collective-permute-start(bf16[2,272,128]{2,1,0:T(8,128)(2,1)S(1)} %get-tuple-element.18.sent), channel_id=1, source_target_pairs={{0,1},{1,0},{2,3},{3,2},{4,5},{5,4},{6,7},{7,6},{8,9},{9,8},{10,11... | collective-permute-start | bytes 417800 | tf_op jit(solution)/shard_map/ppermute | solution.py:319
  10.4 8.0 %collective-permute-start.5 = (bf16[2,32,256]{2,1,0:T(8,128)(2,1)S(1)}, bf16[2,32,256]{2,1,0:T(8,128)(2,1)S(1)}, u32[]{:S(2)}, u32[]{:S(2)}) collective-permute-start(bf16[2,32,256]{2,1,0:T(8,128)(2,1)S(1)} %get-tuple-element.22), channel_id=1, source_target_pairs={{0,8},{4,12},{8,0},{12,4},{16,24},{20,28},{24,16},{28,20},{1,9},{5... | collective-permute-start | bytes 98312 | tf_op jit(solution)/shard_map/ppermute | solution.py:331
  11.9 6.4 %collective-permute-start.6 = (bf16[2,32,256]{2,1,0:T(8,128)(2,1)S(1)}, bf16[2,32,256]{2,1,0:T(8,128)(2,1)S(1)}, u32[]{:S(2)}, u32[]{:S(2)}) collective-permute-start(bf16[2,32,256]{2,1,0:T(8,128)(2,1)S(1)} %get-tuple-element.23), channel_id=1, source_target_pairs={{0,16},{4,20},{8,24},{12,28},{16,0},{20,4},{24,8},{28,12},{1,17},{... | collective-permute-start | bytes 98312 | tf_op jit(solution)/shard_map/ppermute | solution.py:331
  14.5 5.7 %collective-permute-start.7 = (bf16[2,32,256]{2,1,0:T(8,128)(2,1)S(1)}, bf16[2,32,256]{2,1,0:T(8,128)(2,1)S(1)}, u32[]{:S(2)}, u32[]{:S(2)}) collective-permute-start(bf16[2,32,256]{2,1,0:T(8,128)(2,1)S(1)} %get-tuple-element.24), channel_id=1, source_target_pairs={{0,24},{4,28},{8,16},{12,20},{16,8},{20,12},{24,0},{28,4},{1,25},{... | collective-permute-start | bytes 98312 | tf_op jit(solution)/shard_map/ppermute | solution.py:331

commit v6 on v5

--- a/solution.py
+++ b/solution.py
@@ -264,6 +264,10 @@
     swap = [(i, i ^ 1) for i in range(mem_total)]
     assert mem_total & (mem_total - 1) == 0
 
+    def trade(layers):
+        return [(i, i ^ (layers * PAIR)) for i in range(mem_total)]
+
+
     pattern = loc_pattern.T
     far_pattern = lax.ppermute(pattern, "lon", far)
     near_pattern = lax.ppermute(pattern, "lon", near)
@@ -326,9 +330,15 @@
         cost_estimate=cost,
         name="own_share",
     )(here, pattern, pert, weights, innov, to_near)
-    for shift in range(1, length):
-        trade = [(i, i ^ (shift * PAIR)) for i in range(mem_total)]
-        slabs[shift] = lax.ppermute(slabs[shift], "mem", trade)
+    legs = {}
+    for shift in sorted(range(1, length), key=lambda value: -value.bit_count()):
+        legs[shift] = [1 << bit for bit in range(length) if shift >> bit & 1]
+        slabs[shift] = lax.ppermute(slabs[shift], "mem", trade(legs[shift][0]))
+    for turn in range(1, length.bit_length() - 1):
+        held = [shift for shift in legs if len(legs[shift]) > turn]
+        moved, _ = lax.optimization_barrier(([slabs[shift] for shift in held], own))
+        for shift, slab in zip(held, moved):
+            slabs[shift] = lax.ppermute(slab, "mem", trade(legs[shift][turn]))
     root, rows = pl.pallas_call(
         root_kernel,
         out_shape=(shape((mine, members, members), BF16), shape((mine, PAD, members), F32)),

time: 31.9 us -> 32.9 us (1.031)
  starting transfers between devices: 10.1 us -> 11.1 us
    ppermute x3 -> x4, starting transfers between devices: 4.39 us -> 5.38 us  [the longest x3 4.61 us: body(): slabs[shift] = lax.ppermute(slabs[shift], 'mem', trade(legs[shift][0]))]
    ppermute x3 -> x4, waiting for transfers between devices: 1.9 us -> 1.65 us  [the longest x1 1.64 us: body(): slabs[shift] = lax.ppermute(slab, 'mem', trade(legs[shift][turn]))]
  transfers between devices with their start and end apart: 8 -> 9, of which waited for: 1 -> 1; matrix products, arithmetic and copies ran while one was open for 0% -> 0% of each run, Pallas kernels for 26% -> 25%
where the time goes in v6:
time: 32.9 us; the launch traced here: 32.7 us
  starting transfers between devices  11.1 us (34%)
  blocking collectives  10.4 us (32%)
  Pallas kernels  8.76 us (27%)
  waiting for transfers between devices  1.66 us (5%)
  local copies, waits for them, and re-layouts  0.67 us (2%)
    all_to_all x1, blocking collectives, body(): lax.all_to_all(updated.reshape(mem_total, local, span), 'mem', split_axis...  10.4 us
    ppermute x3, starting transfers between devices, body(): slabs[shift] = lax.ppermute(slabs[shift], 'mem', trade(legs[shift][0]))  4.61 us
    ppermute x1, starting transfers between devices, body(): paired = lax.ppermute(state, 'mem', swap)  2.94 us
    pallas_call x1, Pallas kernels, body(): pl.pallas_call(root_kernel, out_shape=(shape((mine, members, members), BF...  2.45 us
    pallas_call x1, Pallas kernels, body(): pl.pallas_call(perturb_kernel, out_shape=(shape((blocks, members, width),...  2.15 us
    ppermute x1, waiting for transfers between devices, body(): slabs[shift] = lax.ppermute(slab, 'mem', trade(legs[shift][turn]))  1.64 us
    pallas_call x1, Pallas kernels, body(): pl.pallas_call(functools.partial(near_kernel, patches), out_shape=(packed...  1.27 us
    pallas_call x1, Pallas kernels, body(): pl.pallas_call(functools.partial(far_kernel, patches), out_shape=packed,...  1.12 us
  transfers between devices with their start and end apart: 9, of which 1 were waited for; matrix products, arithmetic and copies ran while one was open for 0% of the time, Pallas kernels for 25%

profile of v6, /device:TPU:0, one launch (start us, length us, event | category | flops | bytes accessed | tf_op | source)
XLA Modules:
  0.0 32.7 jit_solution(3807992931580472963)
XLA Ops:
  0.0 2.9 %collective-permute-start.1 = (bf16[32,2048]{1,0:T(8,128)(2,1)}, bf16[32,2048]{1,0:T(8,128)(2,1)S(1)}, u32[]{:S(2)}, u32[]{:S(2)}) collective-permute-start(bf16[32,2048]{1,0:T(8,128)(2,1)} %state.1), channel_id=1, source_target_pairs={{0,4},{4,0},{8,12},{12,8},{16,20},{20,16},{24,28},{28,24},{1,5},{5... | collective-permute-start | bytes 393224 | tf_op jit(solution)/shard_map/ppermute | solution.py:274
  2.9 0.7 %collective-permute-start.2 = (s32[8,16]{1,0:T(8,128)}, s32[8,16]{1,0:T(8,128)S(1)}, u32[]{:S(2)}, u32[]{:S(2)}) collective-permute-start(s32[8,16]{1,0:T(8,128)} %bitcast.9), channel_id=1, source_target_pairs={{0,3},{1,2},{2,1},{3,0},{4,7},{5,6},{6,5},{7,4},{8,11},{9,10},{10,... | collective-permute-start | bytes 1544 | tf_op jit(solution)/shard_map/ppermute | solution.py:272
  3.6 1.0 %collective-permute-start = (s32[8,16]{1,0:T(8,128)}, s32[8,16]{1,0:T(8,128)S(1)}, u32[]{:S(2)}, u32[]{:S(2)}) collective-permute-start(s32[8,16]{1,0:T(8,128)} %bitcast.10), channel_id=1, source_target_pairs={{0,1},{1,0},{2,3},{3,2},{4,5},{5,4},{6,7},{7,6},{8,9},{9,8},{10,11... | collective-permute-start | bytes 1544 | tf_op jit(solution)/shard_map/ppermute | solution.py:273
  4.6 0.0 copy-start
  4.6 2.2 %perturb.1 = (bf16[32,256,128]{2,1,0:T(8,128)(2,1)S(1)}, f32[32,128]{1,0:T(8,128)S(1)}, f32[32,128]{1,0:T(8,128)S(1)}) custom-call(s32[32]{0:T(128)} %count_all.1, bf16[32,256,128]{2,1,0:T(8,128)(2,1)} %hx.1, f32[32,128]{1,0:T(8,128)} %value_all.1, f32[32,128]{1,0:T(8,128)} %rinv_all.1), custom_call_target="tpu_custom_call" | custom-call | flops 4194304 | bytes 4194304 | tf_op jit(solution)/shard_map/perturb/pallas_call | solution.py:277
  6.7 0.0 collective-permute-done.2.pattern
  6.7 0.0 copy-start.1
  6.8 1.1 %far_share.1.sent = bf16[2,272,128]{2,1,0:T(8,128)(2,1)S(1)} custom-call(s32[1]{0:T(128)} %bitcast.here, s32[1]{0:T(128)} %bitcast.3.side, s32[8,16]{1,0:T(8,128)S(1)} %collective-permute-done.2.pattern, bf16[32,256,128]{2,1,0:T(8,128)(2,1)S(1)} %get-tuple-element.16.pert, f32[32,128]{1,0:T(8,128)S(1)} %get-tuple-element.17.weights, ...), custom_call_target="tpu_custom_call" | custom-call | flops 285212672 | bytes 1048576 | tf_op jit(solution)/shard_map/far_share/pallas_call | solution.py:303
  7.9 0.5 %collective-permute-start.3 = (bf16[2,272,128]{2,1,0:T(8,128)(2,1)S(1)}, bf16[2,272,128]{2,1,0:T(8,128)(2,1)S(1)}, u32[]{:S(2)}, u32[]{:S(2)}) collective-permute-start(bf16[2,272,128]{2,1,0:T(8,128)(2,1)S(1)} %far_share.1.sent), channel_id=1, source_target_pairs={{0,3},{1,2},{2,1},{3,0},{4,7},{5,6},{6,5},{7,4},{8,11},{9,10},{10,... | collective-permute-start | bytes 417800 | tf_op jit(solution)/shard_map/ppermute | solution.py:312
  8.3 0.0 collective-permute-done.pattern
  8.3 0.0 collective-permute-done.1.paired
  8.4 0.0 copy-done
  8.4 1.3 %near_share.1 = (bf16[2,272,128]{2,1,0:T(8,128)(2,1)S(1)}, bf16[2,32,256]{2,1,0:T(8,128)(2,1)S(1)}, bf16[2,32,256]{2,1,0:T(8,128)(2,1)S(1)}, bf16[2,32,256]{2,1,0:T(8,128)(2,1)S(1)}, bf16[2,32,256]{2,1,0:T(8,128)(2,1)S(1)}) custom-call(s32[1]{0:T(128)} %bitcast.here, s32[1]{0:T(128)} %bitcast.2.side, s32[8,16]{1,0:T(8,128)S(1)} %collective-permute-done.pattern, ...), custom_call_target="tpu_custom_call" | custom-call | flops 285212672 | bytes 1048576 | tf_op jit(solution)/shard_map/near_share/pallas_call | solution.py:313
  9.6 0.7 %collective-permute-start.4 = (bf16[2,272,128]{2,1,0:T(8,128)(2,1)S(1)}, bf16[2,272,128]{2,1,0:T(8,128)(2,1)S(1)}, u32[]{:S(2)}, u32[]{:S(2)}) collective-permute-start(bf16[2,272,128]{2,1,0:T(8,128)(2,1)S(1)} %get-tuple-element.19.sent), channel_id=1, source_target_pairs={{0,1},{1,0},{2,3},{3,2},{4,5},{5,4},{6,7},{7,6},{8,9},{9,8},{10,11... | collective-permute-start | bytes 417800 | tf_op jit(solution)/shard_map/ppermute | solution.py:323
  10.4 1.6 %collective-permute-start.7 = (bf16[2,32,256]{2,1,0:T(8,128)(2,1)S(1)}, bf16[2,32,256]{2,1,0:T(8,128)(2,1)S(1)}, u32[]{:S(2)}, u32[]{:S(2)}) collective-permute-start(bf16[2,32,256]{2,1,0:T(8,128)(2,1)S(1)} %get-tuple-element.25), channel_id=1, source_target_pairs={{0,8},{4,12},{8,0},{12,4},{16,24},{20,28},{24,16},{28,20},{1,9},{5... | collective-permute-start | bytes 98312 | tf_op jit(solution)/shard_map/ppermute | solution.py:336
  11.9 0.4 %collective-permute-start.5 = (bf16[2,32,256]{2,1,0:T(8,128)(2,1)S(1)}, bf16[2,32,256]{2,1,0:T(8,128)(2,1)S(1)}, u32[]{:S(2)}, u32[]{:S(2)}) collective-permute-start(bf16[2,32,256]{2,1,0:T(8,128)(2,1)S(1)} %get-tuple-element.23), channel_id=1, source_target_pairs={{0,8},{4,12},{8,0},{12,4},{16,24},{20,28},{24,16},{28,20},{1,9},{5... | collective-permute-start | bytes 98312 | tf_op jit(solution)/shard_map/ppermute | solution.py:336
  12.4 2.6 %collective-permute-start.6 = (bf16[2,32,256]{2,1,0:T(8,128)(2,1)S(1)}, bf16[2,32,256]{2,1,0:T(8,128)(2,1)S(1)}, u32[]{:S(2)}, u32[]{:S(2)}) collective-permute-start(bf16[2,32,256]{2,1,0:T(8,128)(2,1)S(1)} %get-tuple-element.24), channel_id=1, source_target_pairs={{0,16},{4,20},{8,24},{12,28},{16,0},{20,4},{24,8},{28,12},{1,17},{... | collective-permute-start | bytes 98312 | tf_op jit(solution)/shard_map/ppermute | solution.py:336
  15.0 0.0 copy-done.1
  15.0 1.1 %own_share.1.own = f32[2,272,256]{2,1,0:T(8,128)S(1)} custom-call(s32[1]{0:T(128)} %bitcast.here, s32[8,16]{1,0:T(8,128)S(1)} %bitcast.11, bf16[32,256,128]{2,1,0:T(8,128)(2,1)S(1)} %get-tuple-element.16.pert, f32[32,128]{1,0:T(8,128)S(1)} %get-tuple-element.17.weights, f32[32,128]{1,0:T(8,128)S(1)} %get-tuple-element.18.innov, ...), custom_call_target="tpu_custom_call" | custom-call | flops 285212672 | bytes 1048576 | tf_op jit(solution)/shard_map/own_share/pallas_call | solution.py:324
  16.1 0.0 collective-permute-done.7
  16.1 0.8 %collective-permute-start.8 = (bf16[2,32,256]{2,1,0:T(8,128)(2,1)S(1)}, bf16[2,32,256]{2,1,0:T(8,128)(2,1)S(1)}, u32[]{:S(2)}, u32[]{:S(2)}) collective-permute-start(bf16[2,32,256]{2,1,0:T(8,128)(2,1)S(1)} %collective-permute-done.7), channel_id=1, source_target_pairs={{0,16},{4,20},{8,24},{12,28},{16,0},{20,4},{24,8},{28,12},{1,17},{... | collective-permute-start | bytes 98312 | tf_op jit(solution)/shard_map/ppermute | solution.py:341
  16.9 0.0 collective-permute-done.3.before
  16.9 0.0 collective-permute-done.4.after
  16.9 2.5 %root.1 = (bf16[2,256,256]{2,1,0:T(8,128)(2,1)S(1)}, f32[2,16,256]{2,1,0:T(8,128)S(1)}) custom-call(f32[2,272,256]{2,1,0:T(8,128)S(1)} %own_share.1.own, bf16[2,272,128]{2,1,0:T(8,128)(2,1)S(1)} %collective-permute-done.3.before, bf16[2,272,128]{2,1,0:T(8,128)(2,1)S(1)} %collective-permute-done.4.after), custom_call_target="tpu_custom_call" | custom-call | flops 1006632960 | bytes 1048576 | tf_op jit(solution)/shard_map/root/pallas_call | solution.py:342
  19.3 0.0 collective-permute-done.5.rest_1_
  19.3 0.0 collective-permute-done.6.rest_2_
  19.3 1.6 %collective-permute-done.8.rest_3_ = bf16[2,32,256]{2,1,0:T(8,128)(2,1)S(1)} collective-permute-done((bf16[2,32,256]{2,1,0:T(8,128)(2,1)S(1)}, bf16[2,32,256]{2,1,0:T(8,128)(2,1)S(1)}, u32[]{:S(2)}, u32[]{:S(2)}) %collective-permute-start.8) | collective-permute-done | bytes 32800 | tf_op jit(solution)/shard_map/ppermute | solution.py:341
  21.0 0.7 %apply.1 = bf16[256,256]{1,0:T(8,128)(2,1)S(1)} custom-call(s32[1]{0:T(128)} %bitcast.here, bf16[2,256,256]{2,1,0:T(8,128)(2,1)S(1)} %get-tuple-element.20.root, f32[2,16,256]{2,1,0:T(8,128)S(1)} %get-tuple-element.21.rows, bf16[2,32,256]{2,1,0:T(8,128)(2,1)S(1)} %get-tuple-element.22.rest_0_, bf16[2,32,256]{2,1,0:T(8,128)(2,1)S(1)} %collective-permute-done.5.rest_1_, ...), custom_call_target="tpu_custom_call" | custom-call | flops 33554432 | bytes 524288 | tf_op jit(solution)/shard_map/apply/pallas_call | solution.py:353
  21.7 10.4 %all_to_all.5 = bf16[8,32,256]{2,1,0:T(8,128)(2,1)S(1)} all-to-all(bf16[8,32,256]{2,1,0:T(8,128)(2,1)S(1)} %bitcast.8), channel_id=1, replica_groups=mesh['mem'=8,'lon'=4] {'mem'}, dimensions={0} | all-to-all | bytes 262144 | tf_op jit(solution)/shard_map/all_to_all | solution.py:365
  32.0 0.7 %copy.8 = bf16[8,4,8,256]{3,2,0,1:T(8,128)(2,1)} copy(bf16[8,4,8,256]{3,2,1,0:T(8,128)(2,1)S(1)} %bitcast.12) | data formatting | bytes 262144 | tf_op jit(solution)/shard_map/reshape | solution.py:368
Async XLA Ops:
  0.0 8.4 %collective-permute-start.1 = (bf16[32,2048]{1,0:T(8,128)(2,1)}, bf16[32,2048]{1,0:T(8,128)(2,1)S(1)}, u32[]{:S(2)}, u32[]{:S(2)}) collective-permute-start(bf16[32,2048]{1,0:T(8,128)(2,1)} %state.1), channel_id=1, source_target_pairs={{0,4},{4,0},{8,12},{12,8},{16,20},{20,16},{24,28},{28,24},{1,5},{5... | collective-permute-start | bytes 393224 | tf_op jit(solution)/shard_map/ppermute | solution.py:274
  2.9 3.8 %collective-permute-start.2 = (s32[8,16]{1,0:T(8,128)}, s32[8,16]{1,0:T(8,128)S(1)}, u32[]{:S(2)}, u32[]{:S(2)}) collective-permute-start(s32[8,16]{1,0:T(8,128)} %bitcast.9), channel_id=1, source_target_pairs={{0,3},{1,2},{2,1},{3,0},{4,7},{5,6},{6,5},{7,4},{8,11},{9,10},{10,... | collective-permute-start | bytes 1544 | tf_op jit(solution)/shard_map/ppermute | solution.py:272
  3.6 4.7 %collective-permute-start = (s32[8,16]{1,0:T(8,128)}, s32[8,16]{1,0:T(8,128)S(1)}, u32[]{:S(2)}, u32[]{:S(2)}) collective-permute-start(s32[8,16]{1,0:T(8,128)} %bitcast.10), channel_id=1, source_target_pairs={{0,1},{1,0},{2,3},{3,2},{4,5},{5,4},{6,7},{7,6},{8,9},{9,8},{10,11... | collective-permute-start | bytes 1544 | tf_op jit(solution)/shard_map/ppermute | solution.py:273
  4.6 3.8 %copy-start = (bf16[32,2048]{1,0:T(8,128)(2,1)S(1)}, bf16[32,2048]{1,0:T(8,128)(2,1)}, u32[]{:S(2)}) copy-start(bf16[32,2048]{1,0:T(8,128)(2,1)} %state.1) | copy-start | bytes 393220
  6.7 8.2 %copy-start.1 = (s32[16,8]{0,1:T(8,128)S(1)}, s32[16,8]{0,1:T(8,128)}, u32[]{:S(2)}) copy-start(s32[16,8]{0,1:T(8,128)} %param.11) | copy-start | bytes 1540
  7.9 9.0 %collective-permute-start.3 = (bf16[2,272,128]{2,1,0:T(8,128)(2,1)S(1)}, bf16[2,272,128]{2,1,0:T(8,128)(2,1)S(1)}, u32[]{:S(2)}, u32[]{:S(2)}) collective-permute-start(bf16[2,272,128]{2,1,0:T(8,128)(2,1)S(1)} %far_share.1.sent), channel_id=1, source_target_pairs={{0,3},{1,2},{2,1},{3,0},{4,7},{5,6},{6,5},{7,4},{8,11},{9,10},{10,... | collective-permute-start | bytes 417800 | tf_op jit(solution)/shard_map/ppermute | solution.py:312
  9.6 7.2 %collective-permute-start.4 = (bf16[2,272,128]{2,1,0:T(8,128)(2,1)S(1)}, bf16[2,272,128]{2,1,0:T(8,128)(2,1)S(1)}, u32[]{:S(2)}, u32[]{:S(2)}) collective-permute-start(bf16[2,272,128]{2,1,0:T(8,128)(2,1)S(1)} %get-tuple-element.19.sent), channel_id=1, source_target_pairs={{0,1},{1,0},{2,3},{3,2},{4,5},{5,4},{6,7},{7,6},{8,9},{9,8},{10,11... | collective-permute-start | bytes 417800 | tf_op jit(solution)/shard_map/ppermute | solution.py:323
  10.4 5.7 %collective-permute-start.7 = (bf16[2,32,256]{2,1,0:T(8,128)(2,1)S(1)}, bf16[2,32,256]{2,1,0:T(8,128)(2,1)S(1)}, u32[]{:S(2)}, u32[]{:S(2)}) collective-permute-start(bf16[2,32,256]{2,1,0:T(8,128)(2,1)S(1)} %get-tuple-element.25), channel_id=1, source_target_pairs={{0,8},{4,12},{8,0},{12,4},{16,24},{20,28},{24,16},{28,20},{1,9},{5... | collective-permute-start | bytes 98312 | tf_op jit(solution)/shard_map/ppermute | solution.py:336
  11.9 7.4 %collective-permute-start.5 = (bf16[2,32,256]{2,1,0:T(8,128)(2,1)S(1)}, bf16[2,32,256]{2,1,0:T(8,128)(2,1)S(1)}, u32[]{:S(2)}, u32[]{:S(2)}) collective-permute-start(bf16[2,32,256]{2,1,0:T(8,128)(2,1)S(1)} %get-tuple-element.23), channel_id=1, source_target_pairs={{0,8},{4,12},{8,0},{12,4},{16,24},{20,28},{24,16},{28,20},{1,9},{5... | collective-permute-start | bytes 98312 | tf_op jit(solution)/shard_map/ppermute | solution.py:336
  12.4 6.9 %collective-permute-start.6 = (bf16[2,32,256]{2,1,0:T(8,128)(2,1)S(1)}, bf16[2,32,256]{2,1,0:T(8,128)(2,1)S(1)}, u32[]{:S(2)}, u32[]{:S(2)}) collective-permute-start(bf16[2,32,256]{2,1,0:T(8,128)(2,1)S(1)} %get-tuple-element.24), channel_id=1, source_target_pairs={{0,16},{4,20},{8,24},{12,28},{16,0},{20,4},{24,8},{28,12},{1,17},{... | collective-permute-start | bytes 98312 | tf_op jit(solution)/shard_map/ppermute | solution.py:336
  16.1 4.9 %collective-permute-start.8 = (bf16[2,32,256]{2,1,0:T(8,128)(2,1)S(1)}, bf16[2,32,256]{2,1,0:T(8,128)(2,1)S(1)}, u32[]{:S(2)}, u32[]{:S(2)}) collective-permute-start(bf16[2,32,256]{2,1,0:T(8,128)(2,1)S(1)} %collective-permute-done.7), channel_id=1, source_target_pairs={{0,16},{4,20},{8,24},{12,28},{16,0},{20,4},{24,8},{28,12},{1,17},{... | collective-permute-start | bytes 98312 | tf_op jit(solution)/shard_map/ppermute | solution.py:341

commit v7 on v5

--- a/solution.py
+++ b/solution.py
@@ -59,14 +59,31 @@
     )
 
 
-def perturb_kernel(
-    count_all, hx, value_all, rinv_all, pert, weights, innov, raw, count, value, rinv, sems, small
+def own_kernel(
+    patches,
+    here,
+    count_all,
+    pattern_all,
+    hx,
+    value_all,
+    rinv_all,
+    pert,
+    weights,
+    innov,
+    own,
+    raw,
+    count,
+    pattern,
+    value,
+    rinv,
+    sems,
+    small,
 ):
     blocks, members, width = raw.shape
     smalls = [
         pltpu.make_async_copy(source, target, small.at[i])
         for i, (source, target) in enumerate(
-            ((count_all, count), (value_all, value), (rinv_all, rinv))
+            ((count_all, count), (value_all, value), (rinv_all, rinv), (pattern_all, pattern))
         )
     ]
     copies = [
@@ -88,9 +105,6 @@
         gap = weight * (value[block : block + 1, :] - mean)
         weights[block : block + 1, :] = weight.astype(BF16).astype(F32)
         innov[block : block + 1, :] = gap
-
-
-def own_kernel(patches, here, pattern, pert, weights, innov, sent, own):
     mine = own.shape[0]
     for patch in range(mine):
         row = here[0] * mine + patch
@@ -270,29 +284,31 @@
     paired = lax.ppermute(state, "mem", swap)
     limit = pltpu.CompilerParams(vmem_limit_bytes=16 * 1024 * 1024)
     gram = 2 * padded * members * uses * width
-    pert, weights, innov = pl.pallas_call(
-        perturb_kernel,
+    pert, weights, innov, own = pl.pallas_call(
+        functools.partial(own_kernel, patches),
         out_shape=(
             shape((blocks, members, width), BF16),
             shape((blocks, width), F32),
             shape((blocks, width), F32),
+            shape((mine, padded, members), F32),
         ),
-        in_specs=[HBM] * 4,
-        out_specs=(VMEM,) * 3,
+        in_specs=[SMEM] + [HBM] * 5,
+        out_specs=(VMEM,) * 4,
         scratch_shapes=[
             pltpu.VMEM((blocks, members, width), BF16),
             pltpu.SMEM(obs_count.shape, jnp.int32),
+            pltpu.SMEM(pattern.shape, jnp.int32),
             pltpu.VMEM(obs_value.shape, F32),
             pltpu.VMEM(obs_rinv.shape, F32),
             pltpu.SemaphoreType.DMA((blocks // CHUNK,)),
-            pltpu.SemaphoreType.DMA((3,)),
+            pltpu.SemaphoreType.DMA((4,)),
         ],
         compiler_params=limit,
         cost_estimate=pl.CostEstimate(
-            flops=hx.size * 4, bytes_accessed=2 * hx.size * 2, transcendentals=0
+            flops=hx.size * 4 + mine * gram, bytes_accessed=2 * hx.size * 2, transcendentals=0
         ),
-        name="perturb",
-    )(*(stay(value) for value in (obs_count, hx, obs_value, obs_rinv)))
+        name="own_share",
+    )(here, *(stay(value) for value in (obs_count, pattern, hx, obs_value, obs_rinv)))
     packed = shape((mine, padded, members // 2), BF16)
     slab = shape((PAIR, local, span), BF16)
     cost = pl.CostEstimate(flops=mine * gram, bytes_accessed=hx.size, transcendentals=0)
@@ -317,16 +333,7 @@
         name="near_share",
     )(here, near_side, near_pattern, pert, weights, innov, state, paired, to_far)
     from_near = lax.ppermute(to_near, "lon", near)
-    own = pl.pallas_call(
-        functools.partial(own_kernel, patches),
-        out_shape=shape((mine, padded, members), F32),
-        in_specs=[SMEM] * 2 + [VMEM] * 3 + [pl.BlockSpec(memory_space=pl.ANY)],
-        out_specs=VMEM,
-        compiler_params=limit,
-        cost_estimate=cost,
-        name="own_share",
-    )(here, pattern, pert, weights, innov, to_near)
-    for shift in range(1, length):
+    for shift in [*range(2, length), 1]:
         trade = [(i, i ^ (shift * PAIR)) for i in range(mem_total)]
         slabs[shift] = lax.ppermute(slabs[shift], "mem", trade)
     root, rows = pl.pallas_call(

time: 31.9 us -> 31.9 us (level)
  waiting for transfers between devices: 1.91 us -> 3.05 us
  Pallas kernels: 8.76 us -> 8.08 us
  blocking collectives: 10.1 us -> 9.74 us
    ppermute x3, waiting for transfers between devices: 1.9 us -> 3.03 us  [body(): slabs[shift] = lax.ppermute(slabs[shift], 'mem', trade)]
    ppermute x1, starting transfers between devices: 0.96 us -> 0.01 us  [body(): near_pattern = lax.ppermute(pattern, 'lon', near)]
    ppermute x1, starting transfers between devices: 0.68 us -> 1.63 us  [body(): far_pattern = lax.ppermute(pattern, 'lon', far)]
    pallas_call x2 -> x1, Pallas kernels: 3.25 us -> 2.58 us  [body(): pl.pallas_call(functools.partial(own_kernel, patches), out_shape=(shape((...]
    ppermute x1, starting transfers between devices: 0.73 us -> 0.07 us  [body(): from_near = lax.ppermute(to_near, 'lon', near)]
    ppermute x1, starting transfers between devices: 0.46 us -> 0.98 us  [body(): from_far = lax.ppermute(to_far, 'lon', far)]
    all_to_all x1, blocking collectives: 10.1 us -> 9.74 us  [body(): lax.all_to_all(updated.reshape(mem_total, local, span), 'mem', split_axis...]
  transfers between devices with their start and end apart: 8 -> 8, of which waited for: 1 -> 2; matrix products, arithmetic and copies ran while one was open for 0% -> 0% of each run, Pallas kernels for 26% -> 23%
where the time goes in v7:
time: 31.9 us; the launch traced here: 31.7 us
  starting transfers between devices  10.1 us (32%)
  blocking collectives  9.74 us (31%)
  Pallas kernels  8.08 us (25%)
  waiting for transfers between devices  3.05 us (10%)
  local copies, waits for them, and re-layouts  0.67 us (2%)
    all_to_all x1, blocking collectives, body(): lax.all_to_all(updated.reshape(mem_total, local, span), 'mem', split_axis...  9.74 us
    ppermute x3, starting transfers between devices, body(): slabs[shift] = lax.ppermute(slabs[shift], 'mem', trade)  4.45 us
    ppermute x3, waiting for transfers between devices, body(): slabs[shift] = lax.ppermute(slabs[shift], 'mem', trade)  3.03 us
    ppermute x1, starting transfers between devices, body(): paired = lax.ppermute(state, 'mem', swap)  2.94 us
    pallas_call x1, Pallas kernels, body(): pl.pallas_call(functools.partial(own_kernel, patches), out_shape=(shape((...  2.58 us
    pallas_call x1, Pallas kernels, body(): pl.pallas_call(root_kernel, out_shape=(shape((mine, members, members), BF...  2.45 us
    ppermute x1, starting transfers between devices, body(): far_pattern = lax.ppermute(pattern, 'lon', far)  1.63 us
    pallas_call x1, Pallas kernels, body(): pl.pallas_call(functools.partial(near_kernel, patches), out_shape=(packed...  1.27 us
  transfers between devices with their start and end apart: 8, of which 2 were waited for; matrix products, arithmetic and copies ran while one was open for 0% of the time, Pallas kernels for 23%

profile of v7, /device:TPU:0, one launch (start us, length us, event | category | flops | bytes accessed | tf_op | source)
XLA Modules:
  0.0 31.7 jit_solution(16691997972681355768)
XLA Ops:
  0.0 2.9 %collective-permute-start.3 = (bf16[32,2048]{1,0:T(8,128)(2,1)}, bf16[32,2048]{1,0:T(8,128)(2,1)S(1)}, u32[]{:S(2)}, u32[]{:S(2)}) collective-permute-start(bf16[32,2048]{1,0:T(8,128)(2,1)} %state.1), channel_id=1, source_target_pairs={{0,4},{4,0},{8,12},{12,8},{16,20},{20,16},{24,28},{28,24},{1,5},{5... | collective-permute-start | bytes 393224 | tf_op jit(solution)/shard_map/ppermute | solution.py:284
  2.9 0.0 collective-permute-start.2
  2.9 1.6 %collective-permute-start = (s32[8,16]{1,0:T(8,128)}, s32[8,16]{1,0:T(8,128)S(1)}, u32[]{:S(2)}, u32[]{:S(2)}) collective-permute-start(s32[8,16]{1,0:T(8,128)} %bitcast.11), channel_id=1, source_target_pairs={{0,3},{1,2},{2,1},{3,0},{4,7},{5,6},{6,5},{7,4},{8,11},{9,10},{10,... | collective-permute-start | bytes 1544 | tf_op jit(solution)/shard_map/ppermute | solution.py:282
  4.6 0.0 copy-start
  4.6 2.6 %own_share.1 = (bf16[32,256,128]{2,1,0:T(8,128)(2,1)S(1)}, f32[32,128]{1,0:T(8,128)S(1)}, f32[32,128]{1,0:T(8,128)S(1)}, f32[2,272,256]{2,1,0:T(8,128)S(1)}) custom-call(s32[1]{0:T(128)} %bitcast.here, s32[32]{0:T(128)} %count_all.1, s32[8,16]{1,0:T(8,128)} %bitcast.12, bf16[32,256,128]{2,1,0:T(8,128)(2,1)} %hx.1, f32[32,128]{1,0:T(8,128)} %value_all.1, ...), custom_call_target="tpu_custom_call" | custom-call | flops 289406976 | bytes 4194304 | tf_op jit(solution)/shard_map/own_share/pallas_call | solution.py:287
  7.2 0.0 collective-permute-done.pattern
  7.2 1.1 %far_share.1.sent = bf16[2,272,128]{2,1,0:T(8,128)(2,1)S(1)} custom-call(s32[1]{0:T(128)} %bitcast.here, s32[1]{0:T(128)} %bitcast.2.side, s32[8,16]{1,0:T(8,128)S(1)} %collective-permute-done.pattern, bf16[32,256,128]{2,1,0:T(8,128)(2,1)S(1)} %get-tuple-element.17.pert, f32[32,128]{1,0:T(8,128)S(1)} %get-tuple-element.18.weights, ...), custom_call_target="tpu_custom_call" | custom-call | flops 285212672 | bytes 1048576 | tf_op jit(solution)/shard_map/far_share/pallas_call | solution.py:315
  8.3 1.0 %collective-permute-start.1 = (bf16[2,272,128]{2,1,0:T(8,128)(2,1)S(1)}, bf16[2,272,128]{2,1,0:T(8,128)(2,1)S(1)}, u32[]{:S(2)}, u32[]{:S(2)}) collective-permute-start(bf16[2,272,128]{2,1,0:T(8,128)(2,1)S(1)} %far_share.1.sent), channel_id=1, source_target_pairs={{0,3},{1,2},{2,1},{3,0},{4,7},{5,6},{6,5},{7,4},{8,11},{9,10},{10,... | collective-permute-start | bytes 417800 | tf_op jit(solution)/shard_map/ppermute | solution.py:324
  9.3 0.0 collective-permute-done.2.pattern
  9.3 0.0 collective-permute-done.3.paired
  9.3 0.0 copy-done
  9.3 1.3 %near_share.1 = (bf16[2,272,128]{2,1,0:T(8,128)(2,1)S(1)}, bf16[2,32,256]{2,1,0:T(8,128)(2,1)S(1)}, bf16[2,32,256]{2,1,0:T(8,128)(2,1)S(1)}, bf16[2,32,256]{2,1,0:T(8,128)(2,1)S(1)}, bf16[2,32,256]{2,1,0:T(8,128)(2,1)S(1)}) custom-call(s32[1]{0:T(128)} %bitcast.here, s32[1]{0:T(128)} %bitcast.3.side, s32[8,16]{1,0:T(8,128)S(1)} %collective-permute-done.2.pattern, ...), custom_call_target="tpu_custom_call" | custom-call | flops 285212672 | bytes 1048576 | tf_op jit(solution)/shard_map/near_share/pallas_call | solution.py:325
  10.6 0.1 collective-permute-start.4
  10.7 1.6 %collective-permute-start.5 = (bf16[2,32,256]{2,1,0:T(8,128)(2,1)S(1)}, bf16[2,32,256]{2,1,0:T(8,128)(2,1)S(1)}, u32[]{:S(2)}, u32[]{:S(2)}) collective-permute-start(bf16[2,32,256]{2,1,0:T(8,128)(2,1)S(1)} %get-tuple-element.24), channel_id=1, source_target_pairs={{0,8},{4,12},{8,0},{12,4},{16,24},{20,28},{24,16},{28,20},{1,9},{5... | collective-permute-start | bytes 98312 | tf_op jit(solution)/shard_map/ppermute | solution.py:338
  12.3 2.6 %collective-permute-start.6 = (bf16[2,32,256]{2,1,0:T(8,128)(2,1)S(1)}, bf16[2,32,256]{2,1,0:T(8,128)(2,1)S(1)}, u32[]{:S(2)}, u32[]{:S(2)}) collective-permute-start(bf16[2,32,256]{2,1,0:T(8,128)(2,1)S(1)} %get-tuple-element.25), channel_id=1, source_target_pairs={{0,16},{4,20},{8,24},{12,28},{16,0},{20,4},{24,8},{28,12},{1,17},{... | collective-permute-start | bytes 98312 | tf_op jit(solution)/shard_map/ppermute | solution.py:338
  14.9 0.2 collective-permute-start.7
  15.1 0.0 collective-permute-done.1.before
  15.1 0.0 collective-permute-done.4.after
  15.1 2.5 %root.1 = (bf16[2,256,256]{2,1,0:T(8,128)(2,1)S(1)}, f32[2,16,256]{2,1,0:T(8,128)S(1)}) custom-call(f32[2,272,256]{2,1,0:T(8,128)S(1)} %get-tuple-element.16.own, bf16[2,272,128]{2,1,0:T(8,128)(2,1)S(1)} %collective-permute-done.1.before, bf16[2,272,128]{2,1,0:T(8,128)(2,1)S(1)} %collective-permute-done.4.after), custom_call_target="tpu_custom_call" | custom-call | flops 1006632960 | bytes 1048576 | tf_op jit(solution)/shard_map/root/pallas_call | solution.py:339
  17.6 0.0 collective-permute-done.5.rest_1_
  17.6 0.1 collective-permute-done.6.rest_2_
  17.7 2.9 %collective-permute-done.7.rest_3_ = bf16[2,32,256]{2,1,0:T(8,128)(2,1)S(1)} collective-permute-done((bf16[2,32,256]{2,1,0:T(8,128)(2,1)S(1)}, bf16[2,32,256]{2,1,0:T(8,128)(2,1)S(1)}, u32[]{:S(2)}, u32[]{:S(2)}) %collective-permute-start.7) | collective-permute-done | bytes 32800 | tf_op jit(solution)/shard_map/ppermute | solution.py:338
  20.6 0.7 %apply.1 = bf16[256,256]{1,0:T(8,128)(2,1)S(1)} custom-call(s32[1]{0:T(128)} %bitcast.here, bf16[2,256,256]{2,1,0:T(8,128)(2,1)S(1)} %get-tuple-element.21.root, f32[2,16,256]{2,1,0:T(8,128)S(1)} %get-tuple-element.22.rows, bf16[2,32,256]{2,1,0:T(8,128)(2,1)S(1)} %get-tuple-element.23.rest_0_, bf16[2,32,256]{2,1,0:T(8,128)(2,1)S(1)} %collective-permute-done.5.rest_1_, ...), custom_call_target="tpu_custom_call" | custom-call | flops 33554432 | bytes 524288 | tf_op jit(solution)/shard_map/apply/pallas_call | solution.py:350
  21.3 9.7 %all_to_all.5 = bf16[8,32,256]{2,1,0:T(8,128)(2,1)S(1)} all-to-all(bf16[8,32,256]{2,1,0:T(8,128)(2,1)S(1)} %bitcast.8), channel_id=1, replica_groups=mesh['mem'=8,'lon'=4] {'mem'}, dimensions={0} | all-to-all | bytes 262144 | tf_op jit(solution)/shard_map/all_to_all | solution.py:362
  31.0 0.7 %copy.8 = bf16[8,4,8,256]{3,2,0,1:T(8,128)(2,1)} copy(bf16[8,4,8,256]{3,2,1,0:T(8,128)(2,1)S(1)} %bitcast.9) | data formatting | bytes 262144 | tf_op jit(solution)/shard_map/reshape | solution.py:365
Async XLA Ops:
  0.0 9.3 %collective-permute-start.3 = (bf16[32,2048]{1,0:T(8,128)(2,1)}, bf16[32,2048]{1,0:T(8,128)(2,1)S(1)}, u32[]{:S(2)}, u32[]{:S(2)}) collective-permute-start(bf16[32,2048]{1,0:T(8,128)(2,1)} %state.1), channel_id=1, source_target_pairs={{0,4},{4,0},{8,12},{12,8},{16,20},{20,16},{24,28},{28,24},{1,5},{5... | collective-permute-start | bytes 393224 | tf_op jit(solution)/shard_map/ppermute | solution.py:284
  2.9 6.4 %collective-permute-start.2 = (s32[8,16]{1,0:T(8,128)}, s32[8,16]{1,0:T(8,128)S(1)}, u32[]{:S(2)}, u32[]{:S(2)}) collective-permute-start(s32[8,16]{1,0:T(8,128)} %bitcast.10), channel_id=1, source_target_pairs={{0,1},{1,0},{2,3},{3,2},{4,5},{5,4},{6,7},{7,6},{8,9},{9,8},{10,11... | collective-permute-start | bytes 1544 | tf_op jit(solution)/shard_map/ppermute | solution.py:283
  2.9 4.2 %collective-permute-start = (s32[8,16]{1,0:T(8,128)}, s32[8,16]{1,0:T(8,128)S(1)}, u32[]{:S(2)}, u32[]{:S(2)}) collective-permute-start(s32[8,16]{1,0:T(8,128)} %bitcast.11), channel_id=1, source_target_pairs={{0,3},{1,2},{2,1},{3,0},{4,7},{5,6},{6,5},{7,4},{8,11},{9,10},{10,... | collective-permute-start | bytes 1544 | tf_op jit(solution)/shard_map/ppermute | solution.py:282
  4.6 4.7 %copy-start = (bf16[32,2048]{1,0:T(8,128)(2,1)S(1)}, bf16[32,2048]{1,0:T(8,128)(2,1)}, u32[]{:S(2)}) copy-start(bf16[32,2048]{1,0:T(8,128)(2,1)} %state.1) | copy-start | bytes 393220
  8.3 6.8 %collective-permute-start.1 = (bf16[2,272,128]{2,1,0:T(8,128)(2,1)S(1)}, bf16[2,272,128]{2,1,0:T(8,128)(2,1)S(1)}, u32[]{:S(2)}, u32[]{:S(2)}) collective-permute-start(bf16[2,272,128]{2,1,0:T(8,128)(2,1)S(1)} %far_share.1.sent), channel_id=1, source_target_pairs={{0,3},{1,2},{2,1},{3,0},{4,7},{5,6},{6,5},{7,4},{8,11},{9,10},{10,... | collective-permute-start | bytes 417800 | tf_op jit(solution)/shard_map/ppermute | solution.py:324
  10.6 4.5 %collective-permute-start.4 = (bf16[2,272,128]{2,1,0:T(8,128)(2,1)S(1)}, bf16[2,272,128]{2,1,0:T(8,128)(2,1)S(1)}, u32[]{:S(2)}, u32[]{:S(2)}) collective-permute-start(bf16[2,272,128]{2,1,0:T(8,128)(2,1)S(1)} %get-tuple-element.20), channel_id=1, source_target_pairs={{0,1},{1,0},{2,3},{3,2},{4,5},{5,4},{6,7},{7,6},{8,9},{9,8},{10,11... | collective-permute-start | bytes 417800 | tf_op jit(solution)/shard_map/ppermute | solution.py:335
  10.7 6.9 %collective-permute-start.5 = (bf16[2,32,256]{2,1,0:T(8,128)(2,1)S(1)}, bf16[2,32,256]{2,1,0:T(8,128)(2,1)S(1)}, u32[]{:S(2)}, u32[]{:S(2)}) collective-permute-start(bf16[2,32,256]{2,1,0:T(8,128)(2,1)S(1)} %get-tuple-element.24), channel_id=1, source_target_pairs={{0,8},{4,12},{8,0},{12,4},{16,24},{20,28},{24,16},{28,20},{1,9},{5... | collective-permute-start | bytes 98312 | tf_op jit(solution)/shard_map/ppermute | solution.py:338
  12.3 5.4 %collective-permute-start.6 = (bf16[2,32,256]{2,1,0:T(8,128)(2,1)S(1)}, bf16[2,32,256]{2,1,0:T(8,128)(2,1)S(1)}, u32[]{:S(2)}, u32[]{:S(2)}) collective-permute-start(bf16[2,32,256]{2,1,0:T(8,128)(2,1)S(1)} %get-tuple-element.25), channel_id=1, source_target_pairs={{0,16},{4,20},{8,24},{12,28},{16,0},{20,4},{24,8},{28,12},{1,17},{... | collective-permute-start | bytes 98312 | tf_op jit(solution)/shard_map/ppermute | solution.py:338
  14.9 5.7 %collective-permute-start.7 = (bf16[2,32,256]{2,1,0:T(8,128)(2,1)S(1)}, bf16[2,32,256]{2,1,0:T(8,128)(2,1)S(1)}, u32[]{:S(2)}, u32[]{:S(2)}) collective-permute-start(bf16[2,32,256]{2,1,0:T(8,128)(2,1)S(1)} %get-tuple-element.26), channel_id=1, source_target_pairs={{0,24},{4,28},{8,16},{12,20},{16,8},{20,12},{24,0},{28,4},{1,25},{... | collective-permute-start | bytes 98312 | tf_op jit(solution)/shard_map/ppermute | solution.py:338

commit v8 on v7

--- a/solution.py
+++ b/solution.py
@@ -17,6 +17,10 @@
 VMEM = pl.BlockSpec(memory_space=pltpu.VMEM)
 SMEM = pl.BlockSpec(memory_space=pltpu.SMEM)
 HBM = pl.BlockSpec(memory_space=pltpu.HBM)
+
+
+def turns(length):
+    return [0, *range(2, length), 1][:length]
 
 
 def stay(value):
@@ -145,7 +149,7 @@
     length = len(slabs)
     layer, place = here[0] // PAIR, here[0] % PAIR
     moves = []
-    for shift, slab in enumerate(slabs):
+    for shift, slab in zip(turns(length), slabs):
         target = (layer ^ shift) * PAIR + place
         cols = pl.ds(pl.multiple_of(target * span, span), span)
         moves.append((state.at[:, cols], slab.at[place]))
@@ -196,15 +200,16 @@
             axis=0,
         )
         grams = own[patch, :members, :] + far
-        trace = total(jnp.where(diagonal, grams, 0.0))
+        blocks = grams[:half, :half] + grams[half:, half:]
+        trace = total(jnp.where(above == across, blocks, 0.0))
         norm = jnp.sqrt(total(grams * grams) + 2.0 * base * trace + base * base * members)
         scale.append(norm)
         forcing.append(force + own[patch, members : members + 1, :])
         factor.append(1.5 - 0.5 * (trace / members + base) / norm)
         level = trace / members
         rest.append((grams - jnp.where(diagonal, level, 0.0)) * (-0.5 / norm))
-    lead, tail = list(factor), list(rest)
     small = [rest[p].astype(BF16) for p in each]
+    lead, tail = list(factor), list(small)
     squares = [dot(small[p], small[p]) for p in each]
     for step in range(1, ITERS):
         cubes = [dot(squares[p].astype(BF16), small[p]) for p in each]
@@ -216,16 +221,16 @@
             factor[p] = 1.5 - 1.5 * f * f + f * f * f
             small[p] = rest[p].astype(BF16)
         for p in each:
-            narrow = tail[p].astype(BF16)
+            narrow = tail[p]
             if step < ITERS - 1:
                 both = dot(jnp.concatenate([small[p], narrow], axis=0), small[p])
                 squares[p], cross = both[:members], both[members:]
             else:
                 cross = dot(narrow, small[p])
-            tail[p] = factor[p] * tail[p] + lead[p] * rest[p] + cross
+            tail[p] = (factor[p] * narrow.astype(F32) + lead[p] * rest[p] + cross).astype(BF16)
             lead[p] = factor[p] * lead[p]
     for p in each:
-        high = tail[p].astype(BF16)
+        high = tail[p]
         root_out[p] = high
         force = jnp.broadcast_to(forcing[p], (PAD, members))
         gain = (lead[p] * force + dot(force.astype(BF16), high)) / scale[p]
@@ -240,7 +245,7 @@
     points = out.shape[1] // mine
     length = len(slabs)
     _, local, _ = slabs[0].shape
-    for shift, slab in enumerate(slabs):
+    for shift, slab in zip(turns(length), slabs):
         source = (here[0] // PAIR) ^ shift
         for i in range(PAIR):
             place = pl.ds(pl.multiple_of((source * PAIR + i) * local, local), local)
@@ -333,9 +338,10 @@
         name="near_share",
     )(here, near_side, near_pattern, pert, weights, innov, state, paired, to_far)
     from_near = lax.ppermute(to_near, "lon", near)
-    for shift in [*range(2, length), 1]:
-        trade = [(i, i ^ (shift * PAIR)) for i in range(mem_total)]
-        slabs[shift] = lax.ppermute(slabs[shift], "mem", trade)
+    for i, shift in enumerate(turns(length)):
+        if shift:
+            trade = [(j, j ^ (shift * PAIR)) for j in range(mem_total)]
+            slabs[i] = lax.ppermute(slabs[i], "mem", trade)
     root, rows = pl.pallas_call(
         root_kernel,
         out_shape=(shape((mine, members, members), BF16), shape((mine, PAD, members), F32)),

time: 31.9 us -> 31 us (0.972)
  waiting for transfers between devices: 3.05 us -> 1.75 us
  blocking collectives: 9.74 us -> 10.4 us
    ppermute x3, waiting for transfers between devices: 3.03 us -> 1.73 us  [body(): slabs[i] = lax.ppermute(slabs[i], 'mem', trade)]
    all_to_all x1, blocking collectives: 9.74 us -> 10.4 us  [body(): lax.all_to_all(updated.reshape(mem_total, local, span), 'mem', split_axis...]
  transfers between devices with their start and end apart: 8 -> 8, of which waited for: 2 -> 1; matrix products, arithmetic and copies ran while one was open for 0% -> 0% of each run, Pallas kernels for 23% -> 24%
where the time goes in v8:
time: 31 us; the launch traced here: 30.8 us
  blocking collectives  10.4 us (34%)
  starting transfers between devices  9.86 us (32%)
  Pallas kernels  8.03 us (26%)
  waiting for transfers between devices  1.75 us (6%)
  local copies, waits for them, and re-layouts  0.67 us (2%)
    all_to_all x1, blocking collectives, body(): lax.all_to_all(updated.reshape(mem_total, local, span), 'mem', split_axis...  10.4 us
    ppermute x3, starting transfers between devices, body(): slabs[i] = lax.ppermute(slabs[i], 'mem', trade)  4.24 us
    ppermute x1, starting transfers between devices, body(): paired = lax.ppermute(state, 'mem', swap)  2.94 us
    pallas_call x1, Pallas kernels, body(): pl.pallas_call(functools.partial(own_kernel, patches), out_shape=(shape((...  2.58 us
    pallas_call x1, Pallas kernels, body(): pl.pallas_call(root_kernel, out_shape=(shape((mine, members, members), BF...  2.4 us
    ppermute x3, waiting for transfers between devices, body(): slabs[i] = lax.ppermute(slabs[i], 'mem', trade)  1.73 us
    ppermute x1, starting transfers between devices, body(): far_pattern = lax.ppermute(pattern, 'lon', far)  1.63 us
    pallas_call x1, Pallas kernels, body(): pl.pallas_call(functools.partial(near_kernel, patches), out_shape=(packed...  1.27 us
  transfers between devices with their start and end apart: 8, of which 1 were waited for; matrix products, arithmetic and copies ran while one was open for 0% of the time, Pallas kernels for 24%

profile of v8, /device:TPU:0, one launch (start us, length us, event | category | flops | bytes accessed | tf_op | source)
XLA Modules:
  0.0 30.8 jit_solution(17721601358888413490)
XLA Ops:
  0.0 2.9 %collective-permute-start.3 = (bf16[32,2048]{1,0:T(8,128)(2,1)}, bf16[32,2048]{1,0:T(8,128)(2,1)S(1)}, u32[]{:S(2)}, u32[]{:S(2)}) collective-permute-start(bf16[32,2048]{1,0:T(8,128)(2,1)} %state.1), channel_id=1, source_target_pairs={{0,4},{4,0},{8,12},{12,8},{16,20},{20,16},{24,28},{28,24},{1,5},{5... | collective-permute-start | bytes 393224 | tf_op jit(solution)/shard_map/ppermute | solution.py:289
  2.9 0.0 collective-permute-start.2
  2.9 1.6 %collective-permute-start = (s32[8,16]{1,0:T(8,128)}, s32[8,16]{1,0:T(8,128)S(1)}, u32[]{:S(2)}, u32[]{:S(2)}) collective-permute-start(s32[8,16]{1,0:T(8,128)} %bitcast.11), channel_id=1, source_target_pairs={{0,3},{1,2},{2,1},{3,0},{4,7},{5,6},{6,5},{7,4},{8,11},{9,10},{10,... | collective-permute-start | bytes 1544 | tf_op jit(solution)/shard_map/ppermute | solution.py:287
  4.6 0.0 copy-start
  4.6 2.6 %own_share.1 = (bf16[32,256,128]{2,1,0:T(8,128)(2,1)S(1)}, f32[32,128]{1,0:T(8,128)S(1)}, f32[32,128]{1,0:T(8,128)S(1)}, f32[2,272,256]{2,1,0:T(8,128)S(1)}) custom-call(s32[1]{0:T(128)} %bitcast.here, s32[32]{0:T(128)} %count_all.1, s32[8,16]{1,0:T(8,128)} %bitcast.12, bf16[32,256,128]{2,1,0:T(8,128)(2,1)} %hx.1, f32[32,128]{1,0:T(8,128)} %value_all.1, ...), custom_call_target="tpu_custom_call" | custom-call | flops 289406976 | bytes 4194304 | tf_op jit(solution)/shard_map/own_share/pallas_call | solution.py:292
  7.2 0.0 collective-permute-done.pattern
  7.2 1.1 %far_share.1.sent = bf16[2,272,128]{2,1,0:T(8,128)(2,1)S(1)} custom-call(s32[1]{0:T(128)} %bitcast.here, s32[1]{0:T(128)} %bitcast.2.side, s32[8,16]{1,0:T(8,128)S(1)} %collective-permute-done.pattern, bf16[32,256,128]{2,1,0:T(8,128)(2,1)S(1)} %get-tuple-element.17.pert, f32[32,128]{1,0:T(8,128)S(1)} %get-tuple-element.18.weights, ...), custom_call_target="tpu_custom_call" | custom-call | flops 285212672 | bytes 1048576 | tf_op jit(solution)/shard_map/far_share/pallas_call | solution.py:320
  8.3 1.0 %collective-permute-start.1 = (bf16[2,272,128]{2,1,0:T(8,128)(2,1)S(1)}, bf16[2,272,128]{2,1,0:T(8,128)(2,1)S(1)}, u32[]{:S(2)}, u32[]{:S(2)}) collective-permute-start(bf16[2,272,128]{2,1,0:T(8,128)(2,1)S(1)} %far_share.1.sent), channel_id=1, source_target_pairs={{0,3},{1,2},{2,1},{3,0},{4,7},{5,6},{6,5},{7,4},{8,11},{9,10},{10,... | collective-permute-start | bytes 417800 | tf_op jit(solution)/shard_map/ppermute | solution.py:329
  9.3 0.0 collective-permute-done.2.pattern
  9.3 0.0 collective-permute-done.3.paired
  9.3 0.0 copy-done
  9.3 1.3 %near_share.1 = (bf16[2,272,128]{2,1,0:T(8,128)(2,1)S(1)}, bf16[2,32,256]{2,1,0:T(8,128)(2,1)S(1)}, bf16[2,32,256]{2,1,0:T(8,128)(2,1)S(1)}, bf16[2,32,256]{2,1,0:T(8,128)(2,1)S(1)}, bf16[2,32,256]{2,1,0:T(8,128)(2,1)S(1)}) custom-call(s32[1]{0:T(128)} %bitcast.here, s32[1]{0:T(128)} %bitcast.3.side, s32[8,16]{1,0:T(8,128)S(1)} %collective-permute-done.2.pattern, ...), custom_call_target="tpu_custom_call" | custom-call | flops 285212672 | bytes 1048576 | tf_op jit(solution)/shard_map/near_share/pallas_call | solution.py:330
  10.6 0.1 collective-permute-start.4
  10.7 2.7 %collective-permute-start.5 = (bf16[2,32,256]{2,1,0:T(8,128)(2,1)S(1)}, bf16[2,32,256]{2,1,0:T(8,128)(2,1)S(1)}, u32[]{:S(2)}, u32[]{:S(2)}) collective-permute-start(bf16[2,32,256]{2,1,0:T(8,128)(2,1)S(1)} %get-tuple-element.24), channel_id=1, source_target_pairs={{0,16},{4,20},{8,24},{12,28},{16,0},{20,4},{24,8},{28,12},{1,17},{... | collective-permute-start | bytes 98312 | tf_op jit(solution)/shard_map/ppermute | solution.py:344
  13.3 1.3 %collective-permute-start.6 = (bf16[2,32,256]{2,1,0:T(8,128)(2,1)S(1)}, bf16[2,32,256]{2,1,0:T(8,128)(2,1)S(1)}, u32[]{:S(2)}, u32[]{:S(2)}) collective-permute-start(bf16[2,32,256]{2,1,0:T(8,128)(2,1)S(1)} %get-tuple-element.25), channel_id=1, source_target_pairs={{0,24},{4,28},{8,16},{12,20},{16,8},{20,12},{24,0},{28,4},{1,25},{... | collective-permute-start | bytes 98312 | tf_op jit(solution)/shard_map/ppermute | solution.py:344
  14.7 0.2 collective-permute-start.7
  14.9 0.0 collective-permute-done.1.before
  14.9 0.0 collective-permute-done.4.after
  14.9 2.4 %root.1 = (bf16[2,256,256]{2,1,0:T(8,128)(2,1)S(1)}, f32[2,16,256]{2,1,0:T(8,128)S(1)}) custom-call(f32[2,272,256]{2,1,0:T(8,128)S(1)} %get-tuple-element.16.own, bf16[2,272,128]{2,1,0:T(8,128)(2,1)S(1)} %collective-permute-done.1.before, bf16[2,272,128]{2,1,0:T(8,128)(2,1)S(1)} %collective-permute-done.4.after), custom_call_target="tpu_custom_call" | custom-call | flops 1006632960 | bytes 1048576 | tf_op jit(solution)/shard_map/root/pallas_call | solution.py:345
  17.3 0.0 collective-permute-done.5.rest_1_
  17.3 1.7 %collective-permute-done.6.rest_2_ = bf16[2,32,256]{2,1,0:T(8,128)(2,1)S(1)} collective-permute-done((bf16[2,32,256]{2,1,0:T(8,128)(2,1)S(1)}, bf16[2,32,256]{2,1,0:T(8,128)(2,1)S(1)}, u32[]{:S(2)}, u32[]{:S(2)}) %collective-permute-start.6) | collective-permute-done | bytes 32800 | tf_op jit(solution)/shard_map/ppermute | solution.py:344
  19.0 0.0 collective-permute-done.7.rest_3_
  19.0 0.7 %apply.1 = bf16[256,256]{1,0:T(8,128)(2,1)S(1)} custom-call(s32[1]{0:T(128)} %bitcast.here, bf16[2,256,256]{2,1,0:T(8,128)(2,1)S(1)} %get-tuple-element.21.root, f32[2,16,256]{2,1,0:T(8,128)S(1)} %get-tuple-element.22.rows, bf16[2,32,256]{2,1,0:T(8,128)(2,1)S(1)} %get-tuple-element.23.rest_0_, bf16[2,32,256]{2,1,0:T(8,128)(2,1)S(1)} %collective-permute-done.5.rest_1_, ...), custom_call_target="tpu_custom_call" | custom-call | flops 33554432 | bytes 524288 | tf_op jit(solution)/shard_map/apply/pallas_call | solution.py:356
  19.7 10.4 %all_to_all.5 = bf16[8,32,256]{2,1,0:T(8,128)(2,1)S(1)} all-to-all(bf16[8,32,256]{2,1,0:T(8,128)(2,1)S(1)} %bitcast.8), channel_id=1, replica_groups=mesh['mem'=8,'lon'=4] {'mem'}, dimensions={0} | all-to-all | bytes 262144 | tf_op jit(solution)/shard_map/all_to_all | solution.py:368
  30.2 0.7 %copy.8 = bf16[8,4,8,256]{3,2,0,1:T(8,128)(2,1)} copy(bf16[8,4,8,256]{3,2,1,0:T(8,128)(2,1)S(1)} %bitcast.9) | data formatting | bytes 262144 | tf_op jit(solution)/shard_map/reshape | solution.py:371
Async XLA Ops:
  0.0 9.3 %collective-permute-start.3 = (bf16[32,2048]{1,0:T(8,128)(2,1)}, bf16[32,2048]{1,0:T(8,128)(2,1)S(1)}, u32[]{:S(2)}, u32[]{:S(2)}) collective-permute-start(bf16[32,2048]{1,0:T(8,128)(2,1)} %state.1), channel_id=1, source_target_pairs={{0,4},{4,0},{8,12},{12,8},{16,20},{20,16},{24,28},{28,24},{1,5},{5... | collective-permute-start | bytes 393224 | tf_op jit(solution)/shard_map/ppermute | solution.py:289
  2.9 6.4 %collective-permute-start.2 = (s32[8,16]{1,0:T(8,128)}, s32[8,16]{1,0:T(8,128)S(1)}, u32[]{:S(2)}, u32[]{:S(2)}) collective-permute-start(s32[8,16]{1,0:T(8,128)} %bitcast.10), channel_id=1, source_target_pairs={{0,1},{1,0},{2,3},{3,2},{4,5},{5,4},{6,7},{7,6},{8,9},{9,8},{10,11... | collective-permute-start | bytes 1544 | tf_op jit(solution)/shard_map/ppermute | solution.py:288
  2.9 4.2 %collective-permute-start = (s32[8,16]{1,0:T(8,128)}, s32[8,16]{1,0:T(8,128)S(1)}, u32[]{:S(2)}, u32[]{:S(2)}) collective-permute-start(s32[8,16]{1,0:T(8,128)} %bitcast.11), channel_id=1, source_target_pairs={{0,3},{1,2},{2,1},{3,0},{4,7},{5,6},{6,5},{7,4},{8,11},{9,10},{10,... | collective-permute-start | bytes 1544 | tf_op jit(solution)/shard_map/ppermute | solution.py:287
  4.6 4.7 %copy-start = (bf16[32,2048]{1,0:T(8,128)(2,1)S(1)}, bf16[32,2048]{1,0:T(8,128)(2,1)}, u32[]{:S(2)}) copy-start(bf16[32,2048]{1,0:T(8,128)(2,1)} %state.1) | copy-start | bytes 393220
  8.3 6.6 %collective-permute-start.1 = (bf16[2,272,128]{2,1,0:T(8,128)(2,1)S(1)}, bf16[2,272,128]{2,1,0:T(8,128)(2,1)S(1)}, u32[]{:S(2)}, u32[]{:S(2)}) collective-permute-start(bf16[2,272,128]{2,1,0:T(8,128)(2,1)S(1)} %far_share.1.sent), channel_id=1, source_target_pairs={{0,3},{1,2},{2,1},{3,0},{4,7},{5,6},{6,5},{7,4},{8,11},{9,10},{10,... | collective-permute-start | bytes 417800 | tf_op jit(solution)/shard_map/ppermute | solution.py:329
  10.6 4.3 %collective-permute-start.4 = (bf16[2,272,128]{2,1,0:T(8,128)(2,1)S(1)}, bf16[2,272,128]{2,1,0:T(8,128)(2,1)S(1)}, u32[]{:S(2)}, u32[]{:S(2)}) collective-permute-start(bf16[2,272,128]{2,1,0:T(8,128)(2,1)S(1)} %get-tuple-element.20), channel_id=1, source_target_pairs={{0,1},{1,0},{2,3},{3,2},{4,5},{5,4},{6,7},{7,6},{8,9},{9,8},{10,11... | collective-permute-start | bytes 417800 | tf_op jit(solution)/shard_map/ppermute | solution.py:340
  10.7 6.6 %collective-permute-start.5 = (bf16[2,32,256]{2,1,0:T(8,128)(2,1)S(1)}, bf16[2,32,256]{2,1,0:T(8,128)(2,1)S(1)}, u32[]{:S(2)}, u32[]{:S(2)}) collective-permute-start(bf16[2,32,256]{2,1,0:T(8,128)(2,1)S(1)} %get-tuple-element.24), channel_id=1, source_target_pairs={{0,16},{4,20},{8,24},{12,28},{16,0},{20,4},{24,8},{28,12},{1,17},{... | collective-permute-start | bytes 98312 | tf_op jit(solution)/shard_map/ppermute | solution.py:344
  13.3 5.7 %collective-permute-start.6 = (bf16[2,32,256]{2,1,0:T(8,128)(2,1)S(1)}, bf16[2,32,256]{2,1,0:T(8,128)(2,1)S(1)}, u32[]{:S(2)}, u32[]{:S(2)}) collective-permute-start(bf16[2,32,256]{2,1,0:T(8,128)(2,1)S(1)} %get-tuple-element.25), channel_id=1, source_target_pairs={{0,24},{4,28},{8,16},{12,20},{16,8},{20,12},{24,0},{28,4},{1,25},{... | collective-permute-start | bytes 98312 | tf_op jit(solution)/shard_map/ppermute | solution.py:344
  14.7 4.4 %collective-permute-start.7 = (bf16[2,32,256]{2,1,0:T(8,128)(2,1)S(1)}, bf16[2,32,256]{2,1,0:T(8,128)(2,1)S(1)}, u32[]{:S(2)}, u32[]{:S(2)}) collective-permute-start(bf16[2,32,256]{2,1,0:T(8,128)(2,1)S(1)} %get-tuple-element.26), channel_id=1, source_target_pairs={{0,8},{4,12},{8,0},{12,4},{16,24},{20,28},{24,16},{28,20},{1,9},{5... | collective-permute-start | bytes 98312 | tf_op jit(solution)/shard_map/ppermute | solution.py:344

commit v9 on v8

--- a/solution.py
+++ b/solution.py
@@ -63,21 +63,25 @@
     )
 
 
-def own_kernel(
+def first_kernel(
     patches,
     here,
+    side,
     count_all,
     pattern_all,
     hx,
     value_all,
     rinv_all,
+    near_all,
     pert,
     weights,
     innov,
     own,
+    to_near,
     raw,
     count,
     pattern,
+    near_pattern,
     value,
     rinv,
     sems,
@@ -87,7 +91,7 @@
     smalls = [
         pltpu.make_async_copy(source, target, small.at[i])
         for i, (source, target) in enumerate(
-            ((count_all, count), (value_all, value), (rinv_all, rinv), (pattern_all, pattern))
+            ((count_all, count), (value_all, value), (rinv_all, rinv), (pattern_all, pattern), (near_all, near_pattern))
         )
     ]
     copies = [
@@ -113,6 +117,8 @@
     for patch in range(mine):
         row = here[0] * mine + patch
         own[patch] = share(pattern, row, 1, patches, pert, weights, innov)
+        part = share(near_pattern, row, side[0], patches, pert, weights, innov)
+        pack(part, to_near, patch)
 
 
 def pack(part, out, patch):
@@ -136,30 +142,19 @@
     out[patch, members:, :] = tail.astype(BF16)
 
 
-def far_kernel(patches, here, side, pattern, pert, weights, innov, out):
+def far_kernel(patches, here, side, pattern, pert, weights, innov, state, paired, out, *slabs):
+    span = slabs[0].shape[2]
+    length = len(slabs)
+    layer, place = here[0] // PAIR, here[0] % PAIR
+    for shift, slab in zip(turns(length), slabs):
+        target = (layer ^ shift) * PAIR + place
+        cols = pl.ds(pl.multiple_of(target * span, span), span)
+        slab[place] = state[:, cols]
+        slab[1 - place] = paired[:, cols]
     mine = out.shape[0]
     for patch in range(mine):
         row = here[0] * mine + patch
         pack(share(pattern, row, side[0], patches, pert, weights, innov), out, patch)
-
-
-def near_kernel(patches, here, side, pattern, pert, weights, innov, state, paired, sent, out, *rest):
-    slabs, sems = rest[:-1], rest[-1]
-    span = slabs[0].shape[2]
-    length = len(slabs)
-    layer, place = here[0] // PAIR, here[0] % PAIR
-    moves = []
-    for shift, slab in zip(turns(length), slabs):
-        target = (layer ^ shift) * PAIR + place
-        cols = pl.ds(pl.multiple_of(target * span, span), span)
-        moves.append((state.at[:, cols], slab.at[place]))
-        moves.append((paired.at[:, cols], slab.at[1 - place]))
-    moves = [pltpu.make_async_copy(*move, sems.at[i]) for i, move in enumerate(moves)]
-    for move in moves:
-        move.start()
-    far_kernel(patches, here, side, pattern, pert, weights, innov, out)
-    for move in moves:
-        move.wait()
 
 
 def total(value):
@@ -284,60 +279,58 @@
     assert mem_total & (mem_total - 1) == 0
 
     pattern = loc_pattern.T
+    near_pattern = lax.ppermute(pattern, "lon", near)
     far_pattern = lax.ppermute(pattern, "lon", far)
-    near_pattern = lax.ppermute(pattern, "lon", near)
     paired = lax.ppermute(state, "mem", swap)
     limit = pltpu.CompilerParams(vmem_limit_bytes=16 * 1024 * 1024)
     gram = 2 * padded * members * uses * width
-    pert, weights, innov, own = pl.pallas_call(
-        functools.partial(own_kernel, patches),
+    packed = shape((mine, padded, members // 2), BF16)
+    slab = shape((PAIR, local, span), BF16)
+    pert, weights, innov, own, to_near = pl.pallas_call(
+        functools.partial(first_kernel, patches),
         out_shape=(
             shape((blocks, members, width), BF16),
             shape((blocks, width), F32),
             shape((blocks, width), F32),
             shape((mine, padded, members), F32),
-        ),
-        in_specs=[SMEM] + [HBM] * 5,
-        out_specs=(VMEM,) * 4,
+            packed,
+        ),
+        in_specs=[SMEM] * 2 + [HBM] * 5 + [pl.BlockSpec(memory_space=pl.ANY)],
+        out_specs=(VMEM,) * 5,
         scratch_shapes=[
             pltpu.VMEM((blocks, members, width), BF16),
             pltpu.SMEM(obs_count.shape, jnp.int32),
             pltpu.SMEM(pattern.shape, jnp.int32),
+            pltpu.SMEM(pattern.shape, jnp.int32),
             pltpu.VMEM(obs_value.shape, F32),
             pltpu.VMEM(obs_rinv.shape, F32),
             pltpu.SemaphoreType.DMA((blocks // CHUNK,)),
-            pltpu.SemaphoreType.DMA((4,)),
+            pltpu.SemaphoreType.DMA((5,)),
         ],
         compiler_params=limit,
         cost_estimate=pl.CostEstimate(
-            flops=hx.size * 4 + mine * gram, bytes_accessed=2 * hx.size * 2, transcendentals=0
-        ),
-        name="own_share",
-    )(here, *(stay(value) for value in (obs_count, pattern, hx, obs_value, obs_rinv)))
-    packed = shape((mine, padded, members // 2), BF16)
-    slab = shape((PAIR, local, span), BF16)
-    cost = pl.CostEstimate(flops=mine * gram, bytes_accessed=hx.size, transcendentals=0)
-    to_far = pl.pallas_call(
+            flops=hx.size * 4 + 2 * mine * gram, bytes_accessed=4 * hx.size, transcendentals=0
+        ),
+        name="first_shares",
+    )(
+        here,
+        near_side,
+        *(stay(value) for value in (obs_count, pattern, hx, obs_value, obs_rinv)),
+        near_pattern,
+    )
+    to_far, *slabs = pl.pallas_call(
         functools.partial(far_kernel, patches),
-        out_shape=packed,
-        in_specs=[SMEM] * 3 + [VMEM] * 3,
-        out_specs=VMEM,
+        out_shape=(packed,) + (slab,) * length,
+        in_specs=[SMEM] * 3 + [VMEM] * 5,
+        out_specs=(VMEM,) * (1 + length),
         compiler_params=limit,
-        cost_estimate=cost,
+        cost_estimate=pl.CostEstimate(
+            flops=mine * gram, bytes_accessed=hx.size, transcendentals=0
+        ),
         name="far_share",
-    )(here, far_side, far_pattern, pert, weights, innov)
+    )(here, far_side, far_pattern, pert, weights, innov, state, paired)
     from_far = lax.ppermute(to_far, "lon", far)
-    to_near, *slabs = pl.pallas_call(
-        functools.partial(near_kernel, patches),
-        out_shape=(packed,) + (slab,) * length,
-        in_specs=[SMEM] * 3 + [VMEM] * 3 + [HBM] * 2 + [pl.BlockSpec(memory_space=pl.ANY)],
-        out_specs=(VMEM,) * (1 + length),
-        scratch_shapes=[pltpu.SemaphoreType.DMA((PAIR * length,))],
-        compiler_params=limit,
-        cost_estimate=cost,
-        name="near_share",
-    )(here, near_side, near_pattern, pert, weights, innov, state, paired, to_far)
-    from_near = lax.ppermute(to_near, "lon", near)
+    from_near = lax.ppermute(lax.optimization_barrier((to_near, to_far))[0], "lon", near)
     for i, shift in enumerate(turns(length)):
         if shift:
             trade = [(j, j ^ (shift * PAIR)) for j in range(mem_total)]
@@ -352,7 +345,7 @@
             flops=mine * 15 * 2 * members**3, bytes_accessed=2**20, transcendentals=0
         ),
         name="root",
-    )(own, from_far, from_near)
+    )(own, from_near, from_far)
     updated = pl.pallas_call(
         apply_kernel,
         out_shape=shape((members, span), BF16),

time: 31 us -> 31.9 us (1.029)
  blocking collectives: 10.4 us -> 11.8 us
  waiting for transfers between devices: 1.75 us -> 2.78 us
  Pallas kernels: 8.03 us -> 7.01 us
  starting transfers between devices: 9.86 us -> 9.42 us
    all_to_all x1, blocking collectives: 10.4 us -> 11.8 us  [body(): lax.all_to_all(updated.reshape(mem_total, local, span), 'mem', split_axis...]
    ppermute x1, waiting for transfers between devices: 0.01 us -> 1.27 us  [body(): from_far = lax.ppermute(to_far, 'lon', far)]
    ppermute x3, waiting for transfers between devices: 1.73 us -> 0.47 us  [body(): slabs[i] = lax.ppermute(slabs[i], 'mem', trade)]
    ppermute x1, waiting for transfers between devices: 0.01 us -> 1.03 us  [body(): near_pattern = lax.ppermute(pattern, 'lon', near)]
    pallas_call x3 -> x2, Pallas kernels: 4.98 us -> 3.96 us  [the longest x1 2.82 us: body(): pl.pallas_call(functools.partial(first_kernel, patches), out_shape=(shape...]
    ppermute x1, starting transfers between devices: 0.01 us -> 0.96 us  [body(): near_pattern = lax.ppermute(pattern, 'lon', near)]
    ppermute x1, starting transfers between devices: 1.63 us -> 0.68 us  [body(): far_pattern = lax.ppermute(pattern, 'lon', far)]
    ppermute x1, starting transfers between devices: 0.98 us -> 0.28 us  [body(): from_far = lax.ppermute(to_far, 'lon', far)]
  transfers between devices with their start and end apart: 8 -> 8, of which waited for: 1 -> 3; matrix products, arithmetic and copies ran while one was open for 0% -> 0% of each run, Pallas kernels for 24% -> 16%
where the time goes in v9:
time: 31.9 us; the launch traced here: 31.7 us
  blocking collectives  11.8 us (37%)
  starting transfers between devices  9.42 us (30%)
  Pallas kernels  7.01 us (22%)
  waiting for transfers between devices  2.78 us (9%)
  local copies, waits for them, and re-layouts  0.67 us (2%)
    all_to_all x1, blocking collectives, body(): lax.all_to_all(updated.reshape(mem_total, local, span), 'mem', split_axis...  11.8 us
    ppermute x3, starting transfers between devices, body(): slabs[i] = lax.ppermute(slabs[i], 'mem', trade)  4.16 us
    ppermute x1, starting transfers between devices, body(): paired = lax.ppermute(state, 'mem', swap)  2.94 us
    pallas_call x1, Pallas kernels, body(): pl.pallas_call(functools.partial(first_kernel, patches), out_shape=(shape...  2.82 us
    pallas_call x1, Pallas kernels, body(): pl.pallas_call(root_kernel, out_shape=(shape((mine, members, members), BF...  2.39 us
    ppermute x1, waiting for transfers between devices, body(): from_far = lax.ppermute(to_far, 'lon', far)  1.27 us
    pallas_call x1, Pallas kernels, body(): pl.pallas_call(functools.partial(far_kernel, patches), out_shape=(packed,...  1.14 us
    ppermute x1, waiting for transfers between devices, body(): near_pattern = lax.ppermute(pattern, 'lon', near)  1.03 us
  transfers between devices with their start and end apart: 8, of which 3 were waited for; matrix products, arithmetic and copies ran while one was open for 0% of the time, Pallas kernels for 16%

profile of v9, /device:TPU:0, one launch (start us, length us, event | category | flops | bytes accessed | tf_op | source)
XLA Modules:
  0.0 31.7 jit_solution(10348160471994540667)
XLA Ops:
  0.0 0.0 copy-start
  0.0 2.9 %collective-permute-start.2 = (bf16[32,2048]{1,0:T(8,128)(2,1)}, bf16[32,2048]{1,0:T(8,128)(2,1)S(1)}, u32[]{:S(2)}, u32[]{:S(2)}) collective-permute-start(bf16[32,2048]{1,0:T(8,128)(2,1)} %state.1), channel_id=1, source_target_pairs={{0,4},{4,0},{8,12},{12,8},{16,20},{20,16},{24,28},{28,24},{1,5},{5... | collective-permute-start | bytes 393224 | tf_op jit(solution)/shard_map/ppermute | solution.py:284
  2.9 0.7 %collective-permute-start.1 = (s32[8,16]{1,0:T(8,128)}, s32[8,16]{1,0:T(8,128)S(1)}, u32[]{:S(2)}, u32[]{:S(2)}) collective-permute-start(s32[8,16]{1,0:T(8,128)} %bitcast.10), channel_id=1, source_target_pairs={{0,3},{1,2},{2,1},{3,0},{4,7},{5,6},{6,5},{7,4},{8,11},{9,10},{10,... | collective-permute-start | bytes 1544 | tf_op jit(solution)/shard_map/ppermute | solution.py:283
  3.6 1.0 %collective-permute-start = (s32[8,16]{1,0:T(8,128)}, s32[8,16]{1,0:T(8,128)S(1)}, u32[]{:S(2)}, u32[]{:S(2)}) collective-permute-start(s32[8,16]{1,0:T(8,128)} %bitcast.11), channel_id=1, source_target_pairs={{0,1},{1,0},{2,3},{3,2},{4,5},{5,4},{6,7},{7,6},{8,9},{9,8},{10,11... | collective-permute-start | bytes 1544 | tf_op jit(solution)/shard_map/ppermute | solution.py:282
  4.6 1.0 %collective-permute-done.near_all = s32[8,16]{1,0:T(8,128)S(1)} collective-permute-done((s32[8,16]{1,0:T(8,128)}, s32[8,16]{1,0:T(8,128)S(1)}, u32[]{:S(2)}, u32[]{:S(2)}) %collective-permute-start) | collective-permute-done | bytes 544 | tf_op jit(solution)/shard_map/ppermute | solution.py:282
  5.6 2.8 %first_shares.1 = (bf16[32,256,128]{2,1,0:T(8,128)(2,1)S(1)}, f32[32,128]{1,0:T(8,128)S(1)}, f32[32,128]{1,0:T(8,128)S(1)}, f32[2,272,256]{2,1,0:T(8,128)S(1)}, bf16[2,272,128]{2,1,0:T(8,128)(2,1)S(1)}) custom-call(s32[1]{0:T(128)} %bitcast.here, s32[1]{0:T(128)} %bitcast.1.side, s32[32]{0:T(128)} %count_all.1, s32[8,16]{1,0:T(8,128)} %bitcast.12, ...), custom_call_target="tpu_custom_call" | custom-call | flops 574619648 | bytes 4194304 | tf_op jit(solution)/shard_map/first_shares/pallas_call | solution.py:289
  8.4 0.0 collective-permute-done.1.pattern
  8.4 0.0 collective-permute-done.2.paired
  8.5 0.0 copy-done
  8.5 1.1 %far_share.1 = (bf16[2,272,128]{2,1,0:T(8,128)(2,1)S(1)}, bf16[2,32,256]{2,1,0:T(8,128)(2,1)S(1)}, bf16[2,32,256]{2,1,0:T(8,128)(2,1)S(1)}, bf16[2,32,256]{2,1,0:T(8,128)(2,1)S(1)}, bf16[2,32,256]{2,1,0:T(8,128)(2,1)S(1)}) custom-call(s32[1]{0:T(128)} %bitcast.here, s32[1]{0:T(128)} %bitcast.3.side, s32[8,16]{1,0:T(8,128)S(1)} %collective-permute-done.1.pattern, ...), custom_call_target="tpu_custom_call" | custom-call | flops 285212672 | bytes 1048576 | tf_op jit(solution)/shard_map/far_share/pallas_call | solution.py:321
  9.6 0.4 %collective-permute-start.3 = (bf16[2,272,128]{2,1,0:T(8,128)(2,1)S(1)}, bf16[2,272,128]{2,1,0:T(8,128)(2,1)S(1)}, u32[]{:S(2)}, u32[]{:S(2)}) collective-permute-start(bf16[2,272,128]{2,1,0:T(8,128)(2,1)S(1)} %get-tuple-element.24), channel_id=1, source_target_pairs={{0,1},{1,0},{2,3},{3,2},{4,5},{5,4},{6,7},{7,6},{8,9},{9,8},{10,11... | collective-permute-start | bytes 417800 | tf_op jit(solution)/shard_map/ppermute | solution.py:333
  10.0 0.3 collective-permute-start.4
  10.3 2.6 %collective-permute-start.5 = (bf16[2,32,256]{2,1,0:T(8,128)(2,1)S(1)}, bf16[2,32,256]{2,1,0:T(8,128)(2,1)S(1)}, u32[]{:S(2)}, u32[]{:S(2)}) collective-permute-start(bf16[2,32,256]{2,1,0:T(8,128)(2,1)S(1)} %get-tuple-element.28), channel_id=1, source_target_pairs={{0,16},{4,20},{8,24},{12,28},{16,0},{20,4},{24,8},{28,12},{1,17},{... | collective-permute-start | bytes 98312 | tf_op jit(solution)/shard_map/ppermute | solution.py:337
  12.9 1.4 %collective-permute-start.6 = (bf16[2,32,256]{2,1,0:T(8,128)(2,1)S(1)}, bf16[2,32,256]{2,1,0:T(8,128)(2,1)S(1)}, u32[]{:S(2)}, u32[]{:S(2)}) collective-permute-start(bf16[2,32,256]{2,1,0:T(8,128)(2,1)S(1)} %get-tuple-element.29), channel_id=1, source_target_pairs={{0,24},{4,28},{8,16},{12,20},{16,8},{20,12},{24,0},{28,4},{1,25},{... | collective-permute-start | bytes 98312 | tf_op jit(solution)/shard_map/ppermute | solution.py:337
  14.2 0.2 collective-permute-start.7
  14.5 0.0 collective-permute-done.3.before
  14.5 1.3 %collective-permute-done.4.after = bf16[2,272,128]{2,1,0:T(8,128)(2,1)S(1)} collective-permute-done((bf16[2,272,128]{2,1,0:T(8,128)(2,1)S(1)}, bf16[2,272,128]{2,1,0:T(8,128)(2,1)S(1)}, u32[]{:S(2)}, u32[]{:S(2)}) %collective-permute-start.4) | collective-permute-done | bytes 139296 | tf_op jit(solution)/shard_map/ppermute | solution.py:332
  15.7 2.4 %root.1 = (bf16[2,256,256]{2,1,0:T(8,128)(2,1)S(1)}, f32[2,16,256]{2,1,0:T(8,128)S(1)}) custom-call(f32[2,272,256]{2,1,0:T(8,128)S(1)} %get-tuple-element.18.own, bf16[2,272,128]{2,1,0:T(8,128)(2,1)S(1)} %collective-permute-done.3.before, bf16[2,272,128]{2,1,0:T(8,128)(2,1)S(1)} %collective-permute-done.4.after), custom_call_target="tpu_custom_call" | custom-call | flops 1006632960 | bytes 1048576 | tf_op jit(solution)/shard_map/root/pallas_call | solution.py:338
  18.1 0.0 collective-permute-done.5.rest_1_
  18.1 0.5 %collective-permute-done.6.rest_2_ = bf16[2,32,256]{2,1,0:T(8,128)(2,1)S(1)} collective-permute-done((bf16[2,32,256]{2,1,0:T(8,128)(2,1)S(1)}, bf16[2,32,256]{2,1,0:T(8,128)(2,1)S(1)}, u32[]{:S(2)}, u32[]{:S(2)}) %collective-permute-start.6) | collective-permute-done | bytes 32800 | tf_op jit(solution)/shard_map/ppermute | solution.py:337
  18.6 0.0 collective-permute-done.7.rest_3_
  18.6 0.7 %apply.1 = bf16[256,256]{1,0:T(8,128)(2,1)S(1)} custom-call(s32[1]{0:T(128)} %bitcast.here, bf16[2,256,256]{2,1,0:T(8,128)(2,1)S(1)} %get-tuple-element.25.root, f32[2,16,256]{2,1,0:T(8,128)S(1)} %get-tuple-element.26.rows, bf16[2,32,256]{2,1,0:T(8,128)(2,1)S(1)} %get-tuple-element.27.rest_0_, bf16[2,32,256]{2,1,0:T(8,128)(2,1)S(1)} %collective-permute-done.5.rest_1_, ...), custom_call_target="tpu_custom_call" | custom-call | flops 33554432 | bytes 524288 | tf_op jit(solution)/shard_map/apply/pallas_call | solution.py:349
  19.3 11.8 %all_to_all.5 = bf16[8,32,256]{2,1,0:T(8,128)(2,1)S(1)} all-to-all(bf16[8,32,256]{2,1,0:T(8,128)(2,1)S(1)} %bitcast.8), channel_id=1, replica_groups=mesh['mem'=8,'lon'=4] {'mem'}, dimensions={0} | all-to-all | bytes 262144 | tf_op jit(solution)/shard_map/all_to_all | solution.py:361
  31.0 0.7 %copy.8 = bf16[8,4,8,256]{3,2,0,1:T(8,128)(2,1)} copy(bf16[8,4,8,256]{3,2,1,0:T(8,128)(2,1)S(1)} %bitcast.9) | data formatting | bytes 262144 | tf_op jit(solution)/shard_map/reshape | solution.py:364
Async XLA Ops:
  0.0 8.5 %copy-start = (bf16[32,2048]{1,0:T(8,128)(2,1)S(1)}, bf16[32,2048]{1,0:T(8,128)(2,1)}, u32[]{:S(2)}) copy-start(bf16[32,2048]{1,0:T(8,128)(2,1)} %state.1) | copy-start | bytes 393220
  0.0 8.4 %collective-permute-start.2 = (bf16[32,2048]{1,0:T(8,128)(2,1)}, bf16[32,2048]{1,0:T(8,128)(2,1)S(1)}, u32[]{:S(2)}, u32[]{:S(2)}) collective-permute-start(bf16[32,2048]{1,0:T(8,128)(2,1)} %state.1), channel_id=1, source_target_pairs={{0,4},{4,0},{8,12},{12,8},{16,20},{20,16},{24,28},{28,24},{1,5},{5... | collective-permute-start | bytes 393224 | tf_op jit(solution)/shard_map/ppermute | solution.py:284
  2.9 5.5 %collective-permute-start.1 = (s32[8,16]{1,0:T(8,128)}, s32[8,16]{1,0:T(8,128)S(1)}, u32[]{:S(2)}, u32[]{:S(2)}) collective-permute-start(s32[8,16]{1,0:T(8,128)} %bitcast.10), channel_id=1, source_target_pairs={{0,3},{1,2},{2,1},{3,0},{4,7},{5,6},{6,5},{7,4},{8,11},{9,10},{10,... | collective-permute-start | bytes 1544 | tf_op jit(solution)/shard_map/ppermute | solution.py:283
  3.6 2.0 %collective-permute-start = (s32[8,16]{1,0:T(8,128)}, s32[8,16]{1,0:T(8,128)S(1)}, u32[]{:S(2)}, u32[]{:S(2)}) collective-permute-start(s32[8,16]{1,0:T(8,128)} %bitcast.11), channel_id=1, source_target_pairs={{0,1},{1,0},{2,3},{3,2},{4,5},{5,4},{6,7},{7,6},{8,9},{9,8},{10,11... | collective-permute-start | bytes 1544 | tf_op jit(solution)/shard_map/ppermute | solution.py:282
  9.6 4.9 %collective-permute-start.3 = (bf16[2,272,128]{2,1,0:T(8,128)(2,1)S(1)}, bf16[2,272,128]{2,1,0:T(8,128)(2,1)S(1)}, u32[]{:S(2)}, u32[]{:S(2)}) collective-permute-start(bf16[2,272,128]{2,1,0:T(8,128)(2,1)S(1)} %get-tuple-element.24), channel_id=1, source_target_pairs={{0,1},{1,0},{2,3},{3,2},{4,5},{5,4},{6,7},{7,6},{8,9},{9,8},{10,11... | collective-permute-start | bytes 417800 | tf_op jit(solution)/shard_map/ppermute | solution.py:333
  10.0 5.7 %collective-permute-start.4 = (bf16[2,272,128]{2,1,0:T(8,128)(2,1)S(1)}, bf16[2,272,128]{2,1,0:T(8,128)(2,1)S(1)}, u32[]{:S(2)}, u32[]{:S(2)}) collective-permute-start(bf16[2,272,128]{2,1,0:T(8,128)(2,1)S(1)} %get-tuple-element.23), channel_id=1, source_target_pairs={{0,3},{1,2},{2,1},{3,0},{4,7},{5,6},{6,5},{7,4},{8,11},{9,10},{10,... | collective-permute-start | bytes 417800 | tf_op jit(solution)/shard_map/ppermute | solution.py:332
  10.3 7.8 %collective-permute-start.5 = (bf16[2,32,256]{2,1,0:T(8,128)(2,1)S(1)}, bf16[2,32,256]{2,1,0:T(8,128)(2,1)S(1)}, u32[]{:S(2)}, u32[]{:S(2)}) collective-permute-start(bf16[2,32,256]{2,1,0:T(8,128)(2,1)S(1)} %get-tuple-element.28), channel_id=1, source_target_pairs={{0,16},{4,20},{8,24},{12,28},{16,0},{20,4},{24,8},{28,12},{1,17},{... | collective-permute-start | bytes 98312 | tf_op jit(solution)/shard_map/ppermute | solution.py:337
  12.9 5.7 %collective-permute-start.6 = (bf16[2,32,256]{2,1,0:T(8,128)(2,1)S(1)}, bf16[2,32,256]{2,1,0:T(8,128)(2,1)S(1)}, u32[]{:S(2)}, u32[]{:S(2)}) collective-permute-start(bf16[2,32,256]{2,1,0:T(8,128)(2,1)S(1)} %get-tuple-element.29), channel_id=1, source_target_pairs={{0,24},{4,28},{8,16},{12,20},{16,8},{20,12},{24,0},{28,4},{1,25},{... | collective-permute-start | bytes 98312 | tf_op jit(solution)/shard_map/ppermute | solution.py:337
  14.2 4.4 %collective-permute-start.7 = (bf16[2,32,256]{2,1,0:T(8,128)(2,1)S(1)}, bf16[2,32,256]{2,1,0:T(8,128)(2,1)S(1)}, u32[]{:S(2)}, u32[]{:S(2)}) collective-permute-start(bf16[2,32,256]{2,1,0:T(8,128)(2,1)S(1)} %get-tuple-element.30), channel_id=1, source_target_pairs={{0,8},{4,12},{8,0},{12,4},{16,24},{20,28},{24,16},{28,20},{1,9},{5... | collective-permute-start | bytes 98312 | tf_op jit(solution)/shard_map/ppermute | solution.py:337

commit v10 on v8

--- a/solution.py
+++ b/solution.py
@@ -71,10 +71,12 @@
     hx,
     value_all,
     rinv_all,
+    state,
     pert,
     weights,
     innov,
     own,
+    half,
     raw,
     count,
     pattern,
@@ -82,6 +84,7 @@
     rinv,
     sems,
     small,
+    cut,
 ):
     blocks, members, width = raw.shape
     smalls = [
@@ -94,7 +97,13 @@
         pltpu.make_async_copy(hx.at[pl.ds(i, CHUNK)], raw.at[pl.ds(i, CHUNK)], sems.at[i // CHUNK])
         for i in range(0, blocks, CHUNK)
     ]
-    for copy in smalls + copies:
+    length, _, span = half.shape
+    cuts = []
+    for layer in range(length):
+        start = (layer * PAIR + 1 - here[0] % PAIR) * span
+        cols = pl.ds(pl.multiple_of(start, span), span)
+        cuts.append(pltpu.make_async_copy(state.at[:, cols], half.at[layer], cut.at[layer]))
+    for copy in smalls + copies + cuts:
         copy.start()
     for copy in smalls:
         copy.wait()
@@ -113,6 +122,8 @@
     for patch in range(mine):
         row = here[0] * mine + patch
         own[patch] = share(pattern, row, 1, patches, pert, weights, innov)
+    for copy in cuts:
+        copy.wait()
 
 
 def pack(part, out, patch):
@@ -143,23 +154,16 @@
         pack(share(pattern, row, side[0], patches, pert, weights, innov), out, patch)
 
 
-def near_kernel(patches, here, side, pattern, pert, weights, innov, state, paired, sent, out, *rest):
-    slabs, sems = rest[:-1], rest[-1]
+def near_kernel(patches, here, side, pattern, pert, weights, innov, state, paired, sent, out, *slabs):
     span = slabs[0].shape[2]
     length = len(slabs)
     layer, place = here[0] // PAIR, here[0] % PAIR
-    moves = []
     for shift, slab in zip(turns(length), slabs):
-        target = (layer ^ shift) * PAIR + place
-        cols = pl.ds(pl.multiple_of(target * span, span), span)
-        moves.append((state.at[:, cols], slab.at[place]))
-        moves.append((paired.at[:, cols], slab.at[1 - place]))
-    moves = [pltpu.make_async_copy(*move, sems.at[i]) for i, move in enumerate(moves)]
-    for move in moves:
-        move.start()
+        target = layer ^ shift
+        start = (target * PAIR + place) * span
+        slab[place] = state[:, pl.ds(pl.multiple_of(start, span), span)]
+        slab[1 - place] = paired[target]
     far_kernel(patches, here, side, pattern, pert, weights, innov, out)
-    for move in moves:
-        move.wait()
 
 
 def total(value):
@@ -286,19 +290,19 @@
     pattern = loc_pattern.T
     far_pattern = lax.ppermute(pattern, "lon", far)
     near_pattern = lax.ppermute(pattern, "lon", near)
-    paired = lax.ppermute(state, "mem", swap)
     limit = pltpu.CompilerParams(vmem_limit_bytes=16 * 1024 * 1024)
     gram = 2 * padded * members * uses * width
-    pert, weights, innov, own = pl.pallas_call(
+    pert, weights, innov, own, given = pl.pallas_call(
         functools.partial(own_kernel, patches),
         out_shape=(
             shape((blocks, members, width), BF16),
             shape((blocks, width), F32),
             shape((blocks, width), F32),
             shape((mine, padded, members), F32),
+            shape((length, local, span), BF16),
         ),
-        in_specs=[SMEM] + [HBM] * 5,
-        out_specs=(VMEM,) * 4,
+        in_specs=[SMEM] + [HBM] * 6,
+        out_specs=(VMEM,) * 5,
         scratch_shapes=[
             pltpu.VMEM((blocks, members, width), BF16),
             pltpu.SMEM(obs_count.shape, jnp.int32),
@@ -307,13 +311,16 @@
             pltpu.VMEM(obs_rinv.shape, F32),
             pltpu.SemaphoreType.DMA((blocks // CHUNK,)),
             pltpu.SemaphoreType.DMA((4,)),
+            pltpu.SemaphoreType.DMA((length,)),
         ],
         compiler_params=limit,
         cost_estimate=pl.CostEstimate(
             flops=hx.size * 4 + mine * gram, bytes_accessed=2 * hx.size * 2, transcendentals=0
         ),
         name="own_share",
-    )(here, *(stay(value) for value in (obs_count, pattern, hx, obs_value, obs_rinv)))
+    )(here, *(stay(value) for value in (obs_count, pattern, hx, obs_value, obs_rinv, state)))
+    given, far_pattern, near_pattern = lax.optimization_barrier((given, far_pattern, near_pattern))
+    paired = lax.ppermute(given, "mem", swap)
     packed = shape((mine, padded, members // 2), BF16)
     slab = shape((PAIR, local, span), BF16)
     cost = pl.CostEstimate(flops=mine * gram, bytes_accessed=hx.size, transcendentals=0)
@@ -330,9 +337,8 @@
     to_near, *slabs = pl.pallas_call(
         functools.partial(near_kernel, patches),
         out_shape=(packed,) + (slab,) * length,
-        in_specs=[SMEM] * 3 + [VMEM] * 3 + [HBM] * 2 + [pl.BlockSpec(memory_space=pl.ANY)],
+        in_specs=[SMEM] * 3 + [VMEM] * 5 + [pl.BlockSpec(memory_space=pl.ANY)],
         out_specs=(VMEM,) * (1 + length),
-        scratch_shapes=[pltpu.SemaphoreType.DMA((PAIR * length,))],
         compiler_params=limit,
         cost_estimate=cost,
         name="near_share",

time: 31 us -> 32.6 us (1.052)
  waiting for transfers between devices: 1.75 us -> 3.12 us
  blocking collectives: 10.4 us -> 11.4 us
  starting transfers between devices: 9.86 us -> 9.22 us
    ppermute x1, starting transfers between devices: 2.94 us -> 1.55 us  [body(): paired = lax.ppermute(given, 'mem', swap)]
    ppermute x1, waiting for transfers between devices: 0.01 us -> 1.37 us  [body(): paired = lax.ppermute(given, 'mem', swap)]
    ppermute x1, starting transfers between devices: 1.63 us -> 2.63 us  [body(): far_pattern = lax.ppermute(pattern, 'lon', far)]
    all_to_all x1, blocking collectives: 10.4 us -> 11.4 us  [body(): lax.all_to_all(updated.reshape(mem_total, local, span), 'mem', split_axis...]
    ppermute x1, starting transfers between devices: 0.98 us -> 0.28 us  [body(): from_far = lax.ppermute(to_far, 'lon', far)]
    ppermute x1, starting transfers between devices: 0.01 us -> 0.45 us  [body(): near_pattern = lax.ppermute(pattern, 'lon', near)]
  transfers between devices with their start and end apart: 8 -> 8, of which waited for: 1 -> 2; matrix products, arithmetic and copies ran while one was open for 0% -> 0% of each run, Pallas kernels for 24% -> 22%
where the time goes in v10:
time: 32.6 us; the launch traced here: 32.4 us
  blocking collectives  11.4 us (35%)
  starting transfers between devices  9.22 us (28%)
  Pallas kernels  7.95 us (24%)
  waiting for transfers between devices  3.12 us (10%)
  local copies, waits for them, and re-layouts  0.67 us (2%)
    all_to_all x1, blocking collectives, body(): lax.all_to_all(updated.reshape(mem_total, local, span), 'mem', split_axis...  11.4 us
    ppermute x3, starting transfers between devices, body(): slabs[i] = lax.ppermute(slabs[i], 'mem', trade)  4.23 us
    pallas_call x1, Pallas kernels, body(): pl.pallas_call(functools.partial(own_kernel, patches), out_shape=(shape((...  2.65 us
    ppermute x1, starting transfers between devices, body(): far_pattern = lax.ppermute(pattern, 'lon', far)  2.63 us
    pallas_call x1, Pallas kernels, body(): pl.pallas_call(root_kernel, out_shape=(shape((mine, members, members), BF...  2.39 us
    ppermute x3, waiting for transfers between devices, body(): slabs[i] = lax.ppermute(slabs[i], 'mem', trade)  1.73 us
    ppermute x1, starting transfers between devices, body(): paired = lax.ppermute(given, 'mem', swap)  1.55 us
    ppermute x1, waiting for transfers between devices, body(): paired = lax.ppermute(given, 'mem', swap)  1.37 us
  transfers between devices with their start and end apart: 8, of which 2 were waited for; matrix products, arithmetic and copies ran while one was open for 0% of the time, Pallas kernels for 22%

profile of v10, /device:TPU:0, one launch (start us, length us, event | category | flops | bytes accessed | tf_op | source)
XLA Modules:
  0.0 32.4 jit_solution(2146144419734253960)
XLA Ops:
  0.0 0.5 %collective-permute-start.1 = (s32[8,16]{1,0:T(8,128)}, s32[8,16]{1,0:T(8,128)S(1)}, u32[]{:S(2)}, u32[]{:S(2)}) collective-permute-start(s32[8,16]{1,0:T(8,128)} %bitcast.10), channel_id=1, source_target_pairs={{0,1},{1,0},{2,3},{3,2},{4,5},{5,4},{6,7},{7,6},{8,9},{9,8},{10,11... | collective-permute-start | bytes 1544 | tf_op jit(solution)/shard_map/ppermute | solution.py:292
  0.5 2.6 %collective-permute-start = (s32[8,16]{1,0:T(8,128)}, s32[8,16]{1,0:T(8,128)S(1)}, u32[]{:S(2)}, u32[]{:S(2)}) collective-permute-start(s32[8,16]{1,0:T(8,128)} %bitcast.11), channel_id=1, source_target_pairs={{0,3},{1,2},{2,1},{3,0},{4,7},{5,6},{6,5},{7,4},{8,11},{9,10},{10,... | collective-permute-start | bytes 1544 | tf_op jit(solution)/shard_map/ppermute | solution.py:291
  3.1 0.0 copy-start
  3.1 2.7 %own_share.1 = (bf16[32,256,128]{2,1,0:T(8,128)(2,1)S(1)}, f32[32,128]{1,0:T(8,128)S(1)}, f32[32,128]{1,0:T(8,128)S(1)}, f32[2,272,256]{2,1,0:T(8,128)S(1)}, bf16[4,32,256]{2,1,0:T(8,128)(2,1)S(1)}) custom-call(s32[1]{0:T(128)} %bitcast.here, s32[32]{0:T(128)} %count_all.1, s32[8,16]{1,0:T(8,128)} %bitcast.12, bf16[32,256,128]{2,1,0:T(8,128)(2,1)} %hx.1, ...), custom_call_target="tpu_custom_call" | custom-call | flops 289406976 | bytes 4194304 | tf_op jit(solution)/shard_map/own_share/pallas_call | solution.py:295
  5.7 0.0 collective-permute-done.1.pattern
  5.8 0.0 collective-permute-done.pattern
  5.8 1.6 %collective-permute-start.3 = (bf16[4,32,256]{2,1,0:T(8,128)(2,1)S(1)}, bf16[4,32,256]{2,1,0:T(8,128)(2,1)S(1)}, u32[]{:S(2)}, u32[]{:S(2)}) collective-permute-start(bf16[4,32,256]{2,1,0:T(8,128)(2,1)S(1)} %get-tuple-element.27), channel_id=1, source_target_pairs={{0,4},{4,0},{8,12},{12,8},{16,20},{20,16},{24,28},{28,24},{1,5},{5... | collective-permute-start | bytes 196616 | tf_op jit(solution)/shard_map/ppermute | solution.py:323
  7.3 1.1 %far_share.1.sent = bf16[2,272,128]{2,1,0:T(8,128)(2,1)S(1)} custom-call(s32[1]{0:T(128)} %bitcast.here, s32[1]{0:T(128)} %bitcast.2.side, s32[8,16]{1,0:T(8,128)S(1)} %collective-permute-done.pattern, bf16[32,256,128]{2,1,0:T(8,128)(2,1)S(1)} %get-tuple-element.23.pert, f32[32,128]{1,0:T(8,128)S(1)} %get-tuple-element.24.weights, ...), custom_call_target="tpu_custom_call" | custom-call | flops 285212672 | bytes 1048576 | tf_op jit(solution)/shard_map/far_share/pallas_call | solution.py:327
  8.4 0.3 collective-permute-start.2
  8.7 1.4 %collective-permute-done.3.paired = bf16[4,32,256]{2,1,0:T(8,128)(2,1)S(1)} collective-permute-done((bf16[4,32,256]{2,1,0:T(8,128)(2,1)S(1)}, bf16[4,32,256]{2,1,0:T(8,128)(2,1)S(1)}, u32[]{:S(2)}, u32[]{:S(2)}) %collective-permute-start.3) | collective-permute-done | bytes 65568 | tf_op jit(solution)/shard_map/ppermute | solution.py:323
  10.1 0.0 copy-done
  10.1 1.1 %near_share.1 = (bf16[2,272,128]{2,1,0:T(8,128)(2,1)S(1)}, bf16[2,32,256]{2,1,0:T(8,128)(2,1)S(1)}, bf16[2,32,256]{2,1,0:T(8,128)(2,1)S(1)}, bf16[2,32,256]{2,1,0:T(8,128)(2,1)S(1)}, bf16[2,32,256]{2,1,0:T(8,128)(2,1)S(1)}) custom-call(s32[1]{0:T(128)} %bitcast.here, s32[1]{0:T(128)} %bitcast.3.side, s32[8,16]{1,0:T(8,128)S(1)} %collective-permute-done.1.pattern, ...), custom_call_target="tpu_custom_call" | custom-call | flops 285212672 | bytes 1048576 | tf_op jit(solution)/shard_map/near_share/pallas_call | solution.py:337
  11.2 0.1 collective-permute-start.4
  11.3 2.6 %collective-permute-start.5 = (bf16[2,32,256]{2,1,0:T(8,128)(2,1)S(1)}, bf16[2,32,256]{2,1,0:T(8,128)(2,1)S(1)}, u32[]{:S(2)}, u32[]{:S(2)}) collective-permute-start(bf16[2,32,256]{2,1,0:T(8,128)(2,1)S(1)} %get-tuple-element.32), channel_id=1, source_target_pairs={{0,16},{4,20},{8,24},{12,28},{16,0},{20,4},{24,8},{28,12},{1,17},{... | collective-permute-start | bytes 98312 | tf_op jit(solution)/shard_map/ppermute | solution.py:350
  14.0 1.4 %collective-permute-start.6 = (bf16[2,32,256]{2,1,0:T(8,128)(2,1)S(1)}, bf16[2,32,256]{2,1,0:T(8,128)(2,1)S(1)}, u32[]{:S(2)}, u32[]{:S(2)}) collective-permute-start(bf16[2,32,256]{2,1,0:T(8,128)(2,1)S(1)} %get-tuple-element.33), channel_id=1, source_target_pairs={{0,24},{4,28},{8,16},{12,20},{16,8},{20,12},{24,0},{28,4},{1,25},{... | collective-permute-start | bytes 98312 | tf_op jit(solution)/shard_map/ppermute | solution.py:350
  15.3 0.2 collective-permute-start.7
  15.5 0.0 collective-permute-done.2.before
  15.6 0.0 collective-permute-done.4.after
  15.6 2.4 %root.1 = (bf16[2,256,256]{2,1,0:T(8,128)(2,1)S(1)}, f32[2,16,256]{2,1,0:T(8,128)S(1)}) custom-call(f32[2,272,256]{2,1,0:T(8,128)S(1)} %get-tuple-element.20.own, bf16[2,272,128]{2,1,0:T(8,128)(2,1)S(1)} %collective-permute-done.2.before, bf16[2,272,128]{2,1,0:T(8,128)(2,1)S(1)} %collective-permute-done.4.after), custom_call_target="tpu_custom_call" | custom-call | flops 1006632960 | bytes 1048576 | tf_op jit(solution)/shard_map/root/pallas_call | solution.py:351
  17.9 0.0 collective-permute-done.5.rest_1_
  17.9 1.7 %collective-permute-done.6.rest_2_ = bf16[2,32,256]{2,1,0:T(8,128)(2,1)S(1)} collective-permute-done((bf16[2,32,256]{2,1,0:T(8,128)(2,1)S(1)}, bf16[2,32,256]{2,1,0:T(8,128)(2,1)S(1)}, u32[]{:S(2)}, u32[]{:S(2)}) %collective-permute-start.6) | collective-permute-done | bytes 32800 | tf_op jit(solution)/shard_map/ppermute | solution.py:350
  19.7 0.0 collective-permute-done.7.rest_3_
  19.7 0.7 %apply.1 = bf16[256,256]{1,0:T(8,128)(2,1)S(1)} custom-call(s32[1]{0:T(128)} %bitcast.here, bf16[2,256,256]{2,1,0:T(8,128)(2,1)S(1)} %get-tuple-element.29.root, f32[2,16,256]{2,1,0:T(8,128)S(1)} %get-tuple-element.30.rows, bf16[2,32,256]{2,1,0:T(8,128)(2,1)S(1)} %get-tuple-element.31.rest_0_, bf16[2,32,256]{2,1,0:T(8,128)(2,1)S(1)} %collective-permute-done.5.rest_1_, ...), custom_call_target="tpu_custom_call" | custom-call | flops 33554432 | bytes 524288 | tf_op jit(solution)/shard_map/apply/pallas_call | solution.py:362
  20.4 11.4 %all_to_all.5 = bf16[8,32,256]{2,1,0:T(8,128)(2,1)S(1)} all-to-all(bf16[8,32,256]{2,1,0:T(8,128)(2,1)S(1)} %bitcast.8), channel_id=1, replica_groups=mesh['mem'=8,'lon'=4] {'mem'}, dimensions={0} | all-to-all | bytes 262144 | tf_op jit(solution)/shard_map/all_to_all | solution.py:374
  31.7 0.7 %copy.8 = bf16[8,4,8,256]{3,2,0,1:T(8,128)(2,1)} copy(bf16[8,4,8,256]{3,2,1,0:T(8,128)(2,1)S(1)} %bitcast.9) | data formatting | bytes 262144 | tf_op jit(solution)/shard_map/reshape | solution.py:377
Async XLA Ops:
  0.0 5.7 %collective-permute-start.1 = (s32[8,16]{1,0:T(8,128)}, s32[8,16]{1,0:T(8,128)S(1)}, u32[]{:S(2)}, u32[]{:S(2)}) collective-permute-start(s32[8,16]{1,0:T(8,128)} %bitcast.10), channel_id=1, source_target_pairs={{0,1},{1,0},{2,3},{3,2},{4,5},{5,4},{6,7},{7,6},{8,9},{9,8},{10,11... | collective-permute-start | bytes 1544 | tf_op jit(solution)/shard_map/ppermute | solution.py:292
  0.5 5.3 %collective-permute-start = (s32[8,16]{1,0:T(8,128)}, s32[8,16]{1,0:T(8,128)S(1)}, u32[]{:S(2)}, u32[]{:S(2)}) collective-permute-start(s32[8,16]{1,0:T(8,128)} %bitcast.11), channel_id=1, source_target_pairs={{0,3},{1,2},{2,1},{3,0},{4,7},{5,6},{6,5},{7,4},{8,11},{9,10},{10,... | collective-permute-start | bytes 1544 | tf_op jit(solution)/shard_map/ppermute | solution.py:291
  3.1 7.0 %copy-start = (bf16[32,2048]{1,0:T(8,128)(2,1)S(1)}, bf16[32,2048]{1,0:T(8,128)(2,1)}, u32[]{:S(2)}) copy-start(bf16[32,2048]{1,0:T(8,128)(2,1)} %state.3) | copy-start | bytes 393220
  5.8 4.3 %collective-permute-start.3 = (bf16[4,32,256]{2,1,0:T(8,128)(2,1)S(1)}, bf16[4,32,256]{2,1,0:T(8,128)(2,1)S(1)}, u32[]{:S(2)}, u32[]{:S(2)}) collective-permute-start(bf16[4,32,256]{2,1,0:T(8,128)(2,1)S(1)} %get-tuple-element.27), channel_id=1, source_target_pairs={{0,4},{4,0},{8,12},{12,8},{16,20},{20,16},{24,28},{28,24},{1,5},{5... | collective-permute-start | bytes 196616 | tf_op jit(solution)/shard_map/ppermute | solution.py:323
  8.4 7.1 %collective-permute-start.2 = (bf16[2,272,128]{2,1,0:T(8,128)(2,1)S(1)}, bf16[2,272,128]{2,1,0:T(8,128)(2,1)S(1)}, u32[]{:S(2)}, u32[]{:S(2)}) collective-permute-start(bf16[2,272,128]{2,1,0:T(8,128)(2,1)S(1)} %far_share.1.sent), channel_id=1, source_target_pairs={{0,3},{1,2},{2,1},{3,0},{4,7},{5,6},{6,5},{7,4},{8,11},{9,10},{10,... | collective-permute-start | bytes 417800 | tf_op jit(solution)/shard_map/ppermute | solution.py:336
  11.2 4.3 %collective-permute-start.4 = (bf16[2,272,128]{2,1,0:T(8,128)(2,1)S(1)}, bf16[2,272,128]{2,1,0:T(8,128)(2,1)S(1)}, u32[]{:S(2)}, u32[]{:S(2)}) collective-permute-start(bf16[2,272,128]{2,1,0:T(8,128)(2,1)S(1)} %get-tuple-element.28), channel_id=1, source_target_pairs={{0,1},{1,0},{2,3},{3,2},{4,5},{5,4},{6,7},{7,6},{8,9},{9,8},{10,11... | collective-permute-start | bytes 417800 | tf_op jit(solution)/shard_map/ppermute | solution.py:346
  11.3 6.6 %collective-permute-start.5 = (bf16[2,32,256]{2,1,0:T(8,128)(2,1)S(1)}, bf16[2,32,256]{2,1,0:T(8,128)(2,1)S(1)}, u32[]{:S(2)}, u32[]{:S(2)}) collective-permute-start(bf16[2,32,256]{2,1,0:T(8,128)(2,1)S(1)} %get-tuple-element.32), channel_id=1, source_target_pairs={{0,16},{4,20},{8,24},{12,28},{16,0},{20,4},{24,8},{28,12},{1,17},{... | collective-permute-start | bytes 98312 | tf_op jit(solution)/shard_map/ppermute | solution.py:350
  14.0 5.7 %collective-permute-start.6 = (bf16[2,32,256]{2,1,0:T(8,128)(2,1)S(1)}, bf16[2,32,256]{2,1,0:T(8,128)(2,1)S(1)}, u32[]{:S(2)}, u32[]{:S(2)}) collective-permute-start(bf16[2,32,256]{2,1,0:T(8,128)(2,1)S(1)} %get-tuple-element.33), channel_id=1, source_target_pairs={{0,24},{4,28},{8,16},{12,20},{16,8},{20,12},{24,0},{28,4},{1,25},{... | collective-permute-start | bytes 98312 | tf_op jit(solution)/shard_map/ppermute | solution.py:350
  15.3 4.4 %collective-permute-start.7 = (bf16[2,32,256]{2,1,0:T(8,128)(2,1)S(1)}, bf16[2,32,256]{2,1,0:T(8,128)(2,1)S(1)}, u32[]{:S(2)}, u32[]{:S(2)}) collective-permute-start(bf16[2,32,256]{2,1,0:T(8,128)(2,1)S(1)} %get-tuple-element.34), channel_id=1, source_target_pairs={{0,8},{4,12},{8,0},{12,4},{16,24},{20,28},{24,16},{28,20},{1,9},{5... | collective-permute-start | bytes 98312 | tf_op jit(solution)/shard_map/ppermute | solution.py:350

commit v11 on v5

--- a/solution.py
+++ b/solution.py
@@ -17,6 +17,10 @@
 VMEM = pl.BlockSpec(memory_space=pltpu.VMEM)
 SMEM = pl.BlockSpec(memory_space=pltpu.SMEM)
 HBM = pl.BlockSpec(memory_space=pltpu.HBM)
+
+
+def turns(length):
+    return [0, *range(2, length), 1][:length]
 
 
 def stay(value):
@@ -118,30 +122,38 @@
     out[patch, members:, :] = tail.astype(BF16)
 
 
-def far_kernel(patches, here, side, pattern, pert, weights, innov, out):
-    mine = out.shape[0]
-    for patch in range(mine):
-        row = here[0] * mine + patch
-        pack(share(pattern, row, side[0], patches, pert, weights, innov), out, patch)
-
-
-def near_kernel(patches, here, side, pattern, pert, weights, innov, state, paired, sent, out, *rest):
-    slabs, sems = rest[:-1], rest[-1]
+def neighbour_kernel(
+    patches,
+    here,
+    far_side,
+    near_side,
+    far_pattern,
+    near_pattern,
+    pert,
+    weights,
+    innov,
+    state,
+    paired,
+    to_far,
+    to_near,
+    *slabs,
+):
     span = slabs[0].shape[2]
     length = len(slabs)
     layer, place = here[0] // PAIR, here[0] % PAIR
-    moves = []
-    for shift, slab in enumerate(slabs):
+    for shift, slab in zip(turns(length), slabs):
         target = (layer ^ shift) * PAIR + place
         cols = pl.ds(pl.multiple_of(target * span, span), span)
-        moves.append((state.at[:, cols], slab.at[place]))
-        moves.append((paired.at[:, cols], slab.at[1 - place]))
-    moves = [pltpu.make_async_copy(*move, sems.at[i]) for i, move in enumerate(moves)]
-    for move in moves:
-        move.start()
-    far_kernel(patches, here, side, pattern, pert, weights, innov, out)
-    for move in moves:
-        move.wait()
+        slab[place] = state[:, cols]
+        slab[1 - place] = paired[:, cols]
+    mine = to_far.shape[0]
+    for pattern, side, out in (
+        (far_pattern, far_side, to_far),
+        (near_pattern, near_side, to_near),
+    ):
+        for patch in range(mine):
+            row = here[0] * mine + patch
+            pack(share(pattern, row, side[0], patches, pert, weights, innov), out, patch)
 
 
 def total(value):
@@ -182,15 +194,16 @@
             axis=0,
         )
         grams = own[patch, :members, :] + far
-        trace = total(jnp.where(diagonal, grams, 0.0))
+        blocks = grams[:half, :half] + grams[half:, half:]
+        trace = total(jnp.where(above == across, blocks, 0.0))
         norm = jnp.sqrt(total(grams * grams) + 2.0 * base * trace + base * base * members)
         scale.append(norm)
         forcing.append(force + own[patch, members : members + 1, :])
         factor.append(1.5 - 0.5 * (trace / members + base) / norm)
         level = trace / members
         rest.append((grams - jnp.where(diagonal, level, 0.0)) * (-0.5 / norm))
-    lead, tail = list(factor), list(rest)
     small = [rest[p].astype(BF16) for p in each]
+    lead, tail = list(factor), list(small)
     squares = [dot(small[p], small[p]) for p in each]
     for step in range(1, ITERS):
         cubes = [dot(squares[p].astype(BF16), small[p]) for p in each]
@@ -202,16 +215,16 @@
             factor[p] = 1.5 - 1.5 * f * f + f * f * f
             small[p] = rest[p].astype(BF16)
         for p in each:
-            narrow = tail[p].astype(BF16)
+            narrow = tail[p]
             if step < ITERS - 1:
                 both = dot(jnp.concatenate([small[p], narrow], axis=0), small[p])
                 squares[p], cross = both[:members], both[members:]
             else:
                 cross = dot(narrow, small[p])
-            tail[p] = factor[p] * tail[p] + lead[p] * rest[p] + cross
+            tail[p] = (factor[p] * narrow.astype(F32) + lead[p] * rest[p] + cross).astype(BF16)
             lead[p] = factor[p] * lead[p]
     for p in each:
-        high = tail[p].astype(BF16)
+        high = tail[p]
         root_out[p] = high
         force = jnp.broadcast_to(forcing[p], (PAD, members))
         gain = (lead[p] * force + dot(force.astype(BF16), high)) / scale[p]
@@ -226,7 +239,7 @@
     points = out.shape[1] // mine
     length = len(slabs)
     _, local, _ = slabs[0].shape
-    for shift, slab in enumerate(slabs):
+    for shift, slab in zip(turns(length), slabs):
         source = (here[0] // PAIR) ^ shift
         for i in range(PAIR):
             place = pl.ds(pl.multiple_of((source * PAIR + i) * local, local), local)
@@ -296,26 +309,16 @@
     packed = shape((mine, padded, members // 2), BF16)
     slab = shape((PAIR, local, span), BF16)
     cost = pl.CostEstimate(flops=mine * gram, bytes_accessed=hx.size, transcendentals=0)
-    to_far = pl.pallas_call(
-        functools.partial(far_kernel, patches),
-        out_shape=packed,
-        in_specs=[SMEM] * 3 + [VMEM] * 3,
-        out_specs=VMEM,
+    to_far, to_near, *slabs = pl.pallas_call(
+        functools.partial(neighbour_kernel, patches),
+        out_shape=(packed,) * 2 + (slab,) * length,
+        in_specs=[SMEM] * 5 + [VMEM] * 5,
+        out_specs=(VMEM,) * (2 + length),
         compiler_params=limit,
         cost_estimate=cost,
-        name="far_share",
-    )(here, far_side, far_pattern, pert, weights, innov)
+        name="neighbour_shares",
+    )(here, far_side, near_side, far_pattern, near_pattern, pert, weights, innov, state, paired)
     from_far = lax.ppermute(to_far, "lon", far)
-    to_near, *slabs = pl.pallas_call(
-        functools.partial(near_kernel, patches),
-        out_shape=(packed,) + (slab,) * length,
-        in_specs=[SMEM] * 3 + [VMEM] * 3 + [HBM] * 2 + [pl.BlockSpec(memory_space=pl.ANY)],
-        out_specs=(VMEM,) * (1 + length),
-        scratch_shapes=[pltpu.SemaphoreType.DMA((PAIR * length,))],
-        compiler_params=limit,
-        cost_estimate=cost,
-        name="near_share",
-    )(here, near_side, near_pattern, pert, weights, innov, state, paired, to_far)
     from_near = lax.ppermute(to_near, "lon", near)
     own = pl.pallas_call(
         functools.partial(own_kernel, patches),
@@ -326,9 +329,10 @@
         cost_estimate=cost,
         name="own_share",
     )(here, pattern, pert, weights, innov, to_near)
-    for shift in range(1, length):
-        trade = [(i, i ^ (shift * PAIR)) for i in range(mem_total)]
-        slabs[shift] = lax.ppermute(slabs[shift], "mem", trade)
+    for i, shift in enumerate(turns(length)):
+        if shift:
+            trade = [(j, j ^ (shift * PAIR)) for j in range(mem_total)]
+            slabs[i] = lax.ppermute(slabs[i], "mem", trade)
     root, rows = pl.pallas_call(
         root_kernel,
         out_shape=(shape((mine, members, members), BF16), shape((mine, PAD, members), F32)),

time: 31.9 us -> 31.6 us (level)
  blocking collectives: 10.1 us -> 11.7 us
  waiting for transfers between devices: 1.91 us -> 0.62 us
  Pallas kernels: 8.76 us -> 7.78 us
  starting transfers between devices: 10.1 us -> 10.6 us
    all_to_all x1, blocking collectives: 10.1 us -> 11.7 us  [body(): lax.all_to_all(updated.reshape(mem_total, local, span), 'mem', split_axis...]
    ppermute x3, waiting for transfers between devices: 1.9 us -> 0.61 us  [body(): slabs[i] = lax.ppermute(slabs[i], 'mem', trade)]
    ppermute x1, starting transfers between devices: 0.46 us -> 1.42 us  [body(): from_far = lax.ppermute(to_far, 'lon', far)]
    ppermute x1, starting transfers between devices: 0.96 us -> 0.01 us  [body(): near_pattern = lax.ppermute(pattern, 'lon', near)]
    ppermute x1, starting transfers between devices: 0.68 us -> 1.63 us  [body(): far_pattern = lax.ppermute(pattern, 'lon', far)]
    pallas_call x2 -> x1, Pallas kernels: 2.39 us -> 1.49 us  [body(): pl.pallas_call(functools.partial(neighbour_kernel, patches), out_shape=(p...]
  transfers between devices with their start and end apart: 8 -> 8, of which waited for: 1 -> 1; matrix products, arithmetic and copies ran while one was open for 0% -> 0% of each run, Pallas kernels for 26% -> 18%
where the time goes in v11:
time: 31.6 us; the launch traced here: 31.4 us
  blocking collectives  11.7 us (37%)
  starting transfers between devices  10.6 us (34%)
  Pallas kernels  7.78 us (25%)
  local copies, waits for them, and re-layouts  0.67 us (2%)
  waiting for transfers between devices  0.62 us (2%)
    all_to_all x1, blocking collectives, body(): lax.all_to_all(updated.reshape(mem_total, local, span), 'mem', split_axis...  11.7 us
    ppermute x3, starting transfers between devices, body(): slabs[i] = lax.ppermute(slabs[i], 'mem', trade)  4.16 us
    ppermute x1, starting transfers between devices, body(): paired = lax.ppermute(state, 'mem', swap)  2.94 us
    pallas_call x1, Pallas kernels, body(): pl.pallas_call(root_kernel, out_shape=(shape((mine, members, members), BF...  2.39 us
    pallas_call x1, Pallas kernels, body(): pl.pallas_call(perturb_kernel, out_shape=(shape((blocks, members, width),...  2.13 us
    ppermute x1, starting transfers between devices, body(): far_pattern = lax.ppermute(pattern, 'lon', far)  1.63 us
    pallas_call x1, Pallas kernels, body(): pl.pallas_call(functools.partial(neighbour_kernel, patches), out_shape=(p...  1.49 us
    ppermute x1, starting transfers between devices, body(): from_far = lax.ppermute(to_far, 'lon', far)  1.42 us
  transfers between devices with their start and end apart: 8, of which 1 were waited for; matrix products, arithmetic and copies ran while one was open for 0% of the time, Pallas kernels for 18%

profile of v11, /device:TPU:0, one launch (start us, length us, event | category | flops | bytes accessed | tf_op | source)
XLA Modules:
  0.0 31.4 jit_solution(4782128808656951223)
XLA Ops:
  0.0 0.0 copy-start
  0.0 2.9 %collective-permute-start.2 = (bf16[32,2048]{1,0:T(8,128)(2,1)}, bf16[32,2048]{1,0:T(8,128)(2,1)S(1)}, u32[]{:S(2)}, u32[]{:S(2)}) collective-permute-start(bf16[32,2048]{1,0:T(8,128)(2,1)} %state.1), channel_id=1, source_target_pairs={{0,4},{4,0},{8,12},{12,8},{16,20},{20,16},{24,28},{28,24},{1,5},{5... | collective-permute-start | bytes 393224 | tf_op jit(solution)/shard_map/ppermute | solution.py:283
  2.9 0.0 collective-permute-start.1
  2.9 1.6 %collective-permute-start = (s32[8,16]{1,0:T(8,128)}, s32[8,16]{1,0:T(8,128)S(1)}, u32[]{:S(2)}, u32[]{:S(2)}) collective-permute-start(s32[8,16]{1,0:T(8,128)} %bitcast.10), channel_id=1, source_target_pairs={{0,3},{1,2},{2,1},{3,0},{4,7},{5,6},{6,5},{7,4},{8,11},{9,10},{10,... | collective-permute-start | bytes 1544 | tf_op jit(solution)/shard_map/ppermute | solution.py:281
  4.6 0.0 copy-start.1
  4.6 2.1 %perturb.1 = (bf16[32,256,128]{2,1,0:T(8,128)(2,1)S(1)}, f32[32,128]{1,0:T(8,128)S(1)}, f32[32,128]{1,0:T(8,128)S(1)}) custom-call(s32[32]{0:T(128)} %count_all.1, bf16[32,256,128]{2,1,0:T(8,128)(2,1)} %hx.1, f32[32,128]{1,0:T(8,128)} %value_all.1, f32[32,128]{1,0:T(8,128)} %rinv_all.1), custom_call_target="tpu_custom_call" | custom-call | flops 4194304 | bytes 4194304 | tf_op jit(solution)/shard_map/perturb/pallas_call | solution.py:286
  6.7 0.0 collective-permute-done.1.near_pattern
  6.7 0.0 collective-permute-done.far_pattern
  6.7 0.0 collective-permute-done.2.paired
  6.7 0.0 copy-done
  6.8 1.5 %neighbour_shares.1 = (bf16[2,272,128]{2,1,0:T(8,128)(2,1)S(1)}, bf16[2,272,128]{2,1,0:T(8,128)(2,1)S(1)}, bf16[2,32,256]{2,1,0:T(8,128)(2,1)S(1)}, bf16[2,32,25...) custom-call(s32[1]{0:T(128)} %bitcast.here, s32[1]{0:T(128)} %bitcast.2.far_side, ...), custom_call_target="tpu_custom_call" | custom-call | flops 285212672 | bytes 1048576 | tf_op jit(solution)/shard_map/neighbour_shares/pallas_call | solution.py:312
  8.3 1.4 %collective-permute-start.3 = (bf16[2,272,128]{2,1,0:T(8,128)(2,1)S(1)}, bf16[2,272,128]{2,1,0:T(8,128)(2,1)S(1)}, u32[]{:S(2)}, u32[]{:S(2)}) collective-permute-start(bf16[2,272,128]{2,1,0:T(8,128)(2,1)S(1)} %get-tuple-element.20), channel_id=1, source_target_pairs={{0,3},{1,2},{2,1},{3,0},{4,7},{5,6},{6,5},{7,4},{8,11},{9,10},{10,... | collective-permute-start | bytes 417800 | tf_op jit(solution)/shard_map/ppermute | solution.py:321
  9.7 0.4 %collective-permute-start.4 = (bf16[2,272,128]{2,1,0:T(8,128)(2,1)S(1)}, bf16[2,272,128]{2,1,0:T(8,128)(2,1)S(1)}, u32[]{:S(2)}, u32[]{:S(2)}) collective-permute-start(bf16[2,272,128]{2,1,0:T(8,128)(2,1)S(1)} %get-tuple-element.19.sent), channel_id=1, source_target_pairs={{0,1},{1,0},{2,3},{3,2},{4,5},{5,4},{6,7},{7,6},{8,9},{9,8},{10,11... | collective-permute-start | bytes 417800 | tf_op jit(solution)/shard_map/ppermute | solution.py:322
  10.1 2.6 %collective-permute-start.5 = (bf16[2,32,256]{2,1,0:T(8,128)(2,1)S(1)}, bf16[2,32,256]{2,1,0:T(8,128)(2,1)S(1)}, u32[]{:S(2)}, u32[]{:S(2)}) collective-permute-start(bf16[2,32,256]{2,1,0:T(8,128)(2,1)S(1)} %get-tuple-element.24), channel_id=1, source_target_pairs={{0,16},{4,20},{8,24},{12,28},{16,0},{20,4},{24,8},{28,12},{1,17},{... | collective-permute-start | bytes 98312 | tf_op jit(solution)/shard_map/ppermute | solution.py:335
  12.7 1.3 %collective-permute-start.6 = (bf16[2,32,256]{2,1,0:T(8,128)(2,1)S(1)}, bf16[2,32,256]{2,1,0:T(8,128)(2,1)S(1)}, u32[]{:S(2)}, u32[]{:S(2)}) collective-permute-start(bf16[2,32,256]{2,1,0:T(8,128)(2,1)S(1)} %get-tuple-element.25), channel_id=1, source_target_pairs={{0,24},{4,28},{8,16},{12,20},{16,8},{20,12},{24,0},{28,4},{1,25},{... | collective-permute-start | bytes 98312 | tf_op jit(solution)/shard_map/ppermute | solution.py:335
  14.0 0.2 collective-permute-start.7
  14.3 0.0 copy-done.1
  14.3 1.1 %own_share.1.own = f32[2,272,256]{2,1,0:T(8,128)S(1)} custom-call(s32[1]{0:T(128)} %bitcast.here, s32[8,16]{1,0:T(8,128)S(1)} %bitcast.11, bf16[32,256,128]{2,1,0:T(8,128)(2,1)S(1)} %get-tuple-element.16.pert, f32[32,128]{1,0:T(8,128)S(1)} %get-tuple-element.17.weights, f32[32,128]{1,0:T(8,128)S(1)} %get-tuple-element.18.innov, ...), custom_call_target="tpu_custom_call" | custom-call | flops 285212672 | bytes 1048576 | tf_op jit(solution)/shard_map/own_share/pallas_call | solution.py:323
  15.4 0.0 collective-permute-done.3.before
  15.4 0.0 collective-permute-done.4.after
  15.4 2.4 %root.1 = (bf16[2,256,256]{2,1,0:T(8,128)(2,1)S(1)}, f32[2,16,256]{2,1,0:T(8,128)S(1)}) custom-call(f32[2,272,256]{2,1,0:T(8,128)S(1)} %own_share.1.own, bf16[2,272,128]{2,1,0:T(8,128)(2,1)S(1)} %collective-permute-done.3.before, bf16[2,272,128]{2,1,0:T(8,128)(2,1)S(1)} %collective-permute-done.4.after), custom_call_target="tpu_custom_call" | custom-call | flops 1006632960 | bytes 1048576 | tf_op jit(solution)/shard_map/root/pallas_call | solution.py:336
  17.8 0.0 collective-permute-done.5.rest_1_
  17.8 0.6 %collective-permute-done.6.rest_2_ = bf16[2,32,256]{2,1,0:T(8,128)(2,1)S(1)} collective-permute-done((bf16[2,32,256]{2,1,0:T(8,128)(2,1)S(1)}, bf16[2,32,256]{2,1,0:T(8,128)(2,1)S(1)}, u32[]{:S(2)}, u32[]{:S(2)}) %collective-permute-start.6) | collective-permute-done | bytes 32800 | tf_op jit(solution)/shard_map/ppermute | solution.py:335
  18.4 0.0 collective-permute-done.7.rest_3_
  18.4 0.7 %apply.1 = bf16[256,256]{1,0:T(8,128)(2,1)S(1)} custom-call(s32[1]{0:T(128)} %bitcast.here, bf16[2,256,256]{2,1,0:T(8,128)(2,1)S(1)} %get-tuple-element.21.root, f32[2,16,256]{2,1,0:T(8,128)S(1)} %get-tuple-element.22.rows, bf16[2,32,256]{2,1,0:T(8,128)(2,1)S(1)} %get-tuple-element.23.rest_0_, bf16[2,32,256]{2,1,0:T(8,128)(2,1)S(1)} %collective-permute-done.5.rest_1_, ...), custom_call_target="tpu_custom_call" | custom-call | flops 33554432 | bytes 524288 | tf_op jit(solution)/shard_map/apply/pallas_call | solution.py:347
  19.1 11.7 %all_to_all.5 = bf16[8,32,256]{2,1,0:T(8,128)(2,1)S(1)} all-to-all(bf16[8,32,256]{2,1,0:T(8,128)(2,1)S(1)} %bitcast.8), channel_id=1, replica_groups=mesh['mem'=8,'lon'=4] {'mem'}, dimensions={0} | all-to-all | bytes 262144 | tf_op jit(solution)/shard_map/all_to_all | solution.py:359
  30.7 0.7 %copy.8 = bf16[8,4,8,256]{3,2,0,1:T(8,128)(2,1)} copy(bf16[8,4,8,256]{3,2,1,0:T(8,128)(2,1)S(1)} %bitcast.12) | data formatting | bytes 262144 | tf_op jit(solution)/shard_map/reshape | solution.py:362
Async XLA Ops:
  0.0 6.7 %copy-start = (bf16[32,2048]{1,0:T(8,128)(2,1)S(1)}, bf16[32,2048]{1,0:T(8,128)(2,1)}, u32[]{:S(2)}) copy-start(bf16[32,2048]{1,0:T(8,128)(2,1)} %state.1) | copy-start | bytes 393220
  0.0 6.7 %collective-permute-start.2 = (bf16[32,2048]{1,0:T(8,128)(2,1)}, bf16[32,2048]{1,0:T(8,128)(2,1)S(1)}, u32[]{:S(2)}, u32[]{:S(2)}) collective-permute-start(bf16[32,2048]{1,0:T(8,128)(2,1)} %state.1), channel_id=1, source_target_pairs={{0,4},{4,0},{8,12},{12,8},{16,20},{20,16},{24,28},{28,24},{1,5},{5... | collective-permute-start | bytes 393224 | tf_op jit(solution)/shard_map/ppermute | solution.py:283
  2.9 3.8 %collective-permute-start.1 = (s32[8,16]{1,0:T(8,128)}, s32[8,16]{1,0:T(8,128)S(1)}, u32[]{:S(2)}, u32[]{:S(2)}) collective-permute-start(s32[8,16]{1,0:T(8,128)} %bitcast.9), channel_id=1, source_target_pairs={{0,1},{1,0},{2,3},{3,2},{4,5},{5,4},{6,7},{7,6},{8,9},{9,8},{10,11... | collective-permute-start | bytes 1544 | tf_op jit(solution)/shard_map/ppermute | solution.py:282
  2.9 3.8 %collective-permute-start = (s32[8,16]{1,0:T(8,128)}, s32[8,16]{1,0:T(8,128)S(1)}, u32[]{:S(2)}, u32[]{:S(2)}) collective-permute-start(s32[8,16]{1,0:T(8,128)} %bitcast.10), channel_id=1, source_target_pairs={{0,3},{1,2},{2,1},{3,0},{4,7},{5,6},{6,5},{7,4},{8,11},{9,10},{10,... | collective-permute-start | bytes 1544 | tf_op jit(solution)/shard_map/ppermute | solution.py:281
  4.6 9.7 %copy-start.1 = (s32[16,8]{0,1:T(8,128)S(1)}, s32[16,8]{0,1:T(8,128)}, u32[]{:S(2)}) copy-start(s32[16,8]{0,1:T(8,128)} %param.11) | copy-start | bytes 1540
  8.3 7.1 %collective-permute-start.3 = (bf16[2,272,128]{2,1,0:T(8,128)(2,1)S(1)}, bf16[2,272,128]{2,1,0:T(8,128)(2,1)S(1)}, u32[]{:S(2)}, u32[]{:S(2)}) collective-permute-start(bf16[2,272,128]{2,1,0:T(8,128)(2,1)S(1)} %get-tuple-element.20), channel_id=1, source_target_pairs={{0,3},{1,2},{2,1},{3,0},{4,7},{5,6},{6,5},{7,4},{8,11},{9,10},{10,... | collective-permute-start | bytes 417800 | tf_op jit(solution)/shard_map/ppermute | solution.py:321
  9.7 5.7 %collective-permute-start.4 = (bf16[2,272,128]{2,1,0:T(8,128)(2,1)S(1)}, bf16[2,272,128]{2,1,0:T(8,128)(2,1)S(1)}, u32[]{:S(2)}, u32[]{:S(2)}) collective-permute-start(bf16[2,272,128]{2,1,0:T(8,128)(2,1)S(1)} %get-tuple-element.19.sent), channel_id=1, source_target_pairs={{0,1},{1,0},{2,3},{3,2},{4,5},{5,4},{6,7},{7,6},{8,9},{9,8},{10,11... | collective-permute-start | bytes 417800 | tf_op jit(solution)/shard_map/ppermute | solution.py:322
  10.1 7.7 %collective-permute-start.5 = (bf16[2,32,256]{2,1,0:T(8,128)(2,1)S(1)}, bf16[2,32,256]{2,1,0:T(8,128)(2,1)S(1)}, u32[]{:S(2)}, u32[]{:S(2)}) collective-permute-start(bf16[2,32,256]{2,1,0:T(8,128)(2,1)S(1)} %get-tuple-element.24), channel_id=1, source_target_pairs={{0,16},{4,20},{8,24},{12,28},{16,0},{20,4},{24,8},{28,12},{1,17},{... | collective-permute-start | bytes 98312 | tf_op jit(solution)/shard_map/ppermute | solution.py:335
  12.7 5.7 %collective-permute-start.6 = (bf16[2,32,256]{2,1,0:T(8,128)(2,1)S(1)}, bf16[2,32,256]{2,1,0:T(8,128)(2,1)S(1)}, u32[]{:S(2)}, u32[]{:S(2)}) collective-permute-start(bf16[2,32,256]{2,1,0:T(8,128)(2,1)S(1)} %get-tuple-element.25), channel_id=1, source_target_pairs={{0,24},{4,28},{8,16},{12,20},{16,8},{20,12},{24,0},{28,4},{1,25},{... | collective-permute-start | bytes 98312 | tf_op jit(solution)/shard_map/ppermute | solution.py:335
  14.0 4.4 %collective-permute-start.7 = (bf16[2,32,256]{2,1,0:T(8,128)(2,1)S(1)}, bf16[2,32,256]{2,1,0:T(8,128)(2,1)S(1)}, u32[]{:S(2)}, u32[]{:S(2)}) collective-permute-start(bf16[2,32,256]{2,1,0:T(8,128)(2,1)S(1)} %get-tuple-element.26), channel_id=1, source_target_pairs={{0,8},{4,12},{8,0},{12,4},{16,24},{20,28},{24,16},{28,20},{1,9},{5... | collective-permute-start | bytes 98312 | tf_op jit(solution)/shard_map/ppermute | solution.py:335

commit v12 on v8

--- a/solution.py
+++ b/solution.py
@@ -65,7 +65,6 @@
 
 def own_kernel(
     patches,
-    here,
     count_all,
     pattern_all,
     hx,
@@ -111,7 +110,7 @@
         innov[block : block + 1, :] = gap
     mine = own.shape[0]
     for patch in range(mine):
-        row = here[0] * mine + patch
+        row = lax.axis_index("mem") * mine + patch
         own[patch] = share(pattern, row, 1, patches, pert, weights, innov)
 
 
@@ -136,30 +135,28 @@
     out[patch, members:, :] = tail.astype(BF16)
 
 
-def far_kernel(patches, here, side, pattern, pert, weights, innov, out):
+def neighbour(patches, side, pattern, pert, weights, innov, out):
     mine = out.shape[0]
     for patch in range(mine):
-        row = here[0] * mine + patch
-        pack(share(pattern, row, side[0], patches, pert, weights, innov), out, patch)
-
-
-def near_kernel(patches, here, side, pattern, pert, weights, innov, state, paired, sent, out, *rest):
-    slabs, sems = rest[:-1], rest[-1]
+        row = lax.axis_index("mem") * mine + patch
+        pack(share(pattern, row, side, patches, pert, weights, innov), out, patch)
+
+
+def far_kernel(patches, pattern, pert, weights, innov, out):
+    side = 2 - 2 * (lax.axis_index("lon") % 2)
+    neighbour(patches, side, pattern, pert, weights, innov, out)
+
+
+def near_kernel(patches, pattern, pert, weights, innov, state, paired, sent, out, *slabs):
     span = slabs[0].shape[2]
     length = len(slabs)
-    layer, place = here[0] // PAIR, here[0] % PAIR
-    moves = []
+    layer, place = lax.axis_index("mem") // PAIR, lax.axis_index("mem") % PAIR
     for shift, slab in zip(turns(length), slabs):
         target = (layer ^ shift) * PAIR + place
         cols = pl.ds(pl.multiple_of(target * span, span), span)
-        moves.append((state.at[:, cols], slab.at[place]))
-        moves.append((paired.at[:, cols], slab.at[1 - place]))
-    moves = [pltpu.make_async_copy(*move, sems.at[i]) for i, move in enumerate(moves)]
-    for move in moves:
-        move.start()
-    far_kernel(patches, here, side, pattern, pert, weights, innov, out)
-    for move in moves:
-        move.wait()
+        slab[place] = state[:, cols]
+        slab[1 - place] = paired[:, cols]
+    neighbour(patches, 2 * (lax.axis_index("lon") % 2), pattern, pert, weights, innov, out)
 
 
 def total(value):
@@ -239,14 +236,14 @@
         rows_out[p] = jnp.where(index == 0, gain, jnp.where(index == 1, lead[p], spread))
 
 
-def apply_kernel(here, root, rows, *rest):
+def apply_kernel(root, rows, *rest):
     slabs, (out, columns) = rest[:-2], rest[-2:]
     mine, members, _ = root.shape
     points = out.shape[1] // mine
     length = len(slabs)
     _, local, _ = slabs[0].shape
     for shift, slab in zip(turns(length), slabs):
-        source = (here[0] // PAIR) ^ shift
+        source = (lax.axis_index("mem") // PAIR) ^ shift
         for i in range(PAIR):
             place = pl.ds(pl.multiple_of((source * PAIR + i) * local, local), local)
             columns[place, :] = slab[i]
@@ -271,10 +268,6 @@
     ring = lax.axis_size("lon")
     near = [(i, i + 1 - 2 * (i % 2)) for i in range(ring)]
     far = [(i, (i - 1 + 2 * (i % 2)) % ring) for i in range(ring)]
-    odd = lax.axis_index("lon") % 2
-    here, near_side, far_side = (
-        value.astype(jnp.int32).reshape(1) for value in (lax.axis_index("mem"), 2 * odd, 2 - 2 * odd)
-    )
     shape = jax.ShapeDtypeStruct
     padded = members + PAD
 
@@ -297,7 +290,7 @@
             shape((blocks, width), F32),
             shape((mine, padded, members), F32),
         ),
-        in_specs=[SMEM] + [HBM] * 5,
+        in_specs=[HBM] * 5,
         out_specs=(VMEM,) * 4,
         scratch_shapes=[
             pltpu.VMEM((blocks, members, width), BF16),
@@ -313,30 +306,29 @@
             flops=hx.size * 4 + mine * gram, bytes_accessed=2 * hx.size * 2, transcendentals=0
         ),
         name="own_share",
-    )(here, *(stay(value) for value in (obs_count, pattern, hx, obs_value, obs_rinv)))
+    )(*(stay(value) for value in (obs_count, pattern, hx, obs_value, obs_rinv)))
     packed = shape((mine, padded, members // 2), BF16)
     slab = shape((PAIR, local, span), BF16)
     cost = pl.CostEstimate(flops=mine * gram, bytes_accessed=hx.size, transcendentals=0)
     to_far = pl.pallas_call(
         functools.partial(far_kernel, patches),
         out_shape=packed,
-        in_specs=[SMEM] * 3 + [VMEM] * 3,
+        in_specs=[SMEM] + [VMEM] * 3,
         out_specs=VMEM,
         compiler_params=limit,
         cost_estimate=cost,
         name="far_share",
-    )(here, far_side, far_pattern, pert, weights, innov)
+    )(far_pattern, pert, weights, innov)
     from_far = lax.ppermute(to_far, "lon", far)
     to_near, *slabs = pl.pallas_call(
         functools.partial(near_kernel, patches),
         out_shape=(packed,) + (slab,) * length,
-        in_specs=[SMEM] * 3 + [VMEM] * 3 + [HBM] * 2 + [pl.BlockSpec(memory_space=pl.ANY)],
+        in_specs=[SMEM] + [VMEM] * 5 + [pl.BlockSpec(memory_space=pl.ANY)],
         out_specs=(VMEM,) * (1 + length),
-        scratch_shapes=[pltpu.SemaphoreType.DMA((PAIR * length,))],
         compiler_params=limit,
         cost_estimate=cost,
         name="near_share",
-    )(here, near_side, near_pattern, pert, weights, innov, state, paired, to_far)
+    )(near_pattern, pert, weights, innov, state, paired, to_far)
     from_near = lax.ppermute(to_near, "lon", near)
     for i, shift in enumerate(turns(length)):
         if shift:
@@ -356,7 +348,7 @@
     updated = pl.pallas_call(
         apply_kernel,
         out_shape=shape((members, span), BF16),
-        in_specs=[SMEM] + [VMEM] * (2 + length),
+        in_specs=[VMEM] * (2 + length),
         out_specs=VMEM,
         scratch_shapes=[pltpu.VMEM((members, span), BF16)],
         compiler_params=limit,
@@ -364,7 +356,7 @@
             flops=2 * members**2 * span, bytes_accessed=2**19, transcendentals=0
         ),
         name="apply",
-    )(here, root, rows, *slabs)
+    )(root, rows, *slabs)
     pieces = lax.all_to_all(
         updated.reshape(mem_total, local, span), "mem", split_axis=0, concat_axis=0
     )

time: 31 us -> 30.9 us (level)
  no operation moved by 1% of the time
where the time goes in v12:
time: 30.9 us; the launch traced here: 30.7 us
  blocking collectives  10.4 us (34%)
  starting transfers between devices  9.9 us (32%)
  Pallas kernels  7.9 us (26%)
  waiting for transfers between devices  1.76 us (6%)
  local copies, waits for them, and re-layouts  0.67 us (2%)
    all_to_all x1, blocking collectives, body(): lax.all_to_all(updated.reshape(mem_total, local, span), 'mem', split_axis...  10.4 us
    ppermute x3, starting transfers between devices, body(): slabs[i] = lax.ppermute(slabs[i], 'mem', trade)  4.23 us
    ppermute x1, starting transfers between devices, body(): paired = lax.ppermute(state, 'mem', swap)  2.94 us
    pallas_call x1, Pallas kernels, body(): pl.pallas_call(functools.partial(own_kernel, patches), out_shape=(shape((...  2.55 us
    pallas_call x1, Pallas kernels, body(): pl.pallas_call(root_kernel, out_shape=(shape((mine, members, members), BF...  2.39 us
    ppermute x3, waiting for transfers between devices, body(): slabs[i] = lax.ppermute(slabs[i], 'mem', trade)  1.74 us
    ppermute x1, starting transfers between devices, body(): far_pattern = lax.ppermute(pattern, 'lon', far)  1.63 us
    pallas_call x1, Pallas kernels, body(): pl.pallas_call(functools.partial(near_kernel, patches), out_shape=(packed...  1.15 us
  transfers between devices with their start and end apart: 8, of which 1 were waited for; matrix products, arithmetic and copies ran while one was open for 0% of the time, Pallas kernels for 24%

profile of v12, /device:TPU:0, one launch (start us, length us, event | category | flops | bytes accessed | tf_op | source)
XLA Modules:
  0.0 30.7 jit_solution(11917681756444451551)
XLA Ops:
  0.0 2.9 %collective-permute-start.3 = (bf16[32,2048]{1,0:T(8,128)(2,1)}, bf16[32,2048]{1,0:T(8,128)(2,1)S(1)}, u32[]{:S(2)}, u32[]{:S(2)}) collective-permute-start(bf16[32,2048]{1,0:T(8,128)(2,1)} %state.1), channel_id=1, source_target_pairs={{0,4},{4,0},{8,12},{12,8},{16,20},{20,16},{24,28},{28,24},{1,5},{5... | collective-permute-start | bytes 393224 | tf_op jit(solution)/shard_map/ppermute | solution.py:282
  2.9 0.0 copy-start
  2.9 0.0 collective-permute-start.2
  2.9 1.6 %collective-permute-start = (s32[8,16]{1,0:T(8,128)}, s32[8,16]{1,0:T(8,128)S(1)}, u32[]{:S(2)}, u32[]{:S(2)}) collective-permute-start(s32[8,16]{1,0:T(8,128)} %bitcast.8), channel_id=1, source_target_pairs={{0,3},{1,2},{2,1},{3,0},{4,7},{5,6},{6,5},{7,4},{8,11},{9,10},{10,... | collective-permute-start | bytes 1544 | tf_op jit(solution)/shard_map/ppermute | solution.py:280
  4.6 2.6 %own_share.1 = (bf16[32,256,128]{2,1,0:T(8,128)(2,1)S(1)}, f32[32,128]{1,0:T(8,128)S(1)}, f32[32,128]{1,0:T(8,128)S(1)}, f32[2,272,256]{2,1,0:T(8,128)S(1)}) custom-call(s32[32]{0:T(128)} %count_all.1, s32[8,16]{1,0:T(8,128)} %bitcast.9, bf16[32,256,128]{2,1,0:T(8,128)(2,1)} %hx.1, f32[32,128]{1,0:T(8,128)} %value_all.1, f32[32,128]{1,0:T(8,128)} %rinv_all.1), custom_call_target="tpu_custom_call" | custom-call | flops 289406976 | bytes 4194304 | tf_op jit(solution)/shard_map/own_share/pallas_call | solution.py:285
  7.1 0.0 collective-permute-done.pattern
  7.1 1.1 %far_share.1.sent = bf16[2,272,128]{2,1,0:T(8,128)(2,1)S(1)} custom-call(s32[8,16]{1,0:T(8,128)S(1)} %collective-permute-done.pattern, bf16[32,256,128]{2,1,0:T(8,128)(2,1)S(1)} %get-tuple-element.17.pert, f32[32,128]{1,0:T(8,128)S(1)} %get-tuple-element.18.weights, f32[32,128]{1,0:T(8,128)S(1)} %get-tuple-element.19.innov), custom_call_target="tpu_custom_call" | custom-call | flops 285212672 | bytes 1048576 | tf_op jit(solution)/shard_map/far_share/pallas_call | solution.py:313
  8.3 1.0 %collective-permute-start.1 = (bf16[2,272,128]{2,1,0:T(8,128)(2,1)S(1)}, bf16[2,272,128]{2,1,0:T(8,128)(2,1)S(1)}, u32[]{:S(2)}, u32[]{:S(2)}) collective-permute-start(bf16[2,272,128]{2,1,0:T(8,128)(2,1)S(1)} %far_share.1.sent), channel_id=1, source_target_pairs={{0,3},{1,2},{2,1},{3,0},{4,7},{5,6},{6,5},{7,4},{8,11},{9,10},{10,... | collective-permute-start | bytes 417800 | tf_op jit(solution)/shard_map/ppermute | solution.py:322
  9.3 0.0 collective-permute-done.2.pattern
  9.3 0.0 collective-permute-done.3.paired
  9.3 0.0 copy-done
  9.3 1.2 %near_share.1 = (bf16[2,272,128]{2,1,0:T(8,128)(2,1)S(1)}, bf16[2,32,256]{2,1,0:T(8,128)(2,1)S(1)}, bf16[2,32,256]{2,1,0:T(8,128)(2,1)S(1)}, bf16[2,32,256]{2,1,0:T(8,128)(2,1)S(1)}, bf16[2,32,256]{2,1,0:T(8,128)(2,1)S(1)}) custom-call(s32[8,16]{1,0:T(8,128)S(1)} %collective-permute-done.2.pattern, bf16[32,256,128]{2,1,0:T(8,128)(2,1)S(1)} %get-tuple-element.17.pert, ...), custom_call_target="tpu_custom_call" | custom-call | flops 285212672 | bytes 1048576 | tf_op jit(solution)/shard_map/near_share/pallas_call | solution.py:323
  10.5 0.1 collective-permute-start.4
  10.6 2.7 %collective-permute-start.5 = (bf16[2,32,256]{2,1,0:T(8,128)(2,1)S(1)}, bf16[2,32,256]{2,1,0:T(8,128)(2,1)S(1)}, u32[]{:S(2)}, u32[]{:S(2)}) collective-permute-start(bf16[2,32,256]{2,1,0:T(8,128)(2,1)S(1)} %get-tuple-element.24), channel_id=1, source_target_pairs={{0,16},{4,20},{8,24},{12,28},{16,0},{20,4},{24,8},{28,12},{1,17},{... | collective-permute-start | bytes 98312 | tf_op jit(solution)/shard_map/ppermute | solution.py:336
  13.2 1.3 %collective-permute-start.6 = (bf16[2,32,256]{2,1,0:T(8,128)(2,1)S(1)}, bf16[2,32,256]{2,1,0:T(8,128)(2,1)S(1)}, u32[]{:S(2)}, u32[]{:S(2)}) collective-permute-start(bf16[2,32,256]{2,1,0:T(8,128)(2,1)S(1)} %get-tuple-element.25), channel_id=1, source_target_pairs={{0,24},{4,28},{8,16},{12,20},{16,8},{20,12},{24,0},{28,4},{1,25},{... | collective-permute-start | bytes 98312 | tf_op jit(solution)/shard_map/ppermute | solution.py:336
  14.6 0.2 collective-permute-start.7
  14.8 0.0 collective-permute-done.1.before
  14.8 0.0 collective-permute-done.4.after
  14.8 2.4 %root.1 = (bf16[2,256,256]{2,1,0:T(8,128)(2,1)S(1)}, f32[2,16,256]{2,1,0:T(8,128)S(1)}) custom-call(f32[2,272,256]{2,1,0:T(8,128)S(1)} %get-tuple-element.16.own, bf16[2,272,128]{2,1,0:T(8,128)(2,1)S(1)} %collective-permute-done.1.before, bf16[2,272,128]{2,1,0:T(8,128)(2,1)S(1)} %collective-permute-done.4.after), custom_call_target="tpu_custom_call" | custom-call | flops 1006632960 | bytes 1048576 | tf_op jit(solution)/shard_map/root/pallas_call | solution.py:337
  17.2 0.0 collective-permute-done.5.rest_1_
  17.2 1.7 %collective-permute-done.6.rest_2_ = bf16[2,32,256]{2,1,0:T(8,128)(2,1)S(1)} collective-permute-done((bf16[2,32,256]{2,1,0:T(8,128)(2,1)S(1)}, bf16[2,32,256]{2,1,0:T(8,128)(2,1)S(1)}, u32[]{:S(2)}, u32[]{:S(2)}) %collective-permute-start.6) | collective-permute-done | bytes 32800 | tf_op jit(solution)/shard_map/ppermute | solution.py:336
  18.9 0.0 collective-permute-done.7.rest_3_
  18.9 0.7 %apply.1 = bf16[256,256]{1,0:T(8,128)(2,1)S(1)} custom-call(bf16[2,256,256]{2,1,0:T(8,128)(2,1)S(1)} %get-tuple-element.21.root, f32[2,16,256]{2,1,0:T(8,128)S(1)} %get-tuple-element.22.rows, bf16[2,32,256]{2,1,0:T(8,128)(2,1)S(1)} %get-tuple-element.23.rest_0_, bf16[2,32,256]{2,1,0:T(8,128)(2,1)S(1)} %collective-permute-done.5.rest_1_, ...), custom_call_target="tpu_custom_call" | custom-call | flops 33554432 | bytes 524288 | tf_op jit(solution)/shard_map/apply/pallas_call | solution.py:348
  19.6 10.4 %all_to_all.5 = bf16[8,32,256]{2,1,0:T(8,128)(2,1)S(1)} all-to-all(bf16[8,32,256]{2,1,0:T(8,128)(2,1)S(1)} %bitcast.5), channel_id=1, replica_groups=mesh['mem'=8,'lon'=4] {'mem'}, dimensions={0} | all-to-all | bytes 262144 | tf_op jit(solution)/shard_map/all_to_all | solution.py:360
  30.0 0.7 %copy.8 = bf16[8,4,8,256]{3,2,0,1:T(8,128)(2,1)} copy(bf16[8,4,8,256]{3,2,1,0:T(8,128)(2,1)S(1)} %bitcast.6) | data formatting | bytes 262144 | tf_op jit(solution)/shard_map/reshape | solution.py:363
Async XLA Ops:
  0.0 9.3 %collective-permute-start.3 = (bf16[32,2048]{1,0:T(8,128)(2,1)}, bf16[32,2048]{1,0:T(8,128)(2,1)S(1)}, u32[]{:S(2)}, u32[]{:S(2)}) collective-permute-start(bf16[32,2048]{1,0:T(8,128)(2,1)} %state.1), channel_id=1, source_target_pairs={{0,4},{4,0},{8,12},{12,8},{16,20},{20,16},{24,28},{28,24},{1,5},{5... | collective-permute-start | bytes 393224 | tf_op jit(solution)/shard_map/ppermute | solution.py:282
  2.9 6.4 %copy-start = (bf16[32,2048]{1,0:T(8,128)(2,1)S(1)}, bf16[32,2048]{1,0:T(8,128)(2,1)}, u32[]{:S(2)}) copy-start(bf16[32,2048]{1,0:T(8,128)(2,1)} %state.1) | copy-start | bytes 393220
  2.9 6.4 %collective-permute-start.2 = (s32[8,16]{1,0:T(8,128)}, s32[8,16]{1,0:T(8,128)S(1)}, u32[]{:S(2)}, u32[]{:S(2)}) collective-permute-start(s32[8,16]{1,0:T(8,128)} %bitcast.7), channel_id=1, source_target_pairs={{0,1},{1,0},{2,3},{3,2},{4,5},{5,4},{6,7},{7,6},{8,9},{9,8},{10,11... | collective-permute-start | bytes 1544 | tf_op jit(solution)/shard_map/ppermute | solution.py:281
  2.9 4.2 %collective-permute-start = (s32[8,16]{1,0:T(8,128)}, s32[8,16]{1,0:T(8,128)S(1)}, u32[]{:S(2)}, u32[]{:S(2)}) collective-permute-start(s32[8,16]{1,0:T(8,128)} %bitcast.8), channel_id=1, source_target_pairs={{0,3},{1,2},{2,1},{3,0},{4,7},{5,6},{6,5},{7,4},{8,11},{9,10},{10,... | collective-permute-start | bytes 1544 | tf_op jit(solution)/shard_map/ppermute | solution.py:280
  8.3 6.5 %collective-permute-start.1 = (bf16[2,272,128]{2,1,0:T(8,128)(2,1)S(1)}, bf16[2,272,128]{2,1,0:T(8,128)(2,1)S(1)}, u32[]{:S(2)}, u32[]{:S(2)}) collective-permute-start(bf16[2,272,128]{2,1,0:T(8,128)(2,1)S(1)} %far_share.1.sent), channel_id=1, source_target_pairs={{0,3},{1,2},{2,1},{3,0},{4,7},{5,6},{6,5},{7,4},{8,11},{9,10},{10,... | collective-permute-start | bytes 417800 | tf_op jit(solution)/shard_map/ppermute | solution.py:322
  10.5 4.3 %collective-permute-start.4 = (bf16[2,272,128]{2,1,0:T(8,128)(2,1)S(1)}, bf16[2,272,128]{2,1,0:T(8,128)(2,1)S(1)}, u32[]{:S(2)}, u32[]{:S(2)}) collective-permute-start(bf16[2,272,128]{2,1,0:T(8,128)(2,1)S(1)} %get-tuple-element.20), channel_id=1, source_target_pairs={{0,1},{1,0},{2,3},{3,2},{4,5},{5,4},{6,7},{7,6},{8,9},{9,8},{10,11... | collective-permute-start | bytes 417800 | tf_op jit(solution)/shard_map/ppermute | solution.py:332
  10.6 6.6 %collective-permute-start.5 = (bf16[2,32,256]{2,1,0:T(8,128)(2,1)S(1)}, bf16[2,32,256]{2,1,0:T(8,128)(2,1)S(1)}, u32[]{:S(2)}, u32[]{:S(2)}) collective-permute-start(bf16[2,32,256]{2,1,0:T(8,128)(2,1)S(1)} %get-tuple-element.24), channel_id=1, source_target_pairs={{0,16},{4,20},{8,24},{12,28},{16,0},{20,4},{24,8},{28,12},{1,17},{... | collective-permute-start | bytes 98312 | tf_op jit(solution)/shard_map/ppermute | solution.py:336
  13.2 5.7 %collective-permute-start.6 = (bf16[2,32,256]{2,1,0:T(8,128)(2,1)S(1)}, bf16[2,32,256]{2,1,0:T(8,128)(2,1)S(1)}, u32[]{:S(2)}, u32[]{:S(2)}) collective-permute-start(bf16[2,32,256]{2,1,0:T(8,128)(2,1)S(1)} %get-tuple-element.25), channel_id=1, source_target_pairs={{0,24},{4,28},{8,16},{12,20},{16,8},{20,12},{24,0},{28,4},{1,25},{... | collective-permute-start | bytes 98312 | tf_op jit(solution)/shard_map/ppermute | solution.py:336
  14.6 4.4 %collective-permute-start.7 = (bf16[2,32,256]{2,1,0:T(8,128)(2,1)S(1)}, bf16[2,32,256]{2,1,0:T(8,128)(2,1)S(1)}, u32[]{:S(2)}, u32[]{:S(2)}) collective-permute-start(bf16[2,32,256]{2,1,0:T(8,128)(2,1)S(1)} %get-tuple-element.26), channel_id=1, source_target_pairs={{0,8},{4,12},{8,0},{12,4},{16,24},{20,28},{24,16},{28,20},{1,9},{5... | collective-permute-start | bytes 98312 | tf_op jit(solution)/shard_map/ppermute | solution.py:336

commit v13 on v12

--- a/solution.py
+++ b/solution.py
@@ -98,11 +98,13 @@
     for copy in smalls:
         copy.wait()
     lane = lax.broadcasted_iota(jnp.int32, (1, width), 1)
+    ones = jnp.ones((PAD, members), BF16)
     for block in range(blocks):
         if block % CHUNK == 0:
             copies[block // CHUNK].wait()
         member = raw[block].astype(F32)
-        mean = jnp.sum(member, axis=0, keepdims=True) / members
+        sums = jnp.dot(ones, raw[block], preferred_element_type=F32)
+        mean = sums[0:1] / members
         pert[block] = (member - mean).astype(BF16)
         weight = jnp.where(lane < count[block], rinv[block : block + 1, :], 0.0)
         gap = weight * (value[block : block + 1, :] - mean)
@@ -174,6 +176,9 @@
 
     def dot(left, right):
         return jnp.dot(left, right, preferred_element_type=F32)
+
+    def advance(tail, lead, factor, rest, cross):
+        return (factor * tail.astype(F32) + lead * rest + cross).astype(BF16), factor * lead
 
     each = range(mine)
     rest, factor, scale, forcing = [], [], [], []
@@ -206,26 +211,35 @@
         level = trace / members
         rest.append((grams - jnp.where(diagonal, level, 0.0)) * (-0.5 / norm))
     small = [rest[p].astype(BF16) for p in each]
-    lead, tail = list(factor), list(small)
+    lead, tail = [None] * mine, [None] * mine
     squares = [dot(small[p], small[p]) for p in each]
-    for step in range(1, ITERS):
-        cubes = [dot(squares[p].astype(BF16), small[p]) for p in each]
+    for step in range(ITERS - 1):
+        cubes, crosses, old = [None] * mine, [None] * mine, []
+        for p in each:
+            square = squares[p].astype(BF16)
+            if step == 0:
+                cubes[p] = dot(square, small[p])
+            else:
+                both = dot(jnp.concatenate([square, tail[p]], axis=0), small[p])
+                cubes[p], crosses[p] = both[:members], both[members:]
         for p in each:
             f = factor[p]
+            old.append((f, rest[p]))
             rest[p] = (
                 (3.0 * f * f - 3.0 * f) * rest[p] + (3.0 * f - 1.5) * squares[p] + cubes[p]
             )
             factor[p] = 1.5 - 1.5 * f * f + f * f * f
-            small[p] = rest[p].astype(BF16)
-        for p in each:
-            narrow = tail[p]
-            if step < ITERS - 1:
-                both = dot(jnp.concatenate([small[p], narrow], axis=0), small[p])
-                squares[p], cross = both[:members], both[members:]
-            else:
-                cross = dot(narrow, small[p])
-            tail[p] = (factor[p] * narrow.astype(F32) + lead[p] * rest[p] + cross).astype(BF16)
-            lead[p] = factor[p] * lead[p]
+            past, small[p] = small[p], rest[p].astype(BF16)
+            if step == 0:
+                lead[p], tail[p] = f, past
+        if step < ITERS - 2:
+            squares = [dot(small[p], small[p]) for p in each]
+        if step > 0:
+            for p in each:
+                tail[p], lead[p] = advance(tail[p], lead[p], *old[p], crosses[p])
+    for p in each:
+        cross = dot(tail[p], small[p])
+        tail[p], lead[p] = advance(tail[p], lead[p], factor[p], rest[p], cross)
     for p in each:
         high = tail[p]
         root_out[p] = high

time: 30.9 us -> 31.2 us (level)
  Pallas kernels: 7.9 us -> 8.61 us
  starting transfers between devices: 9.9 us -> 9.5 us
    pallas_call x1, Pallas kernels: 2.55 us -> 3.27 us  [body(): pl.pallas_call(functools.partial(own_kernel, patches), out_shape=(shape((...]
    ppermute x1, starting transfers between devices: 1.02 us -> 0.31 us  [body(): from_far = lax.ppermute(to_far, 'lon', far)]
    ppermute x1, starting transfers between devices: 0.07 us -> 0.44 us  [body(): from_near = lax.ppermute(to_near, 'lon', near)]
  transfers between devices with their start and end apart: 8 -> 8, of which waited for: 1 -> 1; matrix products, arithmetic and copies ran while one was open for 0% -> 0% of each run, Pallas kernels for 24% -> 26%
where the time goes in v13:
time: 31.2 us; the launch traced here: 31 us
  blocking collectives  10.4 us (33%)
  starting transfers between devices  9.5 us (30%)
  Pallas kernels  8.61 us (28%)
  waiting for transfers between devices  1.74 us (6%)
  local copies, waits for them, and re-layouts  0.67 us (2%)
    all_to_all x1, blocking collectives, body(): lax.all_to_all(updated.reshape(mem_total, local, span), 'mem', split_axis...  10.4 us
    ppermute x3, starting transfers between devices, body(): slabs[i] = lax.ppermute(slabs[i], 'mem', trade)  4.17 us
    pallas_call x1, Pallas kernels, body(): pl.pallas_call(functools.partial(own_kernel, patches), out_shape=(shape((...  3.27 us
    ppermute x1, starting transfers between devices, body(): paired = lax.ppermute(state, 'mem', swap)  2.94 us
    pallas_call x1, Pallas kernels, body(): pl.pallas_call(root_kernel, out_shape=(shape((mine, members, members), BF...  2.39 us
    ppermute x3, waiting for transfers between devices, body(): slabs[i] = lax.ppermute(slabs[i], 'mem', trade)  1.73 us
    ppermute x1, starting transfers between devices, body(): far_pattern = lax.ppermute(pattern, 'lon', far)  1.63 us
    pallas_call x1, Pallas kernels, body(): pl.pallas_call(functools.partial(near_kernel, patches), out_shape=(packed...  1.15 us
  transfers between devices with their start and end apart: 8, of which 1 were waited for; matrix products, arithmetic and copies ran while one was open for 0% of the time, Pallas kernels for 26%

profile of v13, /device:TPU:0, one launch (start us, length us, event | category | flops | bytes accessed | tf_op | source)
XLA Modules:
  0.0 31.0 jit_solution(10348146178581870594)
XLA Ops:
  0.0 2.9 %collective-permute-start.3 = (bf16[32,2048]{1,0:T(8,128)(2,1)}, bf16[32,2048]{1,0:T(8,128)(2,1)S(1)}, u32[]{:S(2)}, u32[]{:S(2)}) collective-permute-start(bf16[32,2048]{1,0:T(8,128)(2,1)} %state.1), channel_id=1, source_target_pairs={{0,4},{4,0},{8,12},{12,8},{16,20},{20,16},{24,28},{28,24},{1,5},{5... | collective-permute-start | bytes 393224 | tf_op jit(solution)/shard_map/ppermute | solution.py:296
  2.9 0.0 copy-start
  2.9 0.0 collective-permute-start.2
  2.9 1.6 %collective-permute-start = (s32[8,16]{1,0:T(8,128)}, s32[8,16]{1,0:T(8,128)S(1)}, u32[]{:S(2)}, u32[]{:S(2)}) collective-permute-start(s32[8,16]{1,0:T(8,128)} %bitcast.8), channel_id=1, source_target_pairs={{0,3},{1,2},{2,1},{3,0},{4,7},{5,6},{6,5},{7,4},{8,11},{9,10},{10,... | collective-permute-start | bytes 1544 | tf_op jit(solution)/shard_map/ppermute | solution.py:294
  4.6 3.3 %own_share.1 = (bf16[32,256,128]{2,1,0:T(8,128)(2,1)S(1)}, f32[32,128]{1,0:T(8,128)S(1)}, f32[32,128]{1,0:T(8,128)S(1)}, f32[2,272,256]{2,1,0:T(8,128)S(1)}) custom-call(s32[32]{0:T(128)} %count_all.1, s32[8,16]{1,0:T(8,128)} %bitcast.9, bf16[32,256,128]{2,1,0:T(8,128)(2,1)} %hx.1, f32[32,128]{1,0:T(8,128)} %value_all.1, f32[32,128]{1,0:T(8,128)} %rinv_all.1), custom_call_target="tpu_custom_call" | custom-call | flops 289406976 | bytes 4194304 | tf_op jit(solution)/shard_map/own_share/pallas_call | solution.py:299
  7.9 0.0 collective-permute-done.pattern
  7.9 1.1 %far_share.1.sent = bf16[2,272,128]{2,1,0:T(8,128)(2,1)S(1)} custom-call(s32[8,16]{1,0:T(8,128)S(1)} %collective-permute-done.pattern, bf16[32,256,128]{2,1,0:T(8,128)(2,1)S(1)} %get-tuple-element.17.pert, f32[32,128]{1,0:T(8,128)S(1)} %get-tuple-element.18.weights, f32[32,128]{1,0:T(8,128)S(1)} %get-tuple-element.19.innov), custom_call_target="tpu_custom_call" | custom-call | flops 285212672 | bytes 1048576 | tf_op jit(solution)/shard_map/far_share/pallas_call | solution.py:327
  9.0 0.3 %collective-permute-start.1 = (bf16[2,272,128]{2,1,0:T(8,128)(2,1)S(1)}, bf16[2,272,128]{2,1,0:T(8,128)(2,1)S(1)}, u32[]{:S(2)}, u32[]{:S(2)}) collective-permute-start(bf16[2,272,128]{2,1,0:T(8,128)(2,1)S(1)} %far_share.1.sent), channel_id=1, source_target_pairs={{0,3},{1,2},{2,1},{3,0},{4,7},{5,6},{6,5},{7,4},{8,11},{9,10},{10,... | collective-permute-start | bytes 417800 | tf_op jit(solution)/shard_map/ppermute | solution.py:336
  9.3 0.0 collective-permute-done.2.pattern
  9.3 0.0 collective-permute-done.3.paired
  9.3 0.0 copy-done
  9.3 1.2 %near_share.1 = (bf16[2,272,128]{2,1,0:T(8,128)(2,1)S(1)}, bf16[2,32,256]{2,1,0:T(8,128)(2,1)S(1)}, bf16[2,32,256]{2,1,0:T(8,128)(2,1)S(1)}, bf16[2,32,256]{2,1,0:T(8,128)(2,1)S(1)}, bf16[2,32,256]{2,1,0:T(8,128)(2,1)S(1)}) custom-call(s32[8,16]{1,0:T(8,128)S(1)} %collective-permute-done.2.pattern, bf16[32,256,128]{2,1,0:T(8,128)(2,1)S(1)} %get-tuple-element.17.pert, ...), custom_call_target="tpu_custom_call" | custom-call | flops 285212672 | bytes 1048576 | tf_op jit(solution)/shard_map/near_share/pallas_call | solution.py:337
  10.5 0.4 %collective-permute-start.4 = (bf16[2,272,128]{2,1,0:T(8,128)(2,1)S(1)}, bf16[2,272,128]{2,1,0:T(8,128)(2,1)S(1)}, u32[]{:S(2)}, u32[]{:S(2)}) collective-permute-start(bf16[2,272,128]{2,1,0:T(8,128)(2,1)S(1)} %get-tuple-element.20), channel_id=1, source_target_pairs={{0,1},{1,0},{2,3},{3,2},{4,5},{5,4},{6,7},{7,6},{8,9},{9,8},{10,11... | collective-permute-start | bytes 417800 | tf_op jit(solution)/shard_map/ppermute | solution.py:346
  10.9 2.6 %collective-permute-start.5 = (bf16[2,32,256]{2,1,0:T(8,128)(2,1)S(1)}, bf16[2,32,256]{2,1,0:T(8,128)(2,1)S(1)}, u32[]{:S(2)}, u32[]{:S(2)}) collective-permute-start(bf16[2,32,256]{2,1,0:T(8,128)(2,1)S(1)} %get-tuple-element.24), channel_id=1, source_target_pairs={{0,16},{4,20},{8,24},{12,28},{16,0},{20,4},{24,8},{28,12},{1,17},{... | collective-permute-start | bytes 98312 | tf_op jit(solution)/shard_map/ppermute | solution.py:350
  13.5 1.3 %collective-permute-start.6 = (bf16[2,32,256]{2,1,0:T(8,128)(2,1)S(1)}, bf16[2,32,256]{2,1,0:T(8,128)(2,1)S(1)}, u32[]{:S(2)}, u32[]{:S(2)}) collective-permute-start(bf16[2,32,256]{2,1,0:T(8,128)(2,1)S(1)} %get-tuple-element.25), channel_id=1, source_target_pairs={{0,24},{4,28},{8,16},{12,20},{16,8},{20,12},{24,0},{28,4},{1,25},{... | collective-permute-start | bytes 98312 | tf_op jit(solution)/shard_map/ppermute | solution.py:350
  14.9 0.2 collective-permute-start.7
  15.1 0.0 collective-permute-done.1.before
  15.1 0.0 collective-permute-done.4.after
  15.1 2.4 %root.1 = (bf16[2,256,256]{2,1,0:T(8,128)(2,1)S(1)}, f32[2,16,256]{2,1,0:T(8,128)S(1)}) custom-call(f32[2,272,256]{2,1,0:T(8,128)S(1)} %get-tuple-element.16.own, bf16[2,272,128]{2,1,0:T(8,128)(2,1)S(1)} %collective-permute-done.1.before, bf16[2,272,128]{2,1,0:T(8,128)(2,1)S(1)} %collective-permute-done.4.after), custom_call_target="tpu_custom_call" | custom-call | flops 1006632960 | bytes 1048576 | tf_op jit(solution)/shard_map/root/pallas_call | solution.py:351
  17.5 0.0 collective-permute-done.5.rest_1_
  17.5 1.7 %collective-permute-done.6.rest_2_ = bf16[2,32,256]{2,1,0:T(8,128)(2,1)S(1)} collective-permute-done((bf16[2,32,256]{2,1,0:T(8,128)(2,1)S(1)}, bf16[2,32,256]{2,1,0:T(8,128)(2,1)S(1)}, u32[]{:S(2)}, u32[]{:S(2)}) %collective-permute-start.6) | collective-permute-done | bytes 32800 | tf_op jit(solution)/shard_map/ppermute | solution.py:350
  19.2 0.0 collective-permute-done.7.rest_3_
  19.2 0.7 %apply.1 = bf16[256,256]{1,0:T(8,128)(2,1)S(1)} custom-call(bf16[2,256,256]{2,1,0:T(8,128)(2,1)S(1)} %get-tuple-element.21.root, f32[2,16,256]{2,1,0:T(8,128)S(1)} %get-tuple-element.22.rows, bf16[2,32,256]{2,1,0:T(8,128)(2,1)S(1)} %get-tuple-element.23.rest_0_, bf16[2,32,256]{2,1,0:T(8,128)(2,1)S(1)} %collective-permute-done.5.rest_1_, ...), custom_call_target="tpu_custom_call" | custom-call | flops 33554432 | bytes 524288 | tf_op jit(solution)/shard_map/apply/pallas_call | solution.py:362
  19.9 10.4 %all_to_all.5 = bf16[8,32,256]{2,1,0:T(8,128)(2,1)S(1)} all-to-all(bf16[8,32,256]{2,1,0:T(8,128)(2,1)S(1)} %bitcast.5), channel_id=1, replica_groups=mesh['mem'=8,'lon'=4] {'mem'}, dimensions={0} | all-to-all | bytes 262144 | tf_op jit(solution)/shard_map/all_to_all | solution.py:374
  30.3 0.7 %copy.8 = bf16[8,4,8,256]{3,2,0,1:T(8,128)(2,1)} copy(bf16[8,4,8,256]{3,2,1,0:T(8,128)(2,1)S(1)} %bitcast.6) | data formatting | bytes 262144 | tf_op jit(solution)/shard_map/reshape | solution.py:377
Async XLA Ops:
  0.0 9.3 %collective-permute-start.3 = (bf16[32,2048]{1,0:T(8,128)(2,1)}, bf16[32,2048]{1,0:T(8,128)(2,1)S(1)}, u32[]{:S(2)}, u32[]{:S(2)}) collective-permute-start(bf16[32,2048]{1,0:T(8,128)(2,1)} %state.1), channel_id=1, source_target_pairs={{0,4},{4,0},{8,12},{12,8},{16,20},{20,16},{24,28},{28,24},{1,5},{5... | collective-permute-start | bytes 393224 | tf_op jit(solution)/shard_map/ppermute | solution.py:296
  2.9 6.4 %copy-start = (bf16[32,2048]{1,0:T(8,128)(2,1)S(1)}, bf16[32,2048]{1,0:T(8,128)(2,1)}, u32[]{:S(2)}) copy-start(bf16[32,2048]{1,0:T(8,128)(2,1)} %state.1) | copy-start | bytes 393220
  2.9 6.4 %collective-permute-start.2 = (s32[8,16]{1,0:T(8,128)}, s32[8,16]{1,0:T(8,128)S(1)}, u32[]{:S(2)}, u32[]{:S(2)}) collective-permute-start(s32[8,16]{1,0:T(8,128)} %bitcast.7), channel_id=1, source_target_pairs={{0,1},{1,0},{2,3},{3,2},{4,5},{5,4},{6,7},{7,6},{8,9},{9,8},{10,11... | collective-permute-start | bytes 1544 | tf_op jit(solution)/shard_map/ppermute | solution.py:295
  2.9 4.9 %collective-permute-start = (s32[8,16]{1,0:T(8,128)}, s32[8,16]{1,0:T(8,128)S(1)}, u32[]{:S(2)}, u32[]{:S(2)}) collective-permute-start(s32[8,16]{1,0:T(8,128)} %bitcast.8), channel_id=1, source_target_pairs={{0,3},{1,2},{2,1},{3,0},{4,7},{5,6},{6,5},{7,4},{8,11},{9,10},{10,... | collective-permute-start | bytes 1544 | tf_op jit(solution)/shard_map/ppermute | solution.py:294
  9.0 6.1 %collective-permute-start.1 = (bf16[2,272,128]{2,1,0:T(8,128)(2,1)S(1)}, bf16[2,272,128]{2,1,0:T(8,128)(2,1)S(1)}, u32[]{:S(2)}, u32[]{:S(2)}) collective-permute-start(bf16[2,272,128]{2,1,0:T(8,128)(2,1)S(1)} %far_share.1.sent), channel_id=1, source_target_pairs={{0,3},{1,2},{2,1},{3,0},{4,7},{5,6},{6,5},{7,4},{8,11},{9,10},{10,... | collective-permute-start | bytes 417800 | tf_op jit(solution)/shard_map/ppermute | solution.py:336
  10.5 4.6 %collective-permute-start.4 = (bf16[2,272,128]{2,1,0:T(8,128)(2,1)S(1)}, bf16[2,272,128]{2,1,0:T(8,128)(2,1)S(1)}, u32[]{:S(2)}, u32[]{:S(2)}) collective-permute-start(bf16[2,272,128]{2,1,0:T(8,128)(2,1)S(1)} %get-tuple-element.20), channel_id=1, source_target_pairs={{0,1},{1,0},{2,3},{3,2},{4,5},{5,4},{6,7},{7,6},{8,9},{9,8},{10,11... | collective-permute-start | bytes 417800 | tf_op jit(solution)/shard_map/ppermute | solution.py:346
  10.9 6.6 %collective-permute-start.5 = (bf16[2,32,256]{2,1,0:T(8,128)(2,1)S(1)}, bf16[2,32,256]{2,1,0:T(8,128)(2,1)S(1)}, u32[]{:S(2)}, u32[]{:S(2)}) collective-permute-start(bf16[2,32,256]{2,1,0:T(8,128)(2,1)S(1)} %get-tuple-element.24), channel_id=1, source_target_pairs={{0,16},{4,20},{8,24},{12,28},{16,0},{20,4},{24,8},{28,12},{1,17},{... | collective-permute-start | bytes 98312 | tf_op jit(solution)/shard_map/ppermute | solution.py:350
  13.5 5.7 %collective-permute-start.6 = (bf16[2,32,256]{2,1,0:T(8,128)(2,1)S(1)}, bf16[2,32,256]{2,1,0:T(8,128)(2,1)S(1)}, u32[]{:S(2)}, u32[]{:S(2)}) collective-permute-start(bf16[2,32,256]{2,1,0:T(8,128)(2,1)S(1)} %get-tuple-element.25), channel_id=1, source_target_pairs={{0,24},{4,28},{8,16},{12,20},{16,8},{20,12},{24,0},{28,4},{1,25},{... | collective-permute-start | bytes 98312 | tf_op jit(solution)/shard_map/ppermute | solution.py:350
  14.9 4.4 %collective-permute-start.7 = (bf16[2,32,256]{2,1,0:T(8,128)(2,1)S(1)}, bf16[2,32,256]{2,1,0:T(8,128)(2,1)S(1)}, u32[]{:S(2)}, u32[]{:S(2)}) collective-permute-start(bf16[2,32,256]{2,1,0:T(8,128)(2,1)S(1)} %get-tuple-element.26), channel_id=1, source_target_pairs={{0,8},{4,12},{8,0},{12,4},{16,24},{20,28},{24,16},{28,20},{1,9},{5... | collective-permute-start | bytes 98312 | tf_op jit(solution)/shard_map/ppermute | solution.py:350

commit v14 on v12

--- a/solution.py
+++ b/solution.py
@@ -9,7 +9,7 @@
 
 ITERS = 6
 PAD = 16
-CHUNK = 4
+CHUNK = 8
 PAIR = 2
 F32 = jnp.float32
 BF16 = jnp.bfloat16
@@ -102,7 +102,7 @@
         if block % CHUNK == 0:
             copies[block // CHUNK].wait()
         member = raw[block].astype(F32)
-        mean = jnp.sum(member, axis=0, keepdims=True) / members
+        mean = jnp.sum(member, axis=0, keepdims=True) * (1.0 / members)
         pert[block] = (member - mean).astype(BF16)
         weight = jnp.where(lane < count[block], rinv[block : block + 1, :], 0.0)
         gap = weight * (value[block : block + 1, :] - mean)

time: 30.9 us -> 30.9 us (level)
  transfers between devices with their start and end apart: 8 -> 8, of which waited for: 1 -> 1; matrix products, arithmetic and copies ran while one was open for 0% -> 0% of each run, Pallas kernels for 24% -> 23%
where the time goes in v14:
time: 30.9 us; the launch traced here: 30.7 us
  blocking collectives  10.4 us (34%)
  starting transfers between devices  10.1 us (33%)
  Pallas kernels  7.66 us (25%)
  waiting for transfers between devices  1.76 us (6%)
  local copies, waits for them, and re-layouts  0.67 us (2%)
    all_to_all x1, blocking collectives, body(): lax.all_to_all(updated.reshape(mem_total, local, span), 'mem', split_axis...  10.4 us
    ppermute x3, starting transfers between devices, body(): slabs[i] = lax.ppermute(slabs[i], 'mem', trade)  4.23 us
    ppermute x1, starting transfers between devices, body(): paired = lax.ppermute(state, 'mem', swap)  2.94 us
    pallas_call x1, Pallas kernels, body(): pl.pallas_call(root_kernel, out_shape=(shape((mine, members, members), BF...  2.39 us
    pallas_call x1, Pallas kernels, body(): pl.pallas_call(functools.partial(own_kernel, patches), out_shape=(shape((...  2.31 us
    ppermute x3, waiting for transfers between devices, body(): slabs[i] = lax.ppermute(slabs[i], 'mem', trade)  1.74 us
    ppermute x1, starting transfers between devices, body(): far_pattern = lax.ppermute(pattern, 'lon', far)  1.63 us
    ppermute x1, starting transfers between devices, body(): from_far = lax.ppermute(to_far, 'lon', far)  1.27 us
  transfers between devices with their start and end apart: 8, of which 1 were waited for; matrix products, arithmetic and copies ran while one was open for 0% of the time, Pallas kernels for 23%

profile of v14, /device:TPU:0, one launch (start us, length us, event | category | flops | bytes accessed | tf_op | source)
XLA Modules:
  0.0 30.7 jit_solution(5117877577167376564)
XLA Ops:
  0.0 2.9 %collective-permute-start.3 = (bf16[32,2048]{1,0:T(8,128)(2,1)}, bf16[32,2048]{1,0:T(8,128)(2,1)S(1)}, u32[]{:S(2)}, u32[]{:S(2)}) collective-permute-start(bf16[32,2048]{1,0:T(8,128)(2,1)} %state.1), channel_id=1, source_target_pairs={{0,4},{4,0},{8,12},{12,8},{16,20},{20,16},{24,28},{28,24},{1,5},{5... | collective-permute-start | bytes 393224 | tf_op jit(solution)/shard_map/ppermute | solution.py:282
  2.9 0.0 copy-start
  2.9 0.0 collective-permute-start.2
  2.9 1.6 %collective-permute-start = (s32[8,16]{1,0:T(8,128)}, s32[8,16]{1,0:T(8,128)S(1)}, u32[]{:S(2)}, u32[]{:S(2)}) collective-permute-start(s32[8,16]{1,0:T(8,128)} %bitcast.8), channel_id=1, source_target_pairs={{0,3},{1,2},{2,1},{3,0},{4,7},{5,6},{6,5},{7,4},{8,11},{9,10},{10,... | collective-permute-start | bytes 1544 | tf_op jit(solution)/shard_map/ppermute | solution.py:280
  4.6 2.3 %own_share.1 = (bf16[32,256,128]{2,1,0:T(8,128)(2,1)S(1)}, f32[32,128]{1,0:T(8,128)S(1)}, f32[32,128]{1,0:T(8,128)S(1)}, f32[2,272,256]{2,1,0:T(8,128)S(1)}) custom-call(s32[32]{0:T(128)} %count_all.1, s32[8,16]{1,0:T(8,128)} %bitcast.9, bf16[32,256,128]{2,1,0:T(8,128)(2,1)} %hx.1, f32[32,128]{1,0:T(8,128)} %value_all.1, f32[32,128]{1,0:T(8,128)} %rinv_all.1), custom_call_target="tpu_custom_call" | custom-call | flops 289406976 | bytes 4194304 | tf_op jit(solution)/shard_map/own_share/pallas_call | solution.py:285
  6.9 0.0 collective-permute-done.pattern
  6.9 1.1 %far_share.1.sent = bf16[2,272,128]{2,1,0:T(8,128)(2,1)S(1)} custom-call(s32[8,16]{1,0:T(8,128)S(1)} %collective-permute-done.pattern, bf16[32,256,128]{2,1,0:T(8,128)(2,1)S(1)} %get-tuple-element.17.pert, f32[32,128]{1,0:T(8,128)S(1)} %get-tuple-element.18.weights, f32[32,128]{1,0:T(8,128)S(1)} %get-tuple-element.19.innov), custom_call_target="tpu_custom_call" | custom-call | flops 285212672 | bytes 1048576 | tf_op jit(solution)/shard_map/far_share/pallas_call | solution.py:313
  8.0 1.3 %collective-permute-start.1 = (bf16[2,272,128]{2,1,0:T(8,128)(2,1)S(1)}, bf16[2,272,128]{2,1,0:T(8,128)(2,1)S(1)}, u32[]{:S(2)}, u32[]{:S(2)}) collective-permute-start(bf16[2,272,128]{2,1,0:T(8,128)(2,1)S(1)} %far_share.1.sent), channel_id=1, source_target_pairs={{0,3},{1,2},{2,1},{3,0},{4,7},{5,6},{6,5},{7,4},{8,11},{9,10},{10,... | collective-permute-start | bytes 417800 | tf_op jit(solution)/shard_map/ppermute | solution.py:322
  9.3 0.0 collective-permute-done.2.pattern
  9.3 0.0 collective-permute-done.3.paired
  9.3 0.0 copy-done
  9.3 1.2 %near_share.1 = (bf16[2,272,128]{2,1,0:T(8,128)(2,1)S(1)}, bf16[2,32,256]{2,1,0:T(8,128)(2,1)S(1)}, bf16[2,32,256]{2,1,0:T(8,128)(2,1)S(1)}, bf16[2,32,256]{2,1,0:T(8,128)(2,1)S(1)}, bf16[2,32,256]{2,1,0:T(8,128)(2,1)S(1)}) custom-call(s32[8,16]{1,0:T(8,128)S(1)} %collective-permute-done.2.pattern, bf16[32,256,128]{2,1,0:T(8,128)(2,1)S(1)} %get-tuple-element.17.pert, ...), custom_call_target="tpu_custom_call" | custom-call | flops 285212672 | bytes 1048576 | tf_op jit(solution)/shard_map/near_share/pallas_call | solution.py:323
  10.5 0.1 collective-permute-start.4
  10.6 2.7 %collective-permute-start.5 = (bf16[2,32,256]{2,1,0:T(8,128)(2,1)S(1)}, bf16[2,32,256]{2,1,0:T(8,128)(2,1)S(1)}, u32[]{:S(2)}, u32[]{:S(2)}) collective-permute-start(bf16[2,32,256]{2,1,0:T(8,128)(2,1)S(1)} %get-tuple-element.24), channel_id=1, source_target_pairs={{0,16},{4,20},{8,24},{12,28},{16,0},{20,4},{24,8},{28,12},{1,17},{... | collective-permute-start | bytes 98312 | tf_op jit(solution)/shard_map/ppermute | solution.py:336
  13.2 1.3 %collective-permute-start.6 = (bf16[2,32,256]{2,1,0:T(8,128)(2,1)S(1)}, bf16[2,32,256]{2,1,0:T(8,128)(2,1)S(1)}, u32[]{:S(2)}, u32[]{:S(2)}) collective-permute-start(bf16[2,32,256]{2,1,0:T(8,128)(2,1)S(1)} %get-tuple-element.25), channel_id=1, source_target_pairs={{0,24},{4,28},{8,16},{12,20},{16,8},{20,12},{24,0},{28,4},{1,25},{... | collective-permute-start | bytes 98312 | tf_op jit(solution)/shard_map/ppermute | solution.py:336
  14.6 0.2 collective-permute-start.7
  14.8 0.0 collective-permute-done.1.before
  14.8 0.0 collective-permute-done.4.after
  14.8 2.4 %root.1 = (bf16[2,256,256]{2,1,0:T(8,128)(2,1)S(1)}, f32[2,16,256]{2,1,0:T(8,128)S(1)}) custom-call(f32[2,272,256]{2,1,0:T(8,128)S(1)} %get-tuple-element.16.own, bf16[2,272,128]{2,1,0:T(8,128)(2,1)S(1)} %collective-permute-done.1.before, bf16[2,272,128]{2,1,0:T(8,128)(2,1)S(1)} %collective-permute-done.4.after), custom_call_target="tpu_custom_call" | custom-call | flops 1006632960 | bytes 1048576 | tf_op jit(solution)/shard_map/root/pallas_call | solution.py:337
  17.2 0.0 collective-permute-done.5.rest_1_
  17.2 1.7 %collective-permute-done.6.rest_2_ = bf16[2,32,256]{2,1,0:T(8,128)(2,1)S(1)} collective-permute-done((bf16[2,32,256]{2,1,0:T(8,128)(2,1)S(1)}, bf16[2,32,256]{2,1,0:T(8,128)(2,1)S(1)}, u32[]{:S(2)}, u32[]{:S(2)}) %collective-permute-start.6) | collective-permute-done | bytes 32800 | tf_op jit(solution)/shard_map/ppermute | solution.py:336
  18.9 0.0 collective-permute-done.7.rest_3_
  18.9 0.7 %apply.1 = bf16[256,256]{1,0:T(8,128)(2,1)S(1)} custom-call(bf16[2,256,256]{2,1,0:T(8,128)(2,1)S(1)} %get-tuple-element.21.root, f32[2,16,256]{2,1,0:T(8,128)S(1)} %get-tuple-element.22.rows, bf16[2,32,256]{2,1,0:T(8,128)(2,1)S(1)} %get-tuple-element.23.rest_0_, bf16[2,32,256]{2,1,0:T(8,128)(2,1)S(1)} %collective-permute-done.5.rest_1_, ...), custom_call_target="tpu_custom_call" | custom-call | flops 33554432 | bytes 524288 | tf_op jit(solution)/shard_map/apply/pallas_call | solution.py:348
  19.6 10.4 %all_to_all.5 = bf16[8,32,256]{2,1,0:T(8,128)(2,1)S(1)} all-to-all(bf16[8,32,256]{2,1,0:T(8,128)(2,1)S(1)} %bitcast.5), channel_id=1, replica_groups=mesh['mem'=8,'lon'=4] {'mem'}, dimensions={0} | all-to-all | bytes 262144 | tf_op jit(solution)/shard_map/all_to_all | solution.py:360
  30.0 0.7 %copy.8 = bf16[8,4,8,256]{3,2,0,1:T(8,128)(2,1)} copy(bf16[8,4,8,256]{3,2,1,0:T(8,128)(2,1)S(1)} %bitcast.6) | data formatting | bytes 262144 | tf_op jit(solution)/shard_map/reshape | solution.py:363
Async XLA Ops:
  0.0 9.3 %collective-permute-start.3 = (bf16[32,2048]{1,0:T(8,128)(2,1)}, bf16[32,2048]{1,0:T(8,128)(2,1)S(1)}, u32[]{:S(2)}, u32[]{:S(2)}) collective-permute-start(bf16[32,2048]{1,0:T(8,128)(2,1)} %state.1), channel_id=1, source_target_pairs={{0,4},{4,0},{8,12},{12,8},{16,20},{20,16},{24,28},{28,24},{1,5},{5... | collective-permute-start | bytes 393224 | tf_op jit(solution)/shard_map/ppermute | solution.py:282
  2.9 6.4 %copy-start = (bf16[32,2048]{1,0:T(8,128)(2,1)S(1)}, bf16[32,2048]{1,0:T(8,128)(2,1)}, u32[]{:S(2)}) copy-start(bf16[32,2048]{1,0:T(8,128)(2,1)} %state.1) | copy-start | bytes 393220
  2.9 6.4 %collective-permute-start.2 = (s32[8,16]{1,0:T(8,128)}, s32[8,16]{1,0:T(8,128)S(1)}, u32[]{:S(2)}, u32[]{:S(2)}) collective-permute-start(s32[8,16]{1,0:T(8,128)} %bitcast.7), channel_id=1, source_target_pairs={{0,1},{1,0},{2,3},{3,2},{4,5},{5,4},{6,7},{7,6},{8,9},{9,8},{10,11... | collective-permute-start | bytes 1544 | tf_op jit(solution)/shard_map/ppermute | solution.py:281
  2.9 4.0 %collective-permute-start = (s32[8,16]{1,0:T(8,128)}, s32[8,16]{1,0:T(8,128)S(1)}, u32[]{:S(2)}, u32[]{:S(2)}) collective-permute-start(s32[8,16]{1,0:T(8,128)} %bitcast.8), channel_id=1, source_target_pairs={{0,3},{1,2},{2,1},{3,0},{4,7},{5,6},{6,5},{7,4},{8,11},{9,10},{10,... | collective-permute-start | bytes 1544 | tf_op jit(solution)/shard_map/ppermute | solution.py:280
  8.0 6.7 %collective-permute-start.1 = (bf16[2,272,128]{2,1,0:T(8,128)(2,1)S(1)}, bf16[2,272,128]{2,1,0:T(8,128)(2,1)S(1)}, u32[]{:S(2)}, u32[]{:S(2)}) collective-permute-start(bf16[2,272,128]{2,1,0:T(8,128)(2,1)S(1)} %far_share.1.sent), channel_id=1, source_target_pairs={{0,3},{1,2},{2,1},{3,0},{4,7},{5,6},{6,5},{7,4},{8,11},{9,10},{10,... | collective-permute-start | bytes 417800 | tf_op jit(solution)/shard_map/ppermute | solution.py:322
  10.5 4.3 %collective-permute-start.4 = (bf16[2,272,128]{2,1,0:T(8,128)(2,1)S(1)}, bf16[2,272,128]{2,1,0:T(8,128)(2,1)S(1)}, u32[]{:S(2)}, u32[]{:S(2)}) collective-permute-start(bf16[2,272,128]{2,1,0:T(8,128)(2,1)S(1)} %get-tuple-element.20), channel_id=1, source_target_pairs={{0,1},{1,0},{2,3},{3,2},{4,5},{5,4},{6,7},{7,6},{8,9},{9,8},{10,11... | collective-permute-start | bytes 417800 | tf_op jit(solution)/shard_map/ppermute | solution.py:332
  10.6 6.6 %collective-permute-start.5 = (bf16[2,32,256]{2,1,0:T(8,128)(2,1)S(1)}, bf16[2,32,256]{2,1,0:T(8,128)(2,1)S(1)}, u32[]{:S(2)}, u32[]{:S(2)}) collective-permute-start(bf16[2,32,256]{2,1,0:T(8,128)(2,1)S(1)} %get-tuple-element.24), channel_id=1, source_target_pairs={{0,16},{4,20},{8,24},{12,28},{16,0},{20,4},{24,8},{28,12},{1,17},{... | collective-permute-start | bytes 98312 | tf_op jit(solution)/shard_map/ppermute | solution.py:336
  13.2 5.7 %collective-permute-start.6 = (bf16[2,32,256]{2,1,0:T(8,128)(2,1)S(1)}, bf16[2,32,256]{2,1,0:T(8,128)(2,1)S(1)}, u32[]{:S(2)}, u32[]{:S(2)}) collective-permute-start(bf16[2,32,256]{2,1,0:T(8,128)(2,1)S(1)} %get-tuple-element.25), channel_id=1, source_target_pairs={{0,24},{4,28},{8,16},{12,20},{16,8},{20,12},{24,0},{28,4},{1,25},{... | collective-permute-start | bytes 98312 | tf_op jit(solution)/shard_map/ppermute | solution.py:336
  14.6 4.4 %collective-permute-start.7 = (bf16[2,32,256]{2,1,0:T(8,128)(2,1)S(1)}, bf16[2,32,256]{2,1,0:T(8,128)(2,1)S(1)}, u32[]{:S(2)}, u32[]{:S(2)}) collective-permute-start(bf16[2,32,256]{2,1,0:T(8,128)(2,1)S(1)} %get-tuple-element.26), channel_id=1, source_target_pairs={{0,8},{4,12},{8,0},{12,4},{16,24},{20,28},{24,16},{28,20},{1,9},{5... | collective-permute-start | bytes 98312 | tf_op jit(solution)/shard_map/ppermute | solution.py:336

commit v15 on v14

--- a/solution.py
+++ b/solution.py
@@ -239,7 +239,7 @@
 def apply_kernel(root, rows, *rest):
     slabs, (out, columns) = rest[:-2], rest[-2:]
     mine, members, _ = root.shape
-    points = out.shape[1] // mine
+    points = out.shape[3]
     length = len(slabs)
     _, local, _ = slabs[0].shape
     for shift, slab in zip(turns(length), slabs):
@@ -256,7 +256,8 @@
             root[p], deviation.astype(BF16), preferred_element_type=F32
         )
         shift = mean + product(split(rows[p]), split(spread))[0:1]
-        out[:, cols] = (shift + rows[p, 2:3, :points] * spread).astype(BF16)
+        result = (shift + rows[p, 2:3, :points] * spread).astype(BF16)
+        out[:, p] = result.reshape(out.shape[0], local, points)
 
 
 def body(state, hx, obs_value, obs_rinv, obs_count, loc_pattern):
@@ -347,7 +348,7 @@
     )(own, from_far, from_near)
     updated = pl.pallas_call(
         apply_kernel,
-        out_shape=shape((members, span), BF16),
+        out_shape=shape((mem_total, mine, local, span // mine), BF16),
         in_specs=[VMEM] * (2 + length),
         out_specs=VMEM,
         scratch_shapes=[pltpu.VMEM((members, span), BF16)],
@@ -357,10 +358,8 @@
         ),
         name="apply",
     )(root, rows, *slabs)
-    pieces = lax.all_to_all(
-        updated.reshape(mem_total, local, span), "mem", split_axis=0, concat_axis=0
-    )
-    return jnp.swapaxes(pieces, 0, 1).reshape(local, points)
+    pieces = lax.all_to_all(updated, "mem", split_axis=0, concat_axis=0)
+    return jnp.transpose(pieces, (2, 0, 1, 3)).reshape(local, points)
 
 
 def solution(mesh):

time: 30.9 us -> 31.1 us (level)
  no operation moved by 1% of the time
where the time goes in v15:
time: 31.1 us; the launch traced here: 30.9 us
  blocking collectives  10.4 us (33%)
  starting transfers between devices  10.1 us (32%)
  Pallas kernels  7.65 us (25%)
  waiting for transfers between devices  1.76 us (6%)
  local copies, waits for them, and re-layouts  0.84 us (3%)
    all_to_all x1, blocking collectives, body(): pieces = lax.all_to_all(updated, 'mem', split_axis=0, concat_axis=0)  10.4 us
    ppermute x3, starting transfers between devices, body(): slabs[i] = lax.ppermute(slabs[i], 'mem', trade)  4.22 us
    ppermute x1, starting transfers between devices, body(): paired = lax.ppermute(state, 'mem', swap)  2.94 us
    pallas_call x1, Pallas kernels, body(): pl.pallas_call(root_kernel, out_shape=(shape((mine, members, members), BF...  2.38 us
    pallas_call x1, Pallas kernels, body(): pl.pallas_call(functools.partial(own_kernel, patches), out_shape=(shape((...  2.31 us
    ppermute x3, waiting for transfers between devices, body(): slabs[i] = lax.ppermute(slabs[i], 'mem', trade)  1.75 us
    ppermute x1, starting transfers between devices, body(): far_pattern = lax.ppermute(pattern, 'lon', far)  1.63 us
    ppermute x1, starting transfers between devices, body(): from_far = lax.ppermute(to_far, 'lon', far)  1.27 us
  transfers between devices with their start and end apart: 8, of which 1 were waited for; matrix products, arithmetic and copies ran while one was open for 0% of the time, Pallas kernels for 23%

profile of v15, /device:TPU:0, one launch (start us, length us, event | category | flops | bytes accessed | tf_op | source)
XLA Modules:
  0.0 30.9 jit_solution(14744089882601259222)
XLA Ops:
  0.0 2.9 %collective-permute-start.3 = (bf16[32,2048]{1,0:T(8,128)(2,1)}, bf16[32,2048]{1,0:T(8,128)(2,1)S(1)}, u32[]{:S(2)}, u32[]{:S(2)}) collective-permute-start(bf16[32,2048]{1,0:T(8,128)(2,1)} %state.1), channel_id=1, source_target_pairs={{0,4},{4,0},{8,12},{12,8},{16,20},{20,16},{24,28},{28,24},{1,5},{5... | collective-permute-start | bytes 393224 | tf_op jit(solution)/shard_map/ppermute | solution.py:283
  2.9 0.0 copy-start
  2.9 0.0 collective-permute-start.2
  2.9 1.6 %collective-permute-start = (s32[8,16]{1,0:T(8,128)}, s32[8,16]{1,0:T(8,128)S(1)}, u32[]{:S(2)}, u32[]{:S(2)}) collective-permute-start(s32[8,16]{1,0:T(8,128)} %bitcast.4), channel_id=1, source_target_pairs={{0,3},{1,2},{2,1},{3,0},{4,7},{5,6},{6,5},{7,4},{8,11},{9,10},{10,... | collective-permute-start | bytes 1544 | tf_op jit(solution)/shard_map/ppermute | solution.py:281
  4.6 2.3 %own_share.1 = (bf16[32,256,128]{2,1,0:T(8,128)(2,1)S(1)}, f32[32,128]{1,0:T(8,128)S(1)}, f32[32,128]{1,0:T(8,128)S(1)}, f32[2,272,256]{2,1,0:T(8,128)S(1)}) custom-call(s32[32]{0:T(128)} %count_all.1, s32[8,16]{1,0:T(8,128)} %bitcast.5, bf16[32,256,128]{2,1,0:T(8,128)(2,1)} %hx.1, f32[32,128]{1,0:T(8,128)} %value_all.1, f32[32,128]{1,0:T(8,128)} %rinv_all.1), custom_call_target="tpu_custom_call" | custom-call | flops 289406976 | bytes 4194304 | tf_op jit(solution)/shard_map/own_share/pallas_call | solution.py:286
  6.9 0.0 collective-permute-done.pattern
  6.9 1.1 %far_share.1.sent = bf16[2,272,128]{2,1,0:T(8,128)(2,1)S(1)} custom-call(s32[8,16]{1,0:T(8,128)S(1)} %collective-permute-done.pattern, bf16[32,256,128]{2,1,0:T(8,128)(2,1)S(1)} %get-tuple-element.17.pert, f32[32,128]{1,0:T(8,128)S(1)} %get-tuple-element.18.weights, f32[32,128]{1,0:T(8,128)S(1)} %get-tuple-element.19.innov), custom_call_target="tpu_custom_call" | custom-call | flops 285212672 | bytes 1048576 | tf_op jit(solution)/shard_map/far_share/pallas_call | solution.py:314
  8.0 1.3 %collective-permute-start.1 = (bf16[2,272,128]{2,1,0:T(8,128)(2,1)S(1)}, bf16[2,272,128]{2,1,0:T(8,128)(2,1)S(1)}, u32[]{:S(2)}, u32[]{:S(2)}) collective-permute-start(bf16[2,272,128]{2,1,0:T(8,128)(2,1)S(1)} %far_share.1.sent), channel_id=1, source_target_pairs={{0,3},{1,2},{2,1},{3,0},{4,7},{5,6},{6,5},{7,4},{8,11},{9,10},{10,... | collective-permute-start | bytes 417800 | tf_op jit(solution)/shard_map/ppermute | solution.py:323
  9.3 0.0 collective-permute-done.2.pattern
  9.3 0.0 collective-permute-done.3.paired
  9.3 0.0 copy-done
  9.3 1.2 %near_share.1 = (bf16[2,272,128]{2,1,0:T(8,128)(2,1)S(1)}, bf16[2,32,256]{2,1,0:T(8,128)(2,1)S(1)}, bf16[2,32,256]{2,1,0:T(8,128)(2,1)S(1)}, bf16[2,32,256]{2,1,0:T(8,128)(2,1)S(1)}, bf16[2,32,256]{2,1,0:T(8,128)(2,1)S(1)}) custom-call(s32[8,16]{1,0:T(8,128)S(1)} %collective-permute-done.2.pattern, bf16[32,256,128]{2,1,0:T(8,128)(2,1)S(1)} %get-tuple-element.17.pert, ...), custom_call_target="tpu_custom_call" | custom-call | flops 285212672 | bytes 1048576 | tf_op jit(solution)/shard_map/near_share/pallas_call | solution.py:324
  10.5 0.1 collective-permute-start.4
  10.6 2.7 %collective-permute-start.5 = (bf16[2,32,256]{2,1,0:T(8,128)(2,1)S(1)}, bf16[2,32,256]{2,1,0:T(8,128)(2,1)S(1)}, u32[]{:S(2)}, u32[]{:S(2)}) collective-permute-start(bf16[2,32,256]{2,1,0:T(8,128)(2,1)S(1)} %get-tuple-element.24), channel_id=1, source_target_pairs={{0,16},{4,20},{8,24},{12,28},{16,0},{20,4},{24,8},{28,12},{1,17},{... | collective-permute-start | bytes 98312 | tf_op jit(solution)/shard_map/ppermute | solution.py:337
  13.2 1.4 %collective-permute-start.6 = (bf16[2,32,256]{2,1,0:T(8,128)(2,1)S(1)}, bf16[2,32,256]{2,1,0:T(8,128)(2,1)S(1)}, u32[]{:S(2)}, u32[]{:S(2)}) collective-permute-start(bf16[2,32,256]{2,1,0:T(8,128)(2,1)S(1)} %get-tuple-element.25), channel_id=1, source_target_pairs={{0,24},{4,28},{8,16},{12,20},{16,8},{20,12},{24,0},{28,4},{1,25},{... | collective-permute-start | bytes 98312 | tf_op jit(solution)/shard_map/ppermute | solution.py:337
  14.6 0.2 collective-permute-start.7
  14.8 0.0 collective-permute-done.1.before
  14.8 0.0 collective-permute-done.4.after
  14.8 2.4 %root.1 = (bf16[2,256,256]{2,1,0:T(8,128)(2,1)S(1)}, f32[2,16,256]{2,1,0:T(8,128)S(1)}) custom-call(f32[2,272,256]{2,1,0:T(8,128)S(1)} %get-tuple-element.16.own, bf16[2,272,128]{2,1,0:T(8,128)(2,1)S(1)} %collective-permute-done.1.before, bf16[2,272,128]{2,1,0:T(8,128)(2,1)S(1)} %collective-permute-done.4.after), custom_call_target="tpu_custom_call" | custom-call | flops 1006632960 | bytes 1048576 | tf_op jit(solution)/shard_map/root/pallas_call | solution.py:338
  17.2 0.0 collective-permute-done.5.rest_1_
  17.2 1.7 %collective-permute-done.6.rest_2_ = bf16[2,32,256]{2,1,0:T(8,128)(2,1)S(1)} collective-permute-done((bf16[2,32,256]{2,1,0:T(8,128)(2,1)S(1)}, bf16[2,32,256]{2,1,0:T(8,128)(2,1)S(1)}, u32[]{:S(2)}, u32[]{:S(2)}) %collective-permute-start.6) | collective-permute-done | bytes 32800 | tf_op jit(solution)/shard_map/ppermute | solution.py:337
  18.9 0.0 collective-permute-done.7.rest_3_
  18.9 0.7 %apply.1 = bf16[8,2,32,128]{3,2,1,0:T(8,128)(2,1)S(1)} custom-call(bf16[2,256,256]{2,1,0:T(8,128)(2,1)S(1)} %get-tuple-element.21.root, f32[2,16,256]{2,1,0:T(8,128)S(1)} %get-tuple-element.22.rows, bf16[2,32,256]{2,1,0:T(8,128)(2,1)S(1)} %get-tuple-element.23.rest_0_, bf16[2,32,256]{2,1,0:T(8,128)(2,1)S(1)} %collective-permute-done.5.rest_1_, ...), custom_call_target="tpu_custom_call" | custom-call | flops 33554432 | bytes 524288 | tf_op jit(solution)/shard_map/apply/pallas_call | solution.py:349
  19.6 10.4 %all_to_all.5 = bf16[8,2,32,128]{3,2,1,0:T(8,128)(2,1)S(1)} all-to-all(bf16[8,2,32,128]{3,2,1,0:T(8,128)(2,1)S(1)} %apply.1), channel_id=1, replica_groups=mesh['mem'=8,'lon'=4] {'mem'}, dimensions={0} | all-to-all | bytes 262144 | tf_op jit(solution)/shard_map/all_to_all | solution.py:361
  30.0 0.1 copy.7
  30.1 0.7 %reshape.3 = bf16[32,2048]{1,0:T(8,128)(2,1)} reshape(bf16[32,8,2,128]{3,2,1,0:T(2,128)(2,1)S(1)} %copy.7) | data formatting | bytes 262144 | tf_op jit(solution)/shard_map/reshape | solution.py:362
Async XLA Ops:
  0.0 9.3 %collective-permute-start.3 = (bf16[32,2048]{1,0:T(8,128)(2,1)}, bf16[32,2048]{1,0:T(8,128)(2,1)S(1)}, u32[]{:S(2)}, u32[]{:S(2)}) collective-permute-start(bf16[32,2048]{1,0:T(8,128)(2,1)} %state.1), channel_id=1, source_target_pairs={{0,4},{4,0},{8,12},{12,8},{16,20},{20,16},{24,28},{28,24},{1,5},{5... | collective-permute-start | bytes 393224 | tf_op jit(solution)/shard_map/ppermute | solution.py:283
  2.9 6.4 %copy-start = (bf16[32,2048]{1,0:T(8,128)(2,1)S(1)}, bf16[32,2048]{1,0:T(8,128)(2,1)}, u32[]{:S(2)}) copy-start(bf16[32,2048]{1,0:T(8,128)(2,1)} %state.1) | copy-start | bytes 393220
  2.9 6.4 %collective-permute-start.2 = (s32[8,16]{1,0:T(8,128)}, s32[8,16]{1,0:T(8,128)S(1)}, u32[]{:S(2)}, u32[]{:S(2)}) collective-permute-start(s32[8,16]{1,0:T(8,128)} %bitcast.3), channel_id=1, source_target_pairs={{0,1},{1,0},{2,3},{3,2},{4,5},{5,4},{6,7},{7,6},{8,9},{9,8},{10,11... | collective-permute-start | bytes 1544 | tf_op jit(solution)/shard_map/ppermute | solution.py:282
  2.9 4.0 %collective-permute-start = (s32[8,16]{1,0:T(8,128)}, s32[8,16]{1,0:T(8,128)S(1)}, u32[]{:S(2)}, u32[]{:S(2)}) collective-permute-start(s32[8,16]{1,0:T(8,128)} %bitcast.4), channel_id=1, source_target_pairs={{0,3},{1,2},{2,1},{3,0},{4,7},{5,6},{6,5},{7,4},{8,11},{9,10},{10,... | collective-permute-start | bytes 1544 | tf_op jit(solution)/shard_map/ppermute | solution.py:281
  8.0 6.7 %collective-permute-start.1 = (bf16[2,272,128]{2,1,0:T(8,128)(2,1)S(1)}, bf16[2,272,128]{2,1,0:T(8,128)(2,1)S(1)}, u32[]{:S(2)}, u32[]{:S(2)}) collective-permute-start(bf16[2,272,128]{2,1,0:T(8,128)(2,1)S(1)} %far_share.1.sent), channel_id=1, source_target_pairs={{0,3},{1,2},{2,1},{3,0},{4,7},{5,6},{6,5},{7,4},{8,11},{9,10},{10,... | collective-permute-start | bytes 417800 | tf_op jit(solution)/shard_map/ppermute | solution.py:323
  10.5 4.3 %collective-permute-start.4 = (bf16[2,272,128]{2,1,0:T(8,128)(2,1)S(1)}, bf16[2,272,128]{2,1,0:T(8,128)(2,1)S(1)}, u32[]{:S(2)}, u32[]{:S(2)}) collective-permute-start(bf16[2,272,128]{2,1,0:T(8,128)(2,1)S(1)} %get-tuple-element.20), channel_id=1, source_target_pairs={{0,1},{1,0},{2,3},{3,2},{4,5},{5,4},{6,7},{7,6},{8,9},{9,8},{10,11... | collective-permute-start | bytes 417800 | tf_op jit(solution)/shard_map/ppermute | solution.py:333
  10.6 6.6 %collective-permute-start.5 = (bf16[2,32,256]{2,1,0:T(8,128)(2,1)S(1)}, bf16[2,32,256]{2,1,0:T(8,128)(2,1)S(1)}, u32[]{:S(2)}, u32[]{:S(2)}) collective-permute-start(bf16[2,32,256]{2,1,0:T(8,128)(2,1)S(1)} %get-tuple-element.24), channel_id=1, source_target_pairs={{0,16},{4,20},{8,24},{12,28},{16,0},{20,4},{24,8},{28,12},{1,17},{... | collective-permute-start | bytes 98312 | tf_op jit(solution)/shard_map/ppermute | solution.py:337
  13.2 5.7 %collective-permute-start.6 = (bf16[2,32,256]{2,1,0:T(8,128)(2,1)S(1)}, bf16[2,32,256]{2,1,0:T(8,128)(2,1)S(1)}, u32[]{:S(2)}, u32[]{:S(2)}) collective-permute-start(bf16[2,32,256]{2,1,0:T(8,128)(2,1)S(1)} %get-tuple-element.25), channel_id=1, source_target_pairs={{0,24},{4,28},{8,16},{12,20},{16,8},{20,12},{24,0},{28,4},{1,25},{... | collective-permute-start | bytes 98312 | tf_op jit(solution)/shard_map/ppermute | solution.py:337
  14.6 4.4 %collective-permute-start.7 = (bf16[2,32,256]{2,1,0:T(8,128)(2,1)S(1)}, bf16[2,32,256]{2,1,0:T(8,128)(2,1)S(1)}, u32[]{:S(2)}, u32[]{:S(2)}) collective-permute-start(bf16[2,32,256]{2,1,0:T(8,128)(2,1)S(1)} %get-tuple-element.26), channel_id=1, source_target_pairs={{0,8},{4,12},{8,0},{12,4},{16,24},{20,28},{24,16},{28,20},{1,9},{5... | collective-permute-start | bytes 98312 | tf_op jit(solution)/shard_map/ppermute | solution.py:337
